TPU v7x, 256 devices: a whole 4x4x8 slice. The times are simulated.
256 devices in a mesh: dp: 32 (over x, z), expert: 8 (over y, core).
Axes of the slice: x: 4, y: 4, z: 8, core: 2. Of those that a mesh axis runs over, the one named last changes fastest.
Arguments:
- tokens: bfloat16 [65536, 768], P(('dp', 'expert')), may hold values from -24 to 24
- expert_ids: int32 [65536, 2], P(('dp', 'expert')), may hold values from 0 to 31, all different within a row; in each aligned block of 256 rows (0 to 255, 256 to 511, ...) at most 32 rows name the same one
- gate_fixed: int32 [65536, 2], P(('dp', 'expert')), may hold values from 8192 to 65535
- cotangent: bfloat16 [65536, 768], P(('dp', 'expert')), may hold values from -24 to 24
- w_gate: bfloat16 [32, 768, 384], P('expert'), may hold values from -0.21875 to 0.21875
- w_up: bfloat16 [32, 768, 384], P('expert'), may hold values from -0.21875 to 0.21875
- w_down: bfloat16 [32, 768, 384], P('expert'), may hold values from -0.3125 to 0.3125
Outputs:
- layer_out: bfloat16 [65536, 768], P(('dp', 'expert'))
- input_grad: bfloat16 [65536, 768], P(('dp', 'expert'))
- grad_gate: float32 [32, 768, 384], P('expert', 'dp')
- grad_up: float32 [32, 768, 384], P('expert', 'dp')
- grad_down: float32 [32, 768, 384], P('expert', 'dp')
Inputs may be any that keep to these rules, and one draw needn't show every extreme that they name: `expert_ids`: A row names 2 different experts. In each aligned block of 256 rows (the rows of one device) no expert is named by more than 32 rows, and in some block one expert is named by exactly 32 rows.
All inputs are finite; a program needn't handle non-finite values.
Results may differ from a plain program's by a relative error of at most 0.015.
Values may be sent and summed in bfloat16 or wider, within the bound.
No kernel may reach another device: no remote copies, remote signals or barrier semaphores. Data moves between devices by JAX's collectives and lax.ppermute only.
A program may use at most 64 MiB of HBM per device.

v0:
```python
import functools

import jax
import jax.numpy as jnp
import numpy as np
from jax import lax
from jax.experimental import pallas as pl
from jax.experimental.pallas import tpu as pltpu
from jax.sharding import PartitionSpec as P

F32, BF16 = jnp.float32, jnp.bfloat16
META = 16


def dot(a, b, dims=((1,), (0,))):
    return lax.dot_general(a, b, (dims, ((), ())), preferred_element_type=F32)


ROOM = pltpu.CompilerParams(vmem_limit_bytes=56 * 2**20)
SCALARS = pl.BlockSpec(memory_space=pltpu.SMEM)


def whole(shape):
    return pl.BlockSpec(shape, lambda i: (0,) * len(shape))


def less_than(size, transposed):
    rows = lax.broadcasted_iota(jnp.int32, (size, size), 0)
    cols = lax.broadcasted_iota(jnp.int32, (size, size), 1)
    return ((cols < rows) if transposed else (rows < cols)).astype(F32).astype(BF16)


def meta_kernel(ids_ref, gate_ref, tok_ref, out_ref):
    n_t, d = tok_ref.shape
    ids, gate = ids_ref[...], gate_ref[...]
    high, low = gate // 256, gate % 256
    meta = jnp.concatenate([ids, high, low], 0).astype(F32)
    meta = jnp.concatenate([meta, jnp.zeros((META - 6, n_t), F32)], 0)
    out_ref[:n_t, :] = tok_ref[...]
    out_ref[n_t:, :n_t] = meta.astype(BF16)
    out_ref[n_t:, n_t:] = jnp.zeros((META, d - n_t), BF16)


def with_meta(ids, gate, tokens):
    n_t, d = tokens.shape
    return pl.pallas_call(
        meta_kernel,
        grid=(1,),
        in_specs=[whole(ids.shape), whole(gate.shape), whole(tokens.shape)],
        out_specs=whole((n_t + META, d)),
        out_shape=jax.ShapeDtypeStruct((n_t + META, d), BF16),
        compiler_params=ROOM,
        cost_estimate=pl.CostEstimate(flops=n_t * d, bytes_accessed=4 * n_t * d, transcendentals=0),
    )(ids, gate, tokens)


def pack_kernel(n, cap, n_e, me_ref, *refs):
    tok, cot = refs[:n], refs[n : 2 * n]
    rows_ref, grads_ref = refs[2 * n :]
    n_t = cot[0].shape[0]
    eid = (me_ref[0] * n_e + lax.broadcasted_iota(jnp.int32, (n_e, n_t), 0)).astype(F32)
    masks, gates = [], []
    for r in range(n):
        meta = tok[r][n_t : n_t + META, :n_t].astype(F32)
        row = lambda i: jnp.broadcast_to(meta[i : i + 1], (n_e, n_t))
        first, second = row(0) == eid, row(1) == eid
        g0 = (row(2) * 256.0 + row(4)) / 65536.0
        g1 = (row(3) * 256.0 + row(5)) / 65536.0
        masks.append(jnp.where(first | second, 1.0, 0.0))
        gates.append(jnp.where(first, g0, jnp.where(second, g1, 0.0)))
    mask = jnp.concatenate(masks, 0)
    rank = jnp.where(mask > 0.5, dot(mask.astype(BF16), less_than(n_t, False)), -1.0)
    slot = lax.broadcasted_iota(jnp.int32, (cap, n_t), 0).astype(F32)
    for r in range(n):
        hots, slot_gates = [], []
        for e in range(n_e):
            i = r * n_e + e
            hot = jnp.where(jnp.broadcast_to(rank[i : i + 1], (cap, n_t)) == slot, 1.0, 0.0)
            hots.append(hot)
            slot_gates.append(jnp.sum(hot * gates[r][e : e + 1], axis=1, keepdims=True))
        hot = jnp.concatenate(hots, 0).astype(BF16)
        slot_gate = jnp.concatenate(slot_gates, 0)
        rows = dot(hot, tok[r][:n_t, :]).astype(BF16)
        grads = (slot_gate * dot(hot, cot[r][...])).astype(BF16)
        for e in range(n_e):
            rows_ref[e, r * cap : (r + 1) * cap, :] = rows[e * cap : (e + 1) * cap]
            grads_ref[e, r * cap : (r + 1) * cap, :] = grads[e * cap : (e + 1) * cap]


def pack(me, tok, cot, cap, n_e):
    n, (n_t, d) = len(cot), cot[0].shape
    out = jax.ShapeDtypeStruct((n_e, n * cap, d), BF16)
    return pl.pallas_call(
        functools.partial(pack_kernel, n, cap, n_e),
        grid=(1,),
        in_specs=[SCALARS] + [whole(a.shape) for a in (*tok, *cot)],
        out_specs=[whole(out.shape)] * 2,
        out_shape=[out, out],
        compiler_params=ROOM,
        cost_estimate=pl.CostEstimate(
            flops=4 * n * n_e * cap * n_t * d, bytes_accessed=4 * n * (n_t + n_e * cap) * d, transcendentals=0
        ),
    )(me, *tok, *cot)


def expert_kernel(first, cap, scale, order_ref, from_ref, near_x, far_x, near_g, far_g, wg_ref, wu_ref, wd_ref, *refs):
    refs = refs[-8:]
    ret, send, keep, acc = refs[0], refs[1:3], refs[3:5], refs[5:8]
    step = pl.program_id(0)
    x = jnp.concatenate([near_x[0], far_x[0]], 0)
    dy = jnp.concatenate([near_g[0], far_g[0]], 0)
    wg, wu, wd = wg_ref[0], wu_ref[0], wd_ref[0]
    pre_gate, pre_up = dot(x, wg), dot(x, wu)
    sig = jax.nn.sigmoid(pre_gate)
    act = pre_gate * sig
    hidden = (act * pre_up).astype(BF16)
    hidden_grad = dot(dy, wd)
    gate_grad = (hidden_grad * pre_up * sig * (1.0 + pre_gate * (1.0 - sig))).astype(BF16)
    up_grad = (hidden_grad * act).astype(BF16)
    shape = acc[0].shape
    acc[0][...] = (dot(x, gate_grad, ((0,), (0,))) * scale).reshape(shape)
    acc[1][...] = (dot(x, up_grad, ((0,), (0,))) * scale).reshape(shape)
    acc[2][...] = (dot(dy, hidden, ((0,), (0,))) * scale).reshape(shape)
    out = dot(hidden, wd, ((1,), (1,))).astype(BF16)
    entry = (dot(gate_grad, wg, ((1,), (1,))) + dot(up_grad, wu, ((1,), (1,)))).astype(BF16)
    for r in range(8):
        ret[from_ref[r], 0, 0] = out[r * cap : (r + 1) * cap]
        ret[from_ref[r], 1, 0] = entry[r * cap : (r + 1) * cap]
    ff, half = wg.shape[1], shape[0] // 2
    for i in range(2):

        @pl.when(step == i)
        def _(i=i):
            for p in range(2 * half):
                chunk = order_ref[first + i, p]
                to = (send if p < half else keep)[i]
                for k in range(3):
                    to[p % half, :, k * ff : (k + 1) * ff] = acc[k][chunk].astype(BF16)


def experts(first, order, sources, near, far, weights, ret, cap, scale, replicas):
    n_e, d, ff = weights[0].shape
    slots = 8 * cap
    part = lambda a: pl.BlockSpec((1, *a.shape[1:]), lambda e: (first + e, 0, 0))
    row = pl.BlockSpec((8, 2, 1, cap, d), lambda e: (0, 0, first + e, 0, 0))
    rows = [near[0], far[0], near[1], far[1]]
    chunks = jax.ShapeDtypeStruct((replicas // 2, d // replicas, 3 * ff), BF16)
    out = pl.pallas_call(
        functools.partial(expert_kernel, first, cap, scale),
        grid=(2,),
        in_specs=[SCALARS] * 2
        + [part(a) for a in (*rows, *weights)]
        + [pl.BlockSpec(memory_space=pl.ANY)] * len(ret),
        out_specs=[row] + [whole(chunks.shape)] * 4,
        out_shape=[jax.ShapeDtypeStruct((8, 2, n_e, cap, d), BF16)] + [chunks] * 4,
        input_output_aliases={9: 0} if ret else {},
        scratch_shapes=[pltpu.VMEM((replicas, d // replicas, ff), F32)] * 3,
        compiler_params=ROOM,
        cost_estimate=pl.CostEstimate(
            flops=36 * slots * d * ff, bytes_accessed=24 * d * ff + 16 * slots * d, transcendentals=2 * slots * ff
        ),
    )(order, sources, *rows, *weights, *ret)
    return out[:1], out[1:3], out[3:5]


def combine_kernel(cap, ids_ref, gate_ref, _, ret, out_ref, grad_ref):
    n_t, count = ids_ref.shape[0], ret.shape[0] * ret.shape[2]
    eid = lax.broadcasted_iota(jnp.int32, (n_t, count), 1)
    first, second = ids_ref[:, 0:1] == eid, ids_ref[:, 1:2] == eid
    mask = jnp.where(first | second, 1.0, 0.0).astype(BF16)
    rank = dot(less_than(n_t, True), mask)
    rows = lax.broadcasted_iota(jnp.int32, (count, count * cap), 0)
    cols = lax.broadcasted_iota(jnp.int32, (count, count * cap), 1)
    spread = jnp.where(cols // cap == rows, 1.0, 0.0).astype(BF16)
    slot = (lax.broadcasted_iota(jnp.int32, (n_t, count * cap), 1) % cap).astype(F32)
    hots = [
        jnp.where(dot(jnp.where(m, rank, -1.0).astype(BF16), spread) == slot, 1.0, 0.0)
        for m in (first, second)
    ]
    both = (hots[0] + hots[1]).astype(BF16)
    hots = [h.astype(BF16) for h in hots]
    outs = ret[:, 0].reshape(count * cap, ret.shape[-1])
    grads = ret[:, 1].reshape(count * cap, ret.shape[-1])
    gate = gate_ref[...].astype(F32) / 65536.0
    total = gate[:, 0:1] * dot(hots[0], outs) + gate[:, 1:2] * dot(hots[1], outs)
    out_ref[...] = total.astype(BF16)
    grad_ref[...] = dot(both, grads).astype(BF16)


def combine(ids, gate, after, ret):
    peers, _, n_e, cap, d = ret.shape
    n_t = ids.shape[0]
    row = jax.ShapeDtypeStruct((n_t, d), BF16)
    return pl.pallas_call(
        functools.partial(combine_kernel, cap),
        grid=(1,),
        in_specs=[whole(ids.shape), whole(gate.shape), pl.BlockSpec(memory_space=pl.ANY), whole(ret.shape)],
        out_specs=[whole(row.shape)] * 2,
        out_shape=[row, row],
        compiler_params=ROOM,
        cost_estimate=pl.CostEstimate(
            flops=6 * n_t * d * peers * n_e * cap, bytes_accessed=40 * n_t * d, transcendentals=0
        ),
    )(ids, gate, after, ret)


PLANS = (
    ("xp", "xq", "zp", "zq", "zf"),
    ("xq", "xp", "zq", "zp", "zg"),
    ("zp", "zq", "xp", "xq", "zf"),
    ("zq", "zp", "xq", "xp", "zg"),
)
FAR = {"zf": (3, 6, 5, 0, 7, 2, 1, 4), "zg": (5, 4, 7, 6, 1, 0, 3, 2)}


def partners(kind, nx, nz):
    out = []
    for x in range(nx):
        for z in range(nz):
            at, n = (x, nx) if kind[0] == "x" else (z, nz)
            if kind in FAR:
                at = FAR[kind][at]
            elif kind[1] == "p":
                at = at ^ 1
            else:
                at = (at + 1) % n if at % 2 else (at - 1) % n
            out.append(at * nz + z if kind[0] == "x" else x * nz + at)
    return out


def chunk_orders(nx, nz):
    plans = []
    for plan in PLANS:
        held = [[i] for i in range(nx * nz)]
        for kind in reversed(plan):
            with_ = partners(kind, nx, nz)
            held = [held[with_[i]] + held[i] for i in range(nx * nz)]
        plans.append(held)
    return np.asarray(plans, np.int32).swapaxes(0, 1)


def reduce_grads(send, keep, nx, nz):
    send, keep = list(send), list(keep)
    swap = lambda a, kind: lax.ppermute(a, "dp", list(enumerate(partners(kind, nx, nz))))
    steps = len(PLANS[0])
    for k in range(steps):
        got = [swap(send[v], PLANS[v][k]) for v in range(4)]
        if k == steps - 1:
            return [keep[v].astype(F32) + got[v].astype(F32) for v in range(4)], send
        half = keep[0].shape[0] // 2
        for v in range(4):
            send[v] = (keep[v][:half].astype(F32) + got[v][:half].astype(F32)).astype(BF16)
            keep[v] = (keep[v][half:].astype(F32) + got[v][half:].astype(F32)).astype(BF16)


def shards(nx, nz, tokens, expert_ids, gate_fixed, cotangent, w_gate, w_up, w_down):
    n_t, top = expert_ids.shape
    n_e, d, ff = w_gate.shape
    peers = lax.axis_size("expert")
    ny = peers // 2
    replicas = nx * nz
    cap = n_t * top * 2 // (n_e * peers)
    scale = float(n_t * replicas * top // n_e) ** (-0.5)
    me = lax.axis_index("expert")
    place = lax.axis_index("dp")

    def to(a, dy, dc):
        perm = [(y * 2 + c, ((y + dy) % ny) * 2 + (c ^ dc)) for y in range(ny) for c in range(2)]
        return lax.ppermute(a, "expert", perm)

    tok = {(0, 0): with_meta(expert_ids.T, gate_fixed.T, tokens)}
    cot = {(0, 0): cotangent}
    tok[3, 0], cot[1, 0] = to(tok[0, 0], 1, 0), to(cot[0, 0], -1, 0)
    cot[3, 0], tok[1, 0] = to(cot[0, 0], 1, 0), to(tok[0, 0], -1, 0)
    tok[2, 0], cot[2, 0] = to(tok[3, 0], 1, 0), to(cot[1, 0], -1, 0)
    for dy in range(4):
        tok[dy, 1], cot[dy, 1] = to(tok[dy, 0], 0, 1), to(cot[dy, 0], 0, 1)
    order = [(dy, dc) for dy in (0, 1, 3, 2) for dc in range(2)]
    mine = me.reshape(1)
    near = pack(mine, [tok[r] for r in order[:6]], [cot[r] for r in order[:6]], cap, n_e)
    far = pack(mine, [tok[r] for r in order[6:]], [cot[r] for r in order[6:]], cap, n_e)
    chunk_order = lax.dynamic_index_in_dim(jnp.asarray(chunk_orders(nx, nz)), place, 0, keepdims=False)
    weights = (w_gate, w_up, w_down)
    y, c = me // 2, me % 2
    sources = jnp.stack([((y + dy) % ny) * 2 + (c + dc) % 2 for dy, dc in order])
    ret, send_a, keep_a = experts(0, chunk_order, sources, near, far, weights, [], cap, scale, replicas)
    ret, send_b, keep_b = experts(2, chunk_order, sources, near, far, weights, ret, cap, scale, replicas)
    total, last = reduce_grads((*send_a, *send_b), (*keep_a, *keep_b), nx, nz)
    back = lax.all_to_all(ret[0], "expert", split_axis=0, concat_axis=0, tiled=True)
    layer_out, input_grad = combine(expert_ids, gate_fixed, last[-1], back)
    total = jnp.concatenate(total, 0)
    return (layer_out, input_grad, total[:, :, :ff], total[:, :, ff : 2 * ff], total[:, :, 2 * ff :])


def solution(mesh):
    nx = 4
    nz = mesh.shape["dp"] // nx
    return jax.shard_map(
        functools.partial(shards, nx, nz),
        mesh=mesh,
        in_specs=(P(("dp", "expert"), None),) * 4 + (P("expert", None, None),) * 3,
        out_specs=(P(("dp", "expert"), None),) * 2 + (P("expert", "dp", None),) * 3,
        check_vma=False,
    )
```

profile of v0, /device:TPU:2, one launch (start us, length us, event | category | flops | bytes accessed | tf_op | source)
XLA Modules:
  0.0 147.8 jit_solution(7215723036175768903)
XLA Ops:
  0.6 3.1 %collective-permute-start.6 = (bf16[256,768]{1,0:T(8,128)(2,1)}, bf16[256,768]{1,0:T(8,128)(2,1)S(1)}, u32[]{:S(2)}, u32[]{:S(2)}) collective-permute-start(bf16[256,768]{1,0:T(8,128)(2,1)} %refs_6_.1), channel_id=1, source_target_pairs={{0,6},{1,7},{2,0},{3,1},{4,2},{5,3},{6,4},{7,5},{8,14},{9,15},{10,... | collective-permute-start | bytes 1179656 | tf_op jit(solution)/shard_map/ppermute | solution.py:269
  3.7 1.8 %shard_map.119.refs_0_ = bf16[272,768]{1,0:T(8,128)(2,1)} custom-call(s32[2,256]{1,0:T(2,128)} %bitcast.13, s32[2,256]{1,0:T(2,128)} %bitcast.14, bf16[256,768]{1,0:T(8,128)(2,1)} %tok_ref.1), custom_call_target="tpu_custom_call" | custom-call | flops 196608 | bytes 786432 | tf_op jit(solution)/shard_map/pallas_call | solution.py:46
  6.2 2.7 %collective-permute-start.1 = (bf16[272,768]{1,0:T(8,128)(2,1)}, bf16[272,768]{1,0:T(8,128)(2,1)S(1)}, u32[]{:S(2)}, u32[]{:S(2)}) collective-permute-start(bf16[272,768]{1,0:T(8,128)(2,1)} %shard_map.119.refs_0_), channel_id=1, source_target_pairs={{0,6},{1,7},{2,0},{3,1},{4,2},{5,3},{6,4},{7,5},{8,14},{9,15},{10,... | collective-permute-start | bytes 1253384 | tf_op jit(solution)/shard_map/ppermute | solution.py:269
  8.8 4.7 %collective-permute-done.6.refs_8_ = bf16[256,768]{1,0:T(8,128)(2,1)S(1)} collective-permute-done((bf16[256,768]{1,0:T(8,128)(2,1)}, bf16[256,768]{1,0:T(8,128)(2,1)S(1)}, u32[]{:S(2)}, u32[]{:S(2)}) %collective-permute-start.6) | collective-permute-done | bytes 393248 | tf_op jit(solution)/shard_map/ppermute | solution.py:269
  13.6 13.1 %collective-permute-done.8.refs_10_ = bf16[256,768]{1,0:T(8,128)(2,1)} collective-permute-done((bf16[256,768]{1,0:T(8,128)(2,1)}, bf16[256,768]{1,0:T(8,128)(2,1)}, u32[]{:S(2)}, u32[]{:S(2)}) %collective-permute-start.8) | collective-permute-done | bytes 393248 | tf_op jit(solution)/shard_map/ppermute | solution.py:269
  26.7 3.2 %collective-permute-start.12 = (bf16[256,768]{1,0:T(8,128)(2,1)S(1)}, bf16[256,768]{1,0:T(8,128)(2,1)}, u32[]{:S(2)}, u32[]{:S(2)}) collective-permute-start(bf16[256,768]{1,0:T(8,128)(2,1)S(1)} %collective-permute-done.6.refs_8_), channel_id=1, source_target_pairs={{0,6},{1,7},{2,0},{3,1},{4,2},{5,3},{6,4},{7,5},{8,14},{9,15},{10,... | collective-permute-start | bytes 1179656 | tf_op jit(solution)/shard_map/ppermute | solution.py:269
  30.6 9.3 %collective-permute-done.10.refs_0_ = bf16[272,768]{1,0:T(8,128)(2,1)S(1)} collective-permute-done((bf16[272,768]{1,0:T(8,128)(2,1)S(1)}, bf16[272,768]{1,0:T(8,128)(2,1)S(1)}, u32[]{:S(2)}, u32[]{:S(2)}) %collective-permute-start.10) | collective-permute-done | bytes 417824 | tf_op jit(solution)/shard_map/ppermute | solution.py:269
  43.2 4.7 %shard_map.120 = (bf16[4,192,768]{2,1,0:T(8,128)(2,1)}, bf16[4,192,768]{2,1,0:T(8,128)(2,1)}) custom-call(s32[1]{0:T(128)} %bitcast.9.me_ref, bf16[272,768]{1,0:T(8,128)(2,1)} %shard_map.119.refs_0_, bf16[272,768]{1,0:T(8,128)(2,1)} %copy-done.6, bf16[272,768]{1,0:T(8,128)(2,1)} %copy-done.5, bf16[272,768]{1,0:T(8,128)(2,1)} %copy-done.8, ...), custom_call_target="tpu_custom_call" | custom-call | flops 603979776 | bytes 7077888 | tf_op jit(solution)/shard_map/pallas_call | solution.py:93
  48.7 2.7 %shard_map.121 = (bf16[4,64,768]{2,1,0:T(8,128)(2,1)}, bf16[4,64,768]{2,1,0:T(8,128)(2,1)}) custom-call(s32[1]{0:T(128)} %bitcast.9.me_ref, bf16[272,768]{1,0:T(8,128)(2,1)} %copy-done.9, bf16[272,768]{1,0:T(8,128)(2,1)} %copy-done.10, bf16[256,768]{1,0:T(8,128)(2,1)} %collective-permute-done.12.refs_2_, bf16[256,768]{1,0:T(8,128)(2,1)} %collective-permute-done.13.refs_3_), custom_call_target="tpu_custom_call" | custom-call | flops 201326592 | bytes 2359296 | tf_op jit(solution)/shard_map/pallas_call | solution.py:93
  51.5 8.6 %shard_map.122 = (bf16[8,2,4,32,768]{4,3,2,1,0:T(8,128)(2,1)}, bf16[16,24,1152]{2,1,0:T(8,128)(2,1)}, bf16[16,24,1152]{2,1,0:T(8,128)(2,1)}, bf16[16,24,1152]{2,1,0:T(8,128)(2,1)}, bf16[16,24,1152]{2,1,0:T(8,128)(2,1)}) custom-call(s32[4,32]{1,0:T(4,128)} %dynamic-slice_bitcast_fusion.order_ref, s32[8]{0:T(128)} %stack.35.from_ref, ...), custom_call_target="tpu_custom_call" | custom-call | flops 2717908992 | bytes 10223616 | tf_op jit(solution)/shard_map/pallas_call | solution.py:148
  60.7 2.2 %collective-permute-start.23 = (bf16[16,24,1152]{2,1,0:T(8,128)(2,1)}, bf16[16,24,1152]{2,1,0:T(8,128)(2,1)}, u32[]{:S(2)}, u32[]{:S(2)}) collective-permute-start(bf16[16,24,1152]{2,1,0:T(8,128)(2,1)} %get-tuple-element.34), channel_id=1, source_target_pairs={{0,192},{8,200},{16,208},{24,216},{32,224},{40,232},{48,240},{56,2... | collective-permute-start | bytes 2654216 | tf_op jit(solution)/shard_map/ppermute | solution.py:244
  64.4 8.6 %shard_map.123 = (bf16[8,2,4,32,768]{4,3,2,1,0:T(8,128)(2,1)}, bf16[16,24,1152]{2,1,0:T(8,128)(2,1)}, bf16[16,24,1152]{2,1,0:T(8,128)(2,1)}, bf16[16,24,1152]{2,1,0:T(8,128)(2,1)}, bf16[16,24,1152]{2,1,0:T(8,128)(2,1)}) custom-call(s32[4,32]{1,0:T(4,128)} %dynamic-slice_bitcast_fusion.order_ref, s32[8]{0:T(128)} %stack.35.from_ref, ...), custom_call_target="tpu_custom_call", output_to_operand_aliasing={{0}: (9, {})} | custom-call | flops 2717908992 | bytes 10223616 | tf_op jit(solution)/shard_map/pallas_call | solution.py:148
  73.0 2.0 %collective-permute-start.28 = (bf16[16,24,1152]{2,1,0:T(8,128)(2,1)}, bf16[16,24,1152]{2,1,0:T(8,128)(2,1)}, u32[]{:S(2)}, u32[]{:S(2)}) collective-permute-start(bf16[16,24,1152]{2,1,0:T(8,128)(2,1)} %get-tuple-element.36), channel_id=1, source_target_pairs={{0,8},{8,0},{16,24},{24,16},{32,40},{40,32},{48,56},{56,48},{64,72... | collective-permute-start | bytes 2654216 | tf_op jit(solution)/shard_map/ppermute | solution.py:244
  75.0 5.0 %collective-permute-start.14 = (bf16[16,24,1152]{2,1,0:T(8,128)(2,1)}, bf16[16,24,1152]{2,1,0:T(8,128)(2,1)}, u32[]{:S(2)}, u32[]{:S(2)}) collective-permute-start(bf16[16,24,1152]{2,1,0:T(8,128)(2,1)} %get-tuple-element.27), channel_id=1, source_target_pairs={{0,56},{8,16},{16,8},{24,32},{32,24},{40,48},{48,40},{56,0},{64,12... | collective-permute-start | bytes 2654216 | tf_op jit(solution)/shard_map/ppermute | solution.py:244
  80.0 3.6 %all-to-all-start = ((bf16[8,2,4,32,768]{4,3,2,1,0:T(8,128)(2,1)}), bf16[8,2,4,32,768]{4,3,2,1,0:T(8,128)(2,1)S(1)}, u32[]{:S(2)}, u32[]{:S(2)}) async-start(bf16[8,2,4,32,768]{4,3,2,1,0:T(8,128)(2,1)} %get-tuple-element.28), calls=%async_computation | async-start | bytes 6291456 | tf_op jit(solution)/shard_map/all_to_all | solution.py:289
  83.7 1.7 %add_convert_fusion.5 = (bf16[8,24,1152]{2,1,0:T(8,128)(2,1)S(1)}, bf16[8,24,1152]{2,1,0:T(8,128)(2,1)S(1)}) fusion(bf16[16,24,1152]{2,1,0:T(8,128)(2,1)} %collective-permute-done.18, bf16[16,24,1152]{2,1,0:T(8,128)(2,1)} %get-tuple-element.31), kind=kLoop, calls=%fused_computation.5 | loop fusion | flops 1769472 | bytes 2654208 | tf_op jit(solution)/shard_map/convert_element_type | solution.py:253
  87.0 2.6 %collective-permute-start.24 = (bf16[8,24,1152]{2,1,0:T(8,128)(2,1)S(1)}, bf16[8,24,1152]{2,1,0:T(8,128)(2,1)S(1)}, u32[]{:S(2)}, u32[]{:S(2)}) collective-permute-start(bf16[8,24,1152]{2,1,0:T(8,128)(2,1)S(1)} %get-tuple-element.40), channel_id=1, source_target_pairs={{0,64},{8,72},{16,80},{24,88},{32,96},{40,104},{48,112},{56,120},{... | collective-permute-start | bytes 1327112 | tf_op jit(solution)/shard_map/ppermute | solution.py:244
  89.7 5.2 %collective-permute-done.28 = bf16[16,24,1152]{2,1,0:T(8,128)(2,1)} collective-permute-done((bf16[16,24,1152]{2,1,0:T(8,128)(2,1)}, bf16[16,24,1152]{2,1,0:T(8,128)(2,1)}, u32[]{:S(2)}, u32[]{:S(2)}) %collective-permute-start.28) | collective-permute-done | bytes 884768 | tf_op jit(solution)/shard_map/ppermute | solution.py:244
  96.3 5.8 %collective-permute-start.29 = (bf16[8,24,1152]{2,1,0:T(8,128)(2,1)S(1)}, bf16[8,24,1152]{2,1,0:T(8,128)(2,1)S(1)}, u32[]{:S(2)}, u32[]{:S(2)}) collective-permute-start(bf16[8,24,1152]{2,1,0:T(8,128)(2,1)S(1)} %get-tuple-element.42), channel_id=1, source_target_pairs={{0,56},{8,16},{16,8},{24,32},{32,24},{40,48},{48,40},{56,0},{64,12... | collective-permute-start | bytes 1327112 | tf_op jit(solution)/shard_map/ppermute | solution.py:244
  103.8 2.1 %collective-permute-start.20 = (bf16[4,24,1152]{2,1,0:T(8,128)(2,1)S(1)}, bf16[4,24,1152]{2,1,0:T(8,128)(2,1)S(1)}, u32[]{:S(2)}, u32[]{:S(2)}) collective-permute-start(bf16[4,24,1152]{2,1,0:T(8,128)(2,1)S(1)} %get-tuple-element.46), channel_id=1, source_target_pairs={{0,8},{8,0},{16,24},{24,16},{32,40},{40,32},{48,56},{56,48},{64,72... | collective-permute-start | bytes 663560 | tf_op jit(solution)/shard_map/ppermute | solution.py:244
  106.6 6.5 %collective-permute-done.29 = bf16[8,24,1152]{2,1,0:T(8,128)(2,1)S(1)} collective-permute-done((bf16[8,24,1152]{2,1,0:T(8,128)(2,1)S(1)}, bf16[8,24,1152]{2,1,0:T(8,128)(2,1)S(1)}, u32[]{:S(2)}, u32[]{:S(2)}) %collective-permute-start.29) | collective-permute-done | bytes 442400 | tf_op jit(solution)/shard_map/ppermute | solution.py:244
  114.7 2.0 %collective-permute-done.15 = bf16[8,24,1152]{2,1,0:T(8,128)(2,1)S(1)} collective-permute-done((bf16[8,24,1152]{2,1,0:T(8,128)(2,1)S(1)}, bf16[8,24,1152]{2,1,0:T(8,128)(2,1)S(1)}, u32[]{:S(2)}, u32[]{:S(2)}) %collective-permute-start.15) | collective-permute-done | bytes 442400 | tf_op jit(solution)/shard_map/ppermute | solution.py:244
  117.3 1.8 %collective-permute-done.20 = bf16[4,24,1152]{2,1,0:T(8,128)(2,1)S(1)} collective-permute-done((bf16[4,24,1152]{2,1,0:T(8,128)(2,1)S(1)}, bf16[4,24,1152]{2,1,0:T(8,128)(2,1)S(1)}, u32[]{:S(2)}, u32[]{:S(2)}) %collective-permute-start.20) | collective-permute-done | bytes 221216 | tf_op jit(solution)/shard_map/ppermute | solution.py:244
  121.4 2.6 %collective-permute-done.16 = bf16[4,24,1152]{2,1,0:T(8,128)(2,1)S(1)} collective-permute-done((bf16[4,24,1152]{2,1,0:T(8,128)(2,1)S(1)}, bf16[4,24,1152]{2,1,0:T(8,128)(2,1)S(1)}, u32[]{:S(2)}, u32[]{:S(2)}) %collective-permute-start.16) | collective-permute-done | bytes 221216 | tf_op jit(solution)/shard_map/ppermute | solution.py:244
  124.1 2.7 %collective-permute-start.17 = (bf16[2,24,1152]{2,1,0:T(8,128)(2,1)S(1)}, bf16[2,24,1152]{2,1,0:T(8,128)(2,1)S(1)}, u32[]{:S(2)}, u32[]{:S(2)}) collective-permute-start(bf16[2,24,1152]{2,1,0:T(8,128)(2,1)S(1)} %get-tuple-element.63), channel_id=1, source_target_pairs={{0,64},{8,72},{16,80},{24,88},{32,96},{40,104},{48,112},{56,120},{... | collective-permute-start | bytes 331784 | tf_op jit(solution)/shard_map/ppermute | solution.py:244
  126.8 2.0 %collective-permute-start.22 = (bf16[1,24,1152]{2,1,0:T(8,128)(2,1)S(1)}, bf16[1,24,1152]{2,1,0:T(8,128)(2,1)S(1)}, u32[]{:S(2)}, u32[]{:S(2)}) collective-permute-start(bf16[1,24,1152]{2,1,0:T(8,128)(2,1)S(1)} %add_convert_fusion.29), channel_id=1, source_target_pairs={{0,24},{8,48},{16,40},{24,0},{32,56},{40,16},{48,8},{56,32},{64,88... | collective-permute-start | bytes 165896 | tf_op jit(solution)/shard_map/ppermute | solution.py:244
  128.8 2.3 %collective-permute-start.27 = (bf16[1,24,1152]{2,1,0:T(8,128)(2,1)S(1)}, bf16[1,24,1152]{2,1,0:T(8,128)(2,1)S(1)}, u32[]{:S(2)}, u32[]{:S(2)}) collective-permute-start(bf16[1,24,1152]{2,1,0:T(8,128)(2,1)S(1)} %add_convert_fusion.27), channel_id=1, source_target_pairs={{0,40},{8,32},{16,56},{24,48},{32,8},{40,0},{48,24},{56,16},{64,10... | collective-permute-start | bytes 165896 | tf_op jit(solution)/shard_map/ppermute | solution.py:244
  131.2 2.0 %collective-permute-start.32 = (bf16[1,24,1152]{2,1,0:T(8,128)(2,1)S(1)}, bf16[1,24,1152]{2,1,0:T(8,128)(2,1)S(1)}, u32[]{:S(2)}, u32[]{:S(2)}) collective-permute-start(bf16[1,24,1152]{2,1,0:T(8,128)(2,1)S(1)} %add_convert_fusion.25), channel_id=1, source_target_pairs={{0,24},{8,48},{16,40},{24,0},{32,56},{40,16},{48,8},{56,32},{64,88... | collective-permute-start | bytes 165896 | tf_op jit(solution)/shard_map/ppermute | solution.py:244
  133.2 1.7 %collective-permute-start.33 = (bf16[1,24,1152]{2,1,0:T(8,128)(2,1)S(1)}, bf16[1,24,1152]{2,1,0:T(8,128)(2,1)S(1)}, u32[]{:S(2)}, u32[]{:S(2)}) collective-permute-start(bf16[1,24,1152]{2,1,0:T(8,128)(2,1)S(1)} %add_convert_fusion.31._), channel_id=1, source_target_pairs={{0,40},{8,32},{16,56},{24,48},{32,8},{40,0},{48,24},{56,16},{64,10... | collective-permute-start | bytes 165896 | tf_op jit(solution)/shard_map/ppermute | solution.py:244
  137.3 3.2 %collective-permute-done.33 = bf16[1,24,1152]{2,1,0:T(8,128)(2,1)S(1)} collective-permute-done((bf16[1,24,1152]{2,1,0:T(8,128)(2,1)S(1)}, bf16[1,24,1152]{2,1,0:T(8,128)(2,1)S(1)}, u32[]{:S(2)}, u32[]{:S(2)}) %collective-permute-start.33) | collective-permute-done | bytes 55328 | tf_op jit(solution)/shard_map/ppermute | solution.py:244
  141.4 1.6 %copy-done = bf16[8,2,4,32,768]{4,3,2,1,0:T(8,128)(2,1)} copy-done((bf16[8,2,4,32,768]{4,3,2,1,0:T(8,128)(2,1)}, bf16[8,2,4,32,768]{4,3,2,1,0:T(8,128)(2,1)S(1)}, u32[]{:S(2)}) %copy-start) | copy-done | bytes 3145752
  143.0 4.8 %shard_map.124 = (bf16[256,768]{1,0:T(8,128)(2,1)}, bf16[256,768]{1,0:T(8,128)(2,1)}) custom-call(s32[256,2]{1,0:T(8,128)} %copy.14.ids_ref, s32[256,2]{1,0:T(8,128)} %copy.15.gate_ref, bf16[1,24,1152]{2,1,0:T(8,128)(2,1)} %copy-done.14, bf16[8,2,4,32,768]{4,3,2,1,0:T(8,128)(2,1)} %copy-done), custom_call_target="tpu_custom_call" | custom-call | flops 1207959552 | bytes 7864320 | tf_op jit(solution)/shard_map/pallas_call | solution.py:194
  (104 shorter events, 21.0 us)
Async XLA Ops:
  0.6 12.9 %collective-permute-start.6 = (bf16[256,768]{1,0:T(8,128)(2,1)}, bf16[256,768]{1,0:T(8,128)(2,1)S(1)}, u32[]{:S(2)}, u32[]{:S(2)}) collective-permute-start(bf16[256,768]{1,0:T(8,128)(2,1)} %refs_6_.1), channel_id=1, source_target_pairs={{0,6},{1,7},{2,0},{3,1},{4,2},{5,3},{6,4},{7,5},{8,14},{9,15},{10,... | collective-permute-start | bytes 1179656 | tf_op jit(solution)/shard_map/ppermute | solution.py:269
  5.6 21.1 %collective-permute-start.3 = (bf16[272,768]{1,0:T(8,128)(2,1)}, bf16[272,768]{1,0:T(8,128)(2,1)S(1)}, u32[]{:S(2)}, u32[]{:S(2)}) collective-permute-start(bf16[272,768]{1,0:T(8,128)(2,1)} %shard_map.119.refs_0_), channel_id=1, source_target_pairs={{0,2},{1,3},{2,4},{3,5},{4,6},{5,7},{6,0},{7,1},{8,10},{9,11},{10,... | collective-permute-start | bytes 1253384 | tf_op jit(solution)/shard_map/ppermute | solution.py:269
  5.6 21.1 %collective-permute-start.8 = (bf16[256,768]{1,0:T(8,128)(2,1)}, bf16[256,768]{1,0:T(8,128)(2,1)}, u32[]{:S(2)}, u32[]{:S(2)}) collective-permute-start(bf16[256,768]{1,0:T(8,128)(2,1)} %refs_6_.1), channel_id=1, source_target_pairs={{0,2},{1,3},{2,4},{3,5},{4,6},{5,7},{6,0},{7,1},{8,10},{9,11},{10,... | collective-permute-start | bytes 1179656 | tf_op jit(solution)/shard_map/ppermute | solution.py:269
  6.2 20.6 %collective-permute-start.5 = (bf16[256,768]{1,0:T(8,128)(2,1)}, bf16[256,768]{1,0:T(8,128)(2,1)S(1)}, u32[]{:S(2)}, u32[]{:S(2)}) collective-permute-start(bf16[256,768]{1,0:T(8,128)(2,1)} %refs_6_.1), channel_id=1, source_target_pairs={{0,1},{1,0},{2,3},{3,2},{4,5},{5,4},{6,7},{7,6},{8,9},{9,8},{10,11... | collective-permute-start | bytes 1179656 | tf_op jit(solution)/shard_map/ppermute | solution.py:269
  6.2 23.8 %collective-permute-start.1 = (bf16[272,768]{1,0:T(8,128)(2,1)}, bf16[272,768]{1,0:T(8,128)(2,1)S(1)}, u32[]{:S(2)}, u32[]{:S(2)}) collective-permute-start(bf16[272,768]{1,0:T(8,128)(2,1)} %shard_map.119.refs_0_), channel_id=1, source_target_pairs={{0,6},{1,7},{2,0},{3,1},{4,2},{5,3},{6,4},{7,5},{8,14},{9,15},{10,... | collective-permute-start | bytes 1253384 | tf_op jit(solution)/shard_map/ppermute | solution.py:269
  13.6 16.4 %collective-permute-start = (bf16[272,768]{1,0:T(8,128)(2,1)}, bf16[272,768]{1,0:T(8,128)(2,1)S(1)}, u32[]{:S(2)}, u32[]{:S(2)}) collective-permute-start(bf16[272,768]{1,0:T(8,128)(2,1)} %shard_map.119.refs_0_), channel_id=1, source_target_pairs={{0,1},{1,0},{2,3},{3,2},{4,5},{5,4},{6,7},{7,6},{8,9},{9,8},{10,11... | collective-permute-start | bytes 1253384 | tf_op jit(solution)/shard_map/ppermute | solution.py:269
  26.6 13.3 %collective-permute-start.10 = (bf16[272,768]{1,0:T(8,128)(2,1)S(1)}, bf16[272,768]{1,0:T(8,128)(2,1)S(1)}, u32[]{:S(2)}, u32[]{:S(2)}) collective-permute-start(bf16[272,768]{1,0:T(8,128)(2,1)S(1)} %collective-permute-done.3.refs_4_), channel_id=1, source_target_pairs={{0,2},{1,3},{2,4},{3,5},{4,6},{5,7},{6,0},{7,1},{8,10},{9,11},{10,... | collective-permute-start | bytes 1253384 | tf_op jit(solution)/shard_map/ppermute | solution.py:269
  26.7 13.2 %collective-permute-start.12 = (bf16[256,768]{1,0:T(8,128)(2,1)S(1)}, bf16[256,768]{1,0:T(8,128)(2,1)}, u32[]{:S(2)}, u32[]{:S(2)}) collective-permute-start(bf16[256,768]{1,0:T(8,128)(2,1)S(1)} %collective-permute-done.6.refs_8_), channel_id=1, source_target_pairs={{0,6},{1,7},{2,0},{3,1},{4,2},{5,3},{6,4},{7,5},{8,14},{9,15},{10,... | collective-permute-start | bytes 1179656 | tf_op jit(solution)/shard_map/ppermute | solution.py:269
  30.0 12.3 %collective-permute-start.4 = (bf16[272,768]{1,0:T(8,128)(2,1)S(1)}, bf16[272,768]{1,0:T(8,128)(2,1)S(1)}, u32[]{:S(2)}, u32[]{:S(2)}) collective-permute-start(bf16[272,768]{1,0:T(8,128)(2,1)S(1)} %collective-permute-done.3.refs_4_), channel_id=1, source_target_pairs={{0,1},{1,0},{2,3},{3,2},{4,5},{5,4},{6,7},{7,6},{8,9},{9,8},{10,11... | collective-permute-start | bytes 1253384 | tf_op jit(solution)/shard_map/ppermute | solution.py:269
  30.0 12.3 %collective-permute-start.2 = (bf16[272,768]{1,0:T(8,128)(2,1)S(1)}, bf16[272,768]{1,0:T(8,128)(2,1)S(1)}, u32[]{:S(2)}, u32[]{:S(2)}) collective-permute-start(bf16[272,768]{1,0:T(8,128)(2,1)S(1)} %collective-permute-done.1.refs_2_), channel_id=1, source_target_pairs={{0,1},{1,0},{2,3},{3,2},{4,5},{5,4},{6,7},{7,6},{8,9},{9,8},{10,11... | collective-permute-start | bytes 1253384 | tf_op jit(solution)/shard_map/ppermute | solution.py:269
  30.5 11.8 %collective-permute-start.9 = (bf16[256,768]{1,0:T(8,128)(2,1)}, bf16[256,768]{1,0:T(8,128)(2,1)}, u32[]{:S(2)}, u32[]{:S(2)}) collective-permute-start(bf16[256,768]{1,0:T(8,128)(2,1)} %collective-permute-done.8.refs_10_), channel_id=1, source_target_pairs={{0,1},{1,0},{2,3},{3,2},{4,5},{5,4},{6,7},{7,6},{8,9},{9,8},{10,11... | collective-permute-start | bytes 1179656 | tf_op jit(solution)/shard_map/ppermute | solution.py:269
  39.9 8.1 %collective-permute-start.11 = (bf16[272,768]{1,0:T(8,128)(2,1)S(1)}, bf16[272,768]{1,0:T(8,128)(2,1)S(1)}, u32[]{:S(2)}, u32[]{:S(2)}) collective-permute-start(bf16[272,768]{1,0:T(8,128)(2,1)S(1)} %collective-permute-done.10.refs_0_), channel_id=1, source_target_pairs={{0,1},{1,0},{2,3},{3,2},{4,5},{5,4},{6,7},{7,6},{8,9},{9,8},{10,11... | collective-permute-start | bytes 1253384 | tf_op jit(solution)/shard_map/ppermute | solution.py:269
  39.9 8.0 %collective-permute-start.13 = (bf16[256,768]{1,0:T(8,128)(2,1)}, bf16[256,768]{1,0:T(8,128)(2,1)}, u32[]{:S(2)}, u32[]{:S(2)}) collective-permute-start(bf16[256,768]{1,0:T(8,128)(2,1)} %collective-permute-done.12.refs_2_), channel_id=1, source_target_pairs={{0,1},{1,0},{2,3},{3,2},{4,5},{5,4},{6,7},{7,6},{8,9},{9,8},{10,11... | collective-permute-start | bytes 1179656 | tf_op jit(solution)/shard_map/ppermute | solution.py:269
  60.1 23.6 %collective-permute-start.18 = (bf16[16,24,1152]{2,1,0:T(8,128)(2,1)}, bf16[16,24,1152]{2,1,0:T(8,128)(2,1)}, u32[]{:S(2)}, u32[]{:S(2)}) collective-permute-start(bf16[16,24,1152]{2,1,0:T(8,128)(2,1)} %get-tuple-element.32), channel_id=1, source_target_pairs={{0,64},{8,72},{16,80},{24,88},{32,96},{40,104},{48,112},{56,120},{... | collective-permute-start | bytes 2654216 | tf_op jit(solution)/shard_map/ppermute | solution.py:244
  60.7 24.9 %collective-permute-start.23 = (bf16[16,24,1152]{2,1,0:T(8,128)(2,1)}, bf16[16,24,1152]{2,1,0:T(8,128)(2,1)}, u32[]{:S(2)}, u32[]{:S(2)}) collective-permute-start(bf16[16,24,1152]{2,1,0:T(8,128)(2,1)} %get-tuple-element.34), channel_id=1, source_target_pairs={{0,192},{8,200},{16,208},{24,216},{32,224},{40,232},{48,240},{56,2... | collective-permute-start | bytes 2654216 | tf_op jit(solution)/shard_map/ppermute | solution.py:244
  73.0 21.9 %collective-permute-start.28 = (bf16[16,24,1152]{2,1,0:T(8,128)(2,1)}, bf16[16,24,1152]{2,1,0:T(8,128)(2,1)}, u32[]{:S(2)}, u32[]{:S(2)}) collective-permute-start(bf16[16,24,1152]{2,1,0:T(8,128)(2,1)} %get-tuple-element.36), channel_id=1, source_target_pairs={{0,8},{8,0},{16,24},{24,16},{32,40},{40,32},{48,56},{56,48},{64,72... | collective-permute-start | bytes 2654216 | tf_op jit(solution)/shard_map/ppermute | solution.py:244
  75.0 27.0 %collective-permute-start.14 = (bf16[16,24,1152]{2,1,0:T(8,128)(2,1)}, bf16[16,24,1152]{2,1,0:T(8,128)(2,1)}, u32[]{:S(2)}, u32[]{:S(2)}) collective-permute-start(bf16[16,24,1152]{2,1,0:T(8,128)(2,1)} %get-tuple-element.27), channel_id=1, source_target_pairs={{0,56},{8,16},{16,8},{24,32},{32,24},{40,48},{48,40},{56,0},{64,12... | collective-permute-start | bytes 2654216 | tf_op jit(solution)/shard_map/ppermute | solution.py:244
  80.0 61.4 %all-to-all-start = ((bf16[8,2,4,32,768]{4,3,2,1,0:T(8,128)(2,1)}), bf16[8,2,4,32,768]{4,3,2,1,0:T(8,128)(2,1)S(1)}, u32[]{:S(2)}, u32[]{:S(2)}) async-start(bf16[8,2,4,32,768]{4,3,2,1,0:T(8,128)(2,1)} %get-tuple-element.28), calls=%async_computation | async-start | bytes 6291456 | tf_op jit(solution)/shard_map/all_to_all | solution.py:289
  85.4 18.3 %collective-permute-start.19 = (bf16[8,24,1152]{2,1,0:T(8,128)(2,1)S(1)}, bf16[8,24,1152]{2,1,0:T(8,128)(2,1)S(1)}, u32[]{:S(2)}, u32[]{:S(2)}) collective-permute-start(bf16[8,24,1152]{2,1,0:T(8,128)(2,1)S(1)} %get-tuple-element.38), channel_id=1, source_target_pairs={{0,192},{8,200},{16,208},{24,216},{32,224},{40,232},{48,240},{56,2... | collective-permute-start | bytes 1327112 | tf_op jit(solution)/shard_map/ppermute | solution.py:244
  87.0 18.9 %collective-permute-start.24 = (bf16[8,24,1152]{2,1,0:T(8,128)(2,1)S(1)}, bf16[8,24,1152]{2,1,0:T(8,128)(2,1)S(1)}, u32[]{:S(2)}, u32[]{:S(2)}) collective-permute-start(bf16[8,24,1152]{2,1,0:T(8,128)(2,1)S(1)} %get-tuple-element.40), channel_id=1, source_target_pairs={{0,64},{8,72},{16,80},{24,88},{32,96},{40,104},{48,112},{56,120},{... | collective-permute-start | bytes 1327112 | tf_op jit(solution)/shard_map/ppermute | solution.py:244
  96.3 16.8 %collective-permute-start.29 = (bf16[8,24,1152]{2,1,0:T(8,128)(2,1)S(1)}, bf16[8,24,1152]{2,1,0:T(8,128)(2,1)S(1)}, u32[]{:S(2)}, u32[]{:S(2)}) collective-permute-start(bf16[8,24,1152]{2,1,0:T(8,128)(2,1)S(1)} %get-tuple-element.42), channel_id=1, source_target_pairs={{0,56},{8,16},{16,8},{24,32},{32,24},{40,48},{48,40},{56,0},{64,12... | collective-permute-start | bytes 1327112 | tf_op jit(solution)/shard_map/ppermute | solution.py:244
  103.4 13.3 %collective-permute-start.15 = (bf16[8,24,1152]{2,1,0:T(8,128)(2,1)S(1)}, bf16[8,24,1152]{2,1,0:T(8,128)(2,1)S(1)}, u32[]{:S(2)}, u32[]{:S(2)}) collective-permute-start(bf16[8,24,1152]{2,1,0:T(8,128)(2,1)S(1)} %get-tuple-element.44), channel_id=1, source_target_pairs={{0,8},{8,0},{16,24},{24,16},{32,40},{40,32},{48,56},{56,48},{64,72... | collective-permute-start | bytes 1327112 | tf_op jit(solution)/shard_map/ppermute | solution.py:244
  103.8 15.2 %collective-permute-start.20 = (bf16[4,24,1152]{2,1,0:T(8,128)(2,1)S(1)}, bf16[4,24,1152]{2,1,0:T(8,128)(2,1)S(1)}, u32[]{:S(2)}, u32[]{:S(2)}) collective-permute-start(bf16[4,24,1152]{2,1,0:T(8,128)(2,1)S(1)} %get-tuple-element.46), channel_id=1, source_target_pairs={{0,8},{8,0},{16,24},{24,16},{32,40},{40,32},{48,56},{56,48},{64,72... | collective-permute-start | bytes 663560 | tf_op jit(solution)/shard_map/ppermute | solution.py:244
  106.0 13.6 %collective-permute-start.25 = (bf16[4,24,1152]{2,1,0:T(8,128)(2,1)S(1)}, bf16[4,24,1152]{2,1,0:T(8,128)(2,1)S(1)}, u32[]{:S(2)}, u32[]{:S(2)}) collective-permute-start(bf16[4,24,1152]{2,1,0:T(8,128)(2,1)S(1)} %get-tuple-element.48), channel_id=1, source_target_pairs={{0,56},{8,16},{16,8},{24,32},{32,24},{40,48},{48,40},{56,0},{64,12... | collective-permute-start | bytes 663560 | tf_op jit(solution)/shard_map/ppermute | solution.py:244
  113.2 7.4 %collective-permute-start.30 = (bf16[4,24,1152]{2,1,0:T(8,128)(2,1)S(1)}, bf16[4,24,1152]{2,1,0:T(8,128)(2,1)S(1)}, u32[]{:S(2)}, u32[]{:S(2)}) collective-permute-start(bf16[4,24,1152]{2,1,0:T(8,128)(2,1)S(1)} %get-tuple-element.50), channel_id=1, source_target_pairs={{0,64},{8,72},{16,80},{24,88},{32,96},{40,104},{48,112},{56,120},{... | collective-permute-start | bytes 663560 | tf_op jit(solution)/shard_map/ppermute | solution.py:244
  119.1 7.6 %collective-permute-start.21 = (bf16[2,24,1152]{2,1,0:T(8,128)(2,1)S(1)}, bf16[2,24,1152]{2,1,0:T(8,128)(2,1)S(1)}, u32[]{:S(2)}, u32[]{:S(2)}) collective-permute-start(bf16[2,24,1152]{2,1,0:T(8,128)(2,1)S(1)} %get-tuple-element.57), channel_id=1, source_target_pairs={{0,56},{8,16},{16,8},{24,32},{32,24},{40,48},{48,40},{56,0},{64,12... | collective-permute-start | bytes 331784 | tf_op jit(solution)/shard_map/ppermute | solution.py:244
  119.7 9.1 %collective-permute-start.26 = (bf16[2,24,1152]{2,1,0:T(8,128)(2,1)S(1)}, bf16[2,24,1152]{2,1,0:T(8,128)(2,1)S(1)}, u32[]{:S(2)}, u32[]{:S(2)}) collective-permute-start(bf16[2,24,1152]{2,1,0:T(8,128)(2,1)S(1)} %get-tuple-element.59), channel_id=1, source_target_pairs={{0,8},{8,0},{16,24},{24,16},{32,40},{40,32},{48,56},{56,48},{64,72... | collective-permute-start | bytes 331784 | tf_op jit(solution)/shard_map/ppermute | solution.py:244
  120.7 10.4 %collective-permute-start.31 = (bf16[2,24,1152]{2,1,0:T(8,128)(2,1)S(1)}, bf16[2,24,1152]{2,1,0:T(8,128)(2,1)S(1)}, u32[]{:S(2)}, u32[]{:S(2)}) collective-permute-start(bf16[2,24,1152]{2,1,0:T(8,128)(2,1)S(1)} %get-tuple-element.61), channel_id=1, source_target_pairs={{0,192},{8,200},{16,208},{24,216},{32,224},{40,232},{48,240},{56,2... | collective-permute-start | bytes 331784 | tf_op jit(solution)/shard_map/ppermute | solution.py:244
  124.1 9.1 %collective-permute-start.17 = (bf16[2,24,1152]{2,1,0:T(8,128)(2,1)S(1)}, bf16[2,24,1152]{2,1,0:T(8,128)(2,1)S(1)}, u32[]{:S(2)}, u32[]{:S(2)}) collective-permute-start(bf16[2,24,1152]{2,1,0:T(8,128)(2,1)S(1)} %get-tuple-element.63), channel_id=1, source_target_pairs={{0,64},{8,72},{16,80},{24,88},{32,96},{40,104},{48,112},{56,120},{... | collective-permute-start | bytes 331784 | tf_op jit(solution)/shard_map/ppermute | solution.py:244
  126.8 8.1 %collective-permute-start.22 = (bf16[1,24,1152]{2,1,0:T(8,128)(2,1)S(1)}, bf16[1,24,1152]{2,1,0:T(8,128)(2,1)S(1)}, u32[]{:S(2)}, u32[]{:S(2)}) collective-permute-start(bf16[1,24,1152]{2,1,0:T(8,128)(2,1)S(1)} %add_convert_fusion.29), channel_id=1, source_target_pairs={{0,24},{8,48},{16,40},{24,0},{32,56},{40,16},{48,8},{56,32},{64,88... | collective-permute-start | bytes 165896 | tf_op jit(solution)/shard_map/ppermute | solution.py:244
  128.8 7.4 %collective-permute-start.27 = (bf16[1,24,1152]{2,1,0:T(8,128)(2,1)S(1)}, bf16[1,24,1152]{2,1,0:T(8,128)(2,1)S(1)}, u32[]{:S(2)}, u32[]{:S(2)}) collective-permute-start(bf16[1,24,1152]{2,1,0:T(8,128)(2,1)S(1)} %add_convert_fusion.27), channel_id=1, source_target_pairs={{0,40},{8,32},{16,56},{24,48},{32,8},{40,0},{48,24},{56,16},{64,10... | collective-permute-start | bytes 165896 | tf_op jit(solution)/shard_map/ppermute | solution.py:244
  133.2 7.4 %collective-permute-start.33 = (bf16[1,24,1152]{2,1,0:T(8,128)(2,1)S(1)}, bf16[1,24,1152]{2,1,0:T(8,128)(2,1)S(1)}, u32[]{:S(2)}, u32[]{:S(2)}) collective-permute-start(bf16[1,24,1152]{2,1,0:T(8,128)(2,1)S(1)} %add_convert_fusion.31._), channel_id=1, source_target_pairs={{0,40},{8,32},{16,56},{24,48},{32,8},{40,0},{48,24},{56,16},{64,10... | collective-permute-start | bytes 165896 | tf_op jit(solution)/shard_map/ppermute | solution.py:244
  (20 other events, 173.2 us)
where the time goes:
time: 149 us; the launch traced here: 148 us
  waiting for transfers between devices  50.9 us (34%)
  starting transfers between devices  50.5 us (34%)
  Pallas kernels  31.2 us (21%)
  local copies, waits for them, and re-layouts  7.55 us (5%)
  other arithmetic  6.74 us (5%)
    ppermute x20, starting transfers between devices, reduce_grads(): lax.ppermute(a, 'dp', list(enumerate(partners(kind, nx, nz))))  36.1 us
    ppermute x14, waiting for transfers between devices, to(): return lax.ppermute(a, 'expert', perm)  27.1 us
    ppermute x20, waiting for transfers between devices, reduce_grads(): lax.ppermute(a, 'dp', list(enumerate(partners(kind, nx, nz))))  23.7 us
    pallas_call x2, Pallas kernels, experts(): pl.pallas_call(functools.partial(expert_kernel, first, cap, scale), grid=...  17.1 us
    ppermute x14, starting transfers between devices, to(): return lax.ppermute(a, 'expert', perm)  10.8 us
    pallas_call x2, Pallas kernels, pack(): pl.pallas_call(functools.partial(pack_kernel, n, cap, n_e), grid=(1,), in...  7.47 us
    convert_element_type x12, other arithmetic, reduce_grads(): (keep[v][half:].astype(F32) + got[v][half:].astype(F32)).astype(BF16)  6.53 us
    unnamed x36, local copies, waits for them, and re-layouts  4.91 us
  transfers between devices with their start and end apart: 35, of which 11 were waited for; matrix products, arithmetic and copies ran while one was open for 7% of the time, Pallas kernels for 10%

commit v1 on v0

--- a/solution.py
+++ b/solution.py
@@ -103,70 +103,109 @@
     )(me, *tok, *cot)
 
 
-def expert_kernel(first, cap, scale, order_ref, from_ref, near_x, far_x, near_g, far_g, wg_ref, wu_ref, wd_ref, *refs):
-    refs = refs[-8:]
-    ret, send, keep, acc = refs[0], refs[1:3], refs[3:5], refs[5:8]
+def grads_kernel(first, scale, place_ref, order_ref, near_x, far_x, near_g, far_g, wg_ref, wu_ref, wd_ref, *refs):
+    saved, send, keep, acc = refs[0], refs[1:3], refs[3:5], refs[5:8]
     step = pl.program_id(0)
     x = jnp.concatenate([near_x[0], far_x[0]], 0)
     dy = jnp.concatenate([near_g[0], far_g[0]], 0)
-    wg, wu, wd = wg_ref[0], wu_ref[0], wd_ref[0]
-    pre_gate, pre_up = dot(x, wg), dot(x, wu)
+    pre_gate, pre_up = dot(x, wg_ref[0]), dot(x, wu_ref[0])
+    hidden_grad = dot(dy, wd_ref[0])
     sig = jax.nn.sigmoid(pre_gate)
     act = pre_gate * sig
     hidden = (act * pre_up).astype(BF16)
-    hidden_grad = dot(dy, wd)
     gate_grad = (hidden_grad * pre_up * sig * (1.0 + pre_gate * (1.0 - sig))).astype(BF16)
     up_grad = (hidden_grad * act).astype(BF16)
+    ff, half = hidden.shape[1], acc[0].shape[0] // 2
+    for k, a in enumerate((hidden, gate_grad, up_grad)):
+        saved[0, :, k * ff : (k + 1) * ff] = a
     shape = acc[0].shape
     acc[0][...] = (dot(x, gate_grad, ((0,), (0,))) * scale).reshape(shape)
     acc[1][...] = (dot(x, up_grad, ((0,), (0,))) * scale).reshape(shape)
     acc[2][...] = (dot(dy, hidden, ((0,), (0,))) * scale).reshape(shape)
-    out = dot(hidden, wd, ((1,), (1,))).astype(BF16)
-    entry = (dot(gate_grad, wg, ((1,), (1,))) + dot(up_grad, wu, ((1,), (1,)))).astype(BF16)
-    for r in range(8):
-        ret[from_ref[r], 0, 0] = out[r * cap : (r + 1) * cap]
-        ret[from_ref[r], 1, 0] = entry[r * cap : (r + 1) * cap]
-    ff, half = wg.shape[1], shape[0] // 2
     for i in range(2):
 
         @pl.when(step == i)
         def _(i=i):
             for p in range(2 * half):
-                chunk = order_ref[first + i, p]
+                chunk = order_ref[place_ref[0], (first + i) * 2 * half + p]
                 to = (send if p < half else keep)[i]
                 for k in range(3):
                     to[p % half, :, k * ff : (k + 1) * ff] = acc[k][chunk].astype(BF16)
 
 
-def experts(first, order, sources, near, far, weights, ret, cap, scale, replicas):
+def expert_grads(first, place, order, near, far, weights, scale):
     n_e, d, ff = weights[0].shape
-    slots = 8 * cap
+    replicas = order.shape[0]
+    slots = near[0].shape[1] + far[0].shape[1]
     part = lambda a: pl.BlockSpec((1, *a.shape[1:]), lambda e: (first + e, 0, 0))
-    row = pl.BlockSpec((8, 2, 1, cap, d), lambda e: (0, 0, first + e, 0, 0))
     rows = [near[0], far[0], near[1], far[1]]
     chunks = jax.ShapeDtypeStruct((replicas // 2, d // replicas, 3 * ff), BF16)
     out = pl.pallas_call(
-        functools.partial(expert_kernel, first, cap, scale),
+        functools.partial(grads_kernel, first, scale),
         grid=(2,),
-        in_specs=[SCALARS] * 2
-        + [part(a) for a in (*rows, *weights)]
-        + [pl.BlockSpec(memory_space=pl.ANY)] * len(ret),
-        out_specs=[row] + [whole(chunks.shape)] * 4,
-        out_shape=[jax.ShapeDtypeStruct((8, 2, n_e, cap, d), BF16)] + [chunks] * 4,
-        input_output_aliases={9: 0} if ret else {},
+        in_specs=[SCALARS] * 2 + [part(a) for a in (*rows, *weights)],
+        out_specs=[pl.BlockSpec((1, slots, 3 * ff), lambda e: (e, 0, 0))] + [whole(chunks.shape)] * 4,
+        out_shape=[jax.ShapeDtypeStruct((2, slots, 3 * ff), BF16)] + [chunks] * 4,
         scratch_shapes=[pltpu.VMEM((replicas, d // replicas, ff), F32)] * 3,
         compiler_params=ROOM,
         cost_estimate=pl.CostEstimate(
-            flops=36 * slots * d * ff, bytes_accessed=24 * d * ff + 16 * slots * d, transcendentals=2 * slots * ff
+            flops=24 * slots * d * ff, bytes_accessed=24 * d * ff + 8 * slots * d, transcendentals=2 * slots * ff
         ),
-    )(order, sources, *rows, *weights, *ret)
-    return out[:1], out[1:3], out[3:5]
+    )(place, order, *rows, *weights)
+    return out[0], out[1:3], out[3:5]
+
+
+def returns_kernel(cap, order, me_ref, saved_a, saved_b, wg_ref, wu_ref, wd_ref, ret):
+    step = pl.program_id(0)
+    half = pl.num_programs(0) // 2
+    saved = jnp.where(step < half, saved_a[0], saved_b[0])
+    ff = saved.shape[1] // 3
+    hidden, gate_grad, up_grad = saved[:, :ff], saved[:, ff : 2 * ff], saved[:, 2 * ff :]
+    out = dot(hidden, wd_ref[0], ((1,), (1,))).astype(BF16)
+    entry = dot(gate_grad, wg_ref[0], ((1,), (1,))) + dot(up_grad, wu_ref[0], ((1,), (1,)))
+    entry = entry.astype(BF16)
+    me, ny = me_ref[0], ret.shape[0] // 2
+    for r, (dy, dc) in enumerate(order):
+        source = lax.rem(me // 2 + dy, ny) * 2 + lax.rem(me + dc, 2)
+        ret[source, 0, 0] = out[r * cap : (r + 1) * cap]
+        ret[source, 1, 0] = entry[r * cap : (r + 1) * cap]
+
+
+def expert_returns(me, order, saved_a, saved_b, weights, cap):
+    n_e, d, ff = weights[0].shape
+    half, slots = n_e // 2, saved_a.shape[1]
+    weight = pl.BlockSpec((1, d, ff), lambda e: (e, 0, 0))
+    block = (1, slots, 3 * ff)
+    return pl.pallas_call(
+        functools.partial(returns_kernel, cap, order),
+        grid=(n_e,),
+        in_specs=[
+            SCALARS,
+            pl.BlockSpec(block, lambda e: (jnp.minimum(e, half - 1), 0, 0)),
+            pl.BlockSpec(block, lambda e: (jnp.maximum(e - half, 0), 0, 0)),
+        ]
+        + [weight] * 3,
+        out_specs=pl.BlockSpec((8, 2, 1, cap, d), lambda e: (0, 0, e, 0, 0)),
+        out_shape=jax.ShapeDtypeStruct((8, 2, n_e, cap, d), BF16),
+        compiler_params=ROOM,
+        cost_estimate=pl.CostEstimate(
+            flops=6 * n_e * slots * d * ff,
+            bytes_accessed=6 * n_e * (d * ff + slots * ff) + 4 * n_e * slots * d,
+            transcendentals=0,
+        ),
+    )(me, saved_a, saved_b, *weights)
+
+
+def columns(a):
+    a = a.astype(F32)
+    return jnp.concatenate([a, jnp.zeros((8 - a.shape[0], a.shape[1]), F32)], 0).T
 
 
 def combine_kernel(cap, ids_ref, gate_ref, _, ret, out_ref, grad_ref):
-    n_t, count = ids_ref.shape[0], ret.shape[0] * ret.shape[2]
-    eid = lax.broadcasted_iota(jnp.int32, (n_t, count), 1)
-    first, second = ids_ref[:, 0:1] == eid, ids_ref[:, 1:2] == eid
+    n_t, count = ids_ref.shape[1], ret.shape[0] * ret.shape[2]
+    eid = lax.broadcasted_iota(jnp.int32, (n_t, count), 1).astype(F32)
+    ids = columns(ids_ref[...])
+    first, second = ids[:, 0:1] == eid, ids[:, 1:2] == eid
     mask = jnp.where(first | second, 1.0, 0.0).astype(BF16)
     rank = dot(less_than(n_t, True), mask)
     rows = lax.broadcasted_iota(jnp.int32, (count, count * cap), 0)
@@ -181,7 +220,7 @@
     hots = [h.astype(BF16) for h in hots]
     outs = ret[:, 0].reshape(count * cap, ret.shape[-1])
     grads = ret[:, 1].reshape(count * cap, ret.shape[-1])
-    gate = gate_ref[...].astype(F32) / 65536.0
+    gate = columns(gate_ref[...]) / 65536.0
     total = gate[:, 0:1] * dot(hots[0], outs) + gate[:, 1:2] * dot(hots[1], outs)
     out_ref[...] = total.astype(BF16)
     grad_ref[...] = dot(both, grads).astype(BF16)
@@ -189,7 +228,7 @@
 
 def combine(ids, gate, after, ret):
     peers, _, n_e, cap, d = ret.shape
-    n_t = ids.shape[0]
+    n_t = ids.shape[1]
     row = jax.ShapeDtypeStruct((n_t, d), BF16)
     return pl.pallas_call(
         functools.partial(combine_kernel, cap),
@@ -197,7 +236,7 @@
         in_specs=[whole(ids.shape), whole(gate.shape), pl.BlockSpec(memory_space=pl.ANY), whole(ret.shape)],
         out_specs=[whole(row.shape)] * 2,
         out_shape=[row, row],
-        compiler_params=ROOM,
+        compiler_params=pltpu.CompilerParams(vmem_limit_bytes=24 * 2**20),
         cost_estimate=pl.CostEstimate(
             flops=6 * n_t * d * peers * n_e * cap, bytes_accessed=40 * n_t * d, transcendentals=0
         ),
@@ -246,7 +285,7 @@
     for k in range(steps):
         got = [swap(send[v], PLANS[v][k]) for v in range(4)]
         if k == steps - 1:
-            return [keep[v].astype(F32) + got[v].astype(F32) for v in range(4)], send
+            return keep, got, send
         half = keep[0].shape[0] // 2
         for v in range(4):
             send[v] = (keep[v][:half].astype(F32) + got[v][:half].astype(F32)).astype(BF16)
@@ -268,27 +307,33 @@
         perm = [(y * 2 + c, ((y + dy) % ny) * 2 + (c ^ dc)) for y in range(ny) for c in range(2)]
         return lax.ppermute(a, "expert", perm)
 
-    tok = {(0, 0): with_meta(expert_ids.T, gate_fixed.T, tokens)}
+    ids, gate = expert_ids.T, gate_fixed.T
+    tok = {(0, 0): with_meta(ids, gate, tokens)}
     cot = {(0, 0): cotangent}
-    tok[3, 0], cot[1, 0] = to(tok[0, 0], 1, 0), to(cot[0, 0], -1, 0)
-    cot[3, 0], tok[1, 0] = to(cot[0, 0], 1, 0), to(tok[0, 0], -1, 0)
-    tok[2, 0], cot[2, 0] = to(tok[3, 0], 1, 0), to(cot[1, 0], -1, 0)
-    for dy in range(4):
-        tok[dy, 1], cot[dy, 1] = to(tok[dy, 0], 0, 1), to(cot[dy, 0], 0, 1)
-    order = [(dy, dc) for dy in (0, 1, 3, 2) for dc in range(2)]
-    mine = me.reshape(1)
+    tok[3, 0], cot[1, 0] = to(tok[0, 0], 1, 0), to(cotangent, -1, 0)
+    tok[0, 1], cot[0, 1] = to(tok[0, 0], 0, 1), to(cotangent, 0, 1)
+    own_t, own_c, tok[3, 0], cot[1, 0] = lax.optimization_barrier((tok[0, 0], cotangent, tok[3, 0], cot[1, 0]))
+    cot[3, 0], tok[1, 0] = to(own_c, 1, 0), to(own_t, -1, 0)
+    tok[3, 1], cot[1, 1] = to(tok[3, 0], 0, 1), to(cot[1, 0], 0, 1)
+    by_t, by_c, cot[3, 0], tok[1, 0] = lax.optimization_barrier((tok[3, 0], cot[1, 0], cot[3, 0], tok[1, 0]))
+    tok[2, 0], cot[2, 0] = to(by_t, 1, 0), to(by_c, -1, 0)
+    cot[3, 1], tok[1, 1] = to(cot[3, 0], 0, 1), to(tok[1, 0], 0, 1)
+    order = tuple((dy, dc) for dy in (0, 1, 3, 2) for dc in range(2))
+    mine, here = me.reshape(1), place.reshape(1)
     near = pack(mine, [tok[r] for r in order[:6]], [cot[r] for r in order[:6]], cap, n_e)
+    near, tok[2, 0], cot[2, 0] = lax.optimization_barrier((near, tok[2, 0], cot[2, 0]))
+    tok[2, 1], cot[2, 1] = to(tok[2, 0], 0, 1), to(cot[2, 0], 0, 1)
     far = pack(mine, [tok[r] for r in order[6:]], [cot[r] for r in order[6:]], cap, n_e)
-    chunk_order = lax.dynamic_index_in_dim(jnp.asarray(chunk_orders(nx, nz)), place, 0, keepdims=False)
+    chunks = jnp.asarray(chunk_orders(nx, nz).reshape(replicas, -1))
     weights = (w_gate, w_up, w_down)
-    y, c = me // 2, me % 2
-    sources = jnp.stack([((y + dy) % ny) * 2 + (c + dc) % 2 for dy, dc in order])
-    ret, send_a, keep_a = experts(0, chunk_order, sources, near, far, weights, [], cap, scale, replicas)
-    ret, send_b, keep_b = experts(2, chunk_order, sources, near, far, weights, ret, cap, scale, replicas)
-    total, last = reduce_grads((*send_a, *send_b), (*keep_a, *keep_b), nx, nz)
-    back = lax.all_to_all(ret[0], "expert", split_axis=0, concat_axis=0, tiled=True)
-    layer_out, input_grad = combine(expert_ids, gate_fixed, last[-1], back)
-    total = jnp.concatenate(total, 0)
+    saved_a, send_a, keep_a = expert_grads(0, here, chunks, near, far, weights, scale)
+    saved_b, send_b, keep_b = expert_grads(2, here, chunks, near, far, weights, scale)
+    keep, got, last = reduce_grads((*send_a, *send_b), (*keep_a, *keep_b), nx, nz)
+    ret = expert_returns(mine, order, saved_a, saved_b, weights, cap)
+    back = lax.all_to_all(ret, "expert", split_axis=0, concat_axis=0, tiled=True)
+    layer_out, input_grad = combine(ids, gate, last[-1], back)
+    got, layer_out = lax.optimization_barrier((got, layer_out))
+    total = jnp.concatenate([a.astype(F32) + b.astype(F32) for a, b in zip(keep, got)], 0)
     return (layer_out, input_grad, total[:, :, :ff], total[:, :, ff : 2 * ff], total[:, :, 2 * ff :])
 
 

time: 149 us -> 140 us (0.940)
  waiting for transfers between devices: 50.9 us -> 40.9 us
  other arithmetic: 6.74 us -> 10.4 us
  starting transfers between devices: 50.5 us -> 47.4 us
  Pallas kernels: 31.2 us -> 34 us
  local copies, waits for them, and re-layouts: 7.55 us -> 5.22 us
    ppermute x20, waiting for transfers between devices: 23.7 us -> 15.7 us  [reduce_grads(): lax.ppermute(a, 'dp', list(enumerate(partners(kind, nx, nz))))]
    pallas_call x2 -> x3, Pallas kernels: 17.1 us -> 21.8 us  [the longest x2 14.6 us: expert_grads(): pl.pallas_call(functools.partial(grads_kernel, first, scale), grid=(2,),...]
    ppermute x20, starting transfers between devices: 36.1 us -> 32.3 us  [reduce_grads(): lax.ppermute(a, 'dp', list(enumerate(partners(kind, nx, nz))))]
    convert_element_type x4, other arithmetic: 0.06 us -> 2.01 us  [reduce_grads(): (keep[v][:half].astype(F32) + got[v][:half].astype(F32)).astype(BF16)]
    ppermute x14, waiting for transfers between devices: 27.1 us -> 25.3 us  [to(): return lax.ppermute(a, 'expert', perm)]
    pallas_call x1, Pallas kernels: 4.78 us -> 2.97 us  [combine(): pl.pallas_call(functools.partial(combine_kernel, cap), grid=(1,), in_spec...]
    add x4 -> x2, other arithmetic: 0.11 us -> 1.77 us  [shards(): a.astype(F32) + b.astype(F32)]
    unnamed x36 -> x54, local copies, waits for them, and re-layouts: 4.91 us -> 4.45 us
  transfers between devices with their start and end apart: 35 -> 35, of which waited for: 11 -> 13; matrix products, arithmetic and copies ran while one was open for 7% -> 6% of each run, Pallas kernels for 10% -> 16%
where the time goes in v1:
time: 140 us; the launch traced here: 139 us
  starting transfers between devices  47.4 us (34%)
  waiting for transfers between devices  40.9 us (29%)
  Pallas kernels  34 us (24%)
  other arithmetic  10.4 us (7%)
  local copies, waits for them, and re-layouts  5.22 us (4%)
    ppermute x20, starting transfers between devices, reduce_grads(): lax.ppermute(a, 'dp', list(enumerate(partners(kind, nx, nz))))  32.3 us
    ppermute x14, waiting for transfers between devices, to(): return lax.ppermute(a, 'expert', perm)  25.3 us
    ppermute x20, waiting for transfers between devices, reduce_grads(): lax.ppermute(a, 'dp', list(enumerate(partners(kind, nx, nz))))  15.7 us
    pallas_call x2, Pallas kernels, expert_grads(): pl.pallas_call(functools.partial(grads_kernel, first, scale), grid=(2,),...  14.6 us
    ppermute x14, starting transfers between devices, to(): return lax.ppermute(a, 'expert', perm)  10.6 us
    pallas_call x2, Pallas kernels, pack(): pl.pallas_call(functools.partial(pack_kernel, n, cap, n_e), grid=(1,), in...  7.44 us
    pallas_call x1, Pallas kernels, expert_returns(): pl.pallas_call(functools.partial(returns_kernel, cap, order), grid=(n_e,)...  7.19 us
    convert_element_type x12, other arithmetic, reduce_grads(): (keep[v][half:].astype(F32) + got[v][half:].astype(F32)).astype(BF16)  6.54 us
  transfers between devices with their start and end apart: 35, of which 13 were waited for; matrix products, arithmetic and copies ran while one was open for 6% of the time, Pallas kernels for 16%

profile of v1, /device:TPU:2, one launch (start us, length us, event | category | flops | bytes accessed | tf_op | source)
XLA Modules:
  0.0 139.0 jit_solution(18131546034512635078)
XLA Ops:
  0.6 1.8 %shard_map.119.refs_0_ = bf16[272,768]{1,0:T(8,128)(2,1)} custom-call(s32[2,256]{1,0:T(2,128)} %bitcast.4, s32[2,256]{1,0:T(2,128)} %bitcast.6, bf16[256,768]{1,0:T(8,128)(2,1)} %tok_ref.1), custom_call_target="tpu_custom_call" | custom-call | flops 196608 | bytes 786432 | tf_op jit(solution)/shard_map/pallas_call | solution.py:46
  4.1 1.7 %collective-permute-start.2 = (bf16[256,768]{1,0:T(8,128)(2,1)}, bf16[256,768]{1,0:T(8,128)(2,1)S(1)}, u32[]{:S(2)}, u32[]{:S(2)}) collective-permute-start(bf16[256,768]{1,0:T(8,128)(2,1)} %refs_6_.1), channel_id=1, source_target_pairs={{0,6},{1,7},{2,0},{3,1},{4,2},{5,3},{6,4},{7,5},{8,14},{9,15},{10,... | collective-permute-start | bytes 1179656 | tf_op jit(solution)/shard_map/ppermute | solution.py:308
  5.7 9.1 %collective-permute-done.2.refs_8_ = bf16[256,768]{1,0:T(8,128)(2,1)S(1)} collective-permute-done((bf16[256,768]{1,0:T(8,128)(2,1)}, bf16[256,768]{1,0:T(8,128)(2,1)S(1)}, u32[]{:S(2)}, u32[]{:S(2)}) %collective-permute-start.2) | collective-permute-done | bytes 393248 | tf_op jit(solution)/shard_map/ppermute | solution.py:308
  15.3 2.5 %collective-permute-start.4 = (bf16[272,768]{1,0:T(8,128)(2,1)}, bf16[272,768]{1,0:T(8,128)(2,1)S(1)}, u32[]{:S(2)}, u32[]{:S(2)}) collective-permute-start(bf16[272,768]{1,0:T(8,128)(2,1)} %shard_map.119.refs_0_), channel_id=1, source_target_pairs={{0,6},{1,7},{2,0},{3,1},{4,2},{5,3},{6,4},{7,5},{8,14},{9,15},{10,... | collective-permute-start | bytes 1253384 | tf_op jit(solution)/shard_map/ppermute | solution.py:308
  18.4 10.4 %collective-permute-done.3.refs_10_ = bf16[256,768]{1,0:T(8,128)(2,1)S(1)} collective-permute-done((bf16[256,768]{1,0:T(8,128)(2,1)}, bf16[256,768]{1,0:T(8,128)(2,1)S(1)}, u32[]{:S(2)}, u32[]{:S(2)}) %collective-permute-start.3) | collective-permute-done | bytes 393248 | tf_op jit(solution)/shard_map/ppermute | solution.py:308
  30.8 3.2 %collective-permute-start.11 = (bf16[256,768]{1,0:T(8,128)(2,1)S(1)}, bf16[256,768]{1,0:T(8,128)(2,1)}, u32[]{:S(2)}, u32[]{:S(2)}) collective-permute-start(bf16[256,768]{1,0:T(8,128)(2,1)S(1)} %collective-permute-done.2.refs_8_), channel_id=1, source_target_pairs={{0,6},{1,7},{2,0},{3,1},{4,2},{5,3},{6,4},{7,5},{8,14},{9,15},{10,... | collective-permute-start | bytes 1179656 | tf_op jit(solution)/shard_map/ppermute | solution.py:308
  34.9 4.7 %shard_map.120 = (bf16[4,192,768]{2,1,0:T(8,128)(2,1)}, bf16[4,192,768]{2,1,0:T(8,128)(2,1)}) custom-call(s32[1]{0:T(128)} %bitcast.1.me_ref, bf16[272,768]{1,0:T(8,128)(2,1)} %shard_map.119.refs_0_, bf16[272,768]{1,0:T(8,128)(2,1)} %copy-done.9, bf16[272,768]{1,0:T(8,128)(2,1)} %copy-done.8, bf16[272,768]{1,0:T(8,128)(2,1)} %copy-done.11, ...), custom_call_target="tpu_custom_call" | custom-call | flops 603979776 | bytes 7077888 | tf_op jit(solution)/shard_map/pallas_call | solution.py:93
  39.6 2.8 %collective-permute-done.11.refs_2_ = bf16[256,768]{1,0:T(8,128)(2,1)} collective-permute-done((bf16[256,768]{1,0:T(8,128)(2,1)S(1)}, bf16[256,768]{1,0:T(8,128)(2,1)}, u32[]{:S(2)}, u32[]{:S(2)}) %collective-permute-start.11) | collective-permute-done | bytes 393248 | tf_op jit(solution)/shard_map/ppermute | solution.py:308
  43.4 2.0 %collective-permute-done.13.refs_3_ = bf16[256,768]{1,0:T(8,128)(2,1)S(1)} collective-permute-done((bf16[256,768]{1,0:T(8,128)(2,1)}, bf16[256,768]{1,0:T(8,128)(2,1)S(1)}, u32[]{:S(2)}, u32[]{:S(2)}) %collective-permute-start.13) | collective-permute-done | bytes 393248 | tf_op jit(solution)/shard_map/ppermute | solution.py:308
  46.9 2.8 %shard_map.121 = (bf16[4,64,768]{2,1,0:T(8,128)(2,1)}, bf16[4,64,768]{2,1,0:T(8,128)(2,1)}) custom-call(s32[1]{0:T(128)} %bitcast.1.me_ref, bf16[272,768]{1,0:T(8,128)(2,1)} %copy-done.12, bf16[272,768]{1,0:T(8,128)(2,1)} %copy-done.13, bf16[256,768]{1,0:T(8,128)(2,1)} %collective-permute-done.11.refs_2_, bf16[256,768]{1,0:T(8,128)(2,1)} %copy-done.18), custom_call_target="tpu_custom_call" | custom-call | flops 201326592 | bytes 2359296 | tf_op jit(solution)/shard_map/pallas_call | solution.py:93
  49.7 7.3 %shard_map.122 = (bf16[2,256,1152]{2,1,0:T(8,128)(2,1)}, bf16[16,24,1152]{2,1,0:T(8,128)(2,1)}, bf16[16,24,1152]{2,1,0:T(8,128)(2,1)}, bf16[16,24,1152]{2,1,0:T(8,128)(2,1)}, bf16[16,24,1152]{2,1,0:T(8,128)(2,1)}) custom-call(s32[1]{0:T(128)} %bitcast.place_ref, s32[32,128]{1,0:T(8,128)} %constant.11.clone.order_ref, ...), custom_call_target="tpu_custom_call" | custom-call | flops 1811939328 | bytes 8650752 | tf_op jit(solution)/shard_map/pallas_call | solution.py:143
  57.1 2.7 %collective-permute-start.19 = (bf16[16,24,1152]{2,1,0:T(8,128)(2,1)}, bf16[16,24,1152]{2,1,0:T(8,128)(2,1)}, u32[]{:S(2)}, u32[]{:S(2)}) collective-permute-start(bf16[16,24,1152]{2,1,0:T(8,128)(2,1)} %get-tuple-element.57), channel_id=1, source_target_pairs={{0,192},{8,200},{16,208},{24,216},{32,224},{40,232},{48,240},{56,2... | collective-permute-start | bytes 2654216 | tf_op jit(solution)/shard_map/ppermute | solution.py:283
  59.8 7.3 %shard_map.123 = (bf16[2,256,1152]{2,1,0:T(8,128)(2,1)}, bf16[16,24,1152]{2,1,0:T(8,128)(2,1)}, bf16[16,24,1152]{2,1,0:T(8,128)(2,1)}, bf16[16,24,1152]{2,1,0:T(8,128)(2,1)}, bf16[16,24,1152]{2,1,0:T(8,128)(2,1)}) custom-call(s32[1]{0:T(128)} %bitcast.place_ref, s32[32,128]{1,0:T(8,128)} %constant.11.clone.order_ref, ...), custom_call_target="tpu_custom_call" | custom-call | flops 1811939328 | bytes 8650752 | tf_op jit(solution)/shard_map/pallas_call | solution.py:143
  67.1 2.0 %collective-permute-start.24 = (bf16[16,24,1152]{2,1,0:T(8,128)(2,1)}, bf16[16,24,1152]{2,1,0:T(8,128)(2,1)}, u32[]{:S(2)}, u32[]{:S(2)}) collective-permute-start(bf16[16,24,1152]{2,1,0:T(8,128)(2,1)} %get-tuple-element.59), channel_id=1, source_target_pairs={{0,8},{8,0},{16,24},{24,16},{32,40},{40,32},{48,56},{56,48},{64,72... | collective-permute-start | bytes 2654216 | tf_op jit(solution)/shard_map/ppermute | solution.py:283
  69.1 4.9 %collective-permute-start.29 = (bf16[16,24,1152]{2,1,0:T(8,128)(2,1)}, bf16[16,24,1152]{2,1,0:T(8,128)(2,1)}, u32[]{:S(2)}, u32[]{:S(2)}) collective-permute-start(bf16[16,24,1152]{2,1,0:T(8,128)(2,1)} %get-tuple-element.61), channel_id=1, source_target_pairs={{0,56},{8,16},{16,8},{24,32},{32,24},{40,48},{48,40},{56,0},{64,12... | collective-permute-start | bytes 2654216 | tf_op jit(solution)/shard_map/ppermute | solution.py:283
  74.0 7.2 %shard_map.124 = bf16[8,2,4,32,768]{4,3,2,1,0:T(8,128)(2,1)} custom-call(s32[1]{0:T(128)} %bitcast.1.me_ref, bf16[2,256,1152]{2,1,0:T(8,128)(2,1)} %get-tuple-element.62.saved_a, bf16[2,256,1152]{2,1,0:T(8,128)(2,1)} %get-tuple-element.63.saved_b, bf16[4,768,384]{2,1,0:T(8,128)(2,1)} %wg_ref.5, bf16[4,768,384]{2,1,0:T(8,128)(2,1)} %wu_ref.5, ...), custom_call_target="tpu_custom_call" | custom-call | flops 1811939328 | bytes 12582912 | tf_op jit(solution)/shard_map/pallas_call | solution.py:179
  81.2 4.6 %all-to-all-start = ((bf16[8,2,4,32,768]{4,3,2,1,0:T(8,128)(2,1)}), bf16[8,2,4,32,768]{4,3,2,1,0:T(8,128)(2,1)S(1)}, u32[]{:S(2)}, u32[]{:S(2)}) async-start(bf16[8,2,4,32,768]{4,3,2,1,0:T(8,128)(2,1)} %shard_map.124), calls=%async_computation | async-start | bytes 6291456 | tf_op jit(solution)/shard_map/all_to_all | solution.py:333
  85.8 1.7 %add_convert_fusion.7 = (bf16[8,24,1152]{2,1,0:T(8,128)(2,1)S(1)}, bf16[8,24,1152]{2,1,0:T(8,128)(2,1)S(1)}) fusion(bf16[16,24,1152]{2,1,0:T(8,128)(2,1)} %collective-permute-done.14, bf16[16,24,1152]{2,1,0:T(8,128)(2,1)} %get-tuple-element.54), kind=kLoop, calls=%fused_computation.7 | loop fusion | flops 1769472 | bytes 2654208 | tf_op jit(solution)/shard_map/convert_element_type | solution.py:292
  89.1 2.6 %collective-permute-start.20 = (bf16[8,24,1152]{2,1,0:T(8,128)(2,1)S(1)}, bf16[8,24,1152]{2,1,0:T(8,128)(2,1)S(1)}, u32[]{:S(2)}, u32[]{:S(2)}) collective-permute-start(bf16[8,24,1152]{2,1,0:T(8,128)(2,1)S(1)} %get-tuple-element.76), channel_id=1, source_target_pairs={{0,64},{8,72},{16,80},{24,88},{32,96},{40,104},{48,112},{56,120},{... | collective-permute-start | bytes 1327112 | tf_op jit(solution)/shard_map/ppermute | solution.py:283
  93.1 2.8 %collective-permute-start.25 = (bf16[8,24,1152]{2,1,0:T(8,128)(2,1)S(1)}, bf16[8,24,1152]{2,1,0:T(8,128)(2,1)S(1)}, u32[]{:S(2)}, u32[]{:S(2)}) collective-permute-start(bf16[8,24,1152]{2,1,0:T(8,128)(2,1)S(1)} %get-tuple-element.74), channel_id=1, source_target_pairs={{0,56},{8,16},{16,8},{24,32},{32,24},{40,48},{48,40},{56,0},{64,12... | collective-permute-start | bytes 1327112 | tf_op jit(solution)/shard_map/ppermute | solution.py:283
  97.3 2.9 %collective-permute-done.15 = bf16[8,24,1152]{2,1,0:T(8,128)(2,1)S(1)} collective-permute-done((bf16[8,24,1152]{2,1,0:T(8,128)(2,1)S(1)}, bf16[8,24,1152]{2,1,0:T(8,128)(2,1)S(1)}, u32[]{:S(2)}, u32[]{:S(2)}) %collective-permute-start.15) | collective-permute-done | bytes 442400 | tf_op jit(solution)/shard_map/ppermute | solution.py:283
  100.4 1.9 %collective-permute-done.20 = bf16[8,24,1152]{2,1,0:T(8,128)(2,1)S(1)} collective-permute-done((bf16[8,24,1152]{2,1,0:T(8,128)(2,1)S(1)}, bf16[8,24,1152]{2,1,0:T(8,128)(2,1)S(1)}, u32[]{:S(2)}, u32[]{:S(2)}) %collective-permute-start.20) | collective-permute-done | bytes 442400 | tf_op jit(solution)/shard_map/ppermute | solution.py:283
  102.8 3.7 %collective-permute-done.25 = bf16[8,24,1152]{2,1,0:T(8,128)(2,1)S(1)} collective-permute-done((bf16[8,24,1152]{2,1,0:T(8,128)(2,1)S(1)}, bf16[8,24,1152]{2,1,0:T(8,128)(2,1)S(1)}, u32[]{:S(2)}, u32[]{:S(2)}) %collective-permute-start.25) | collective-permute-done | bytes 442400 | tf_op jit(solution)/shard_map/ppermute | solution.py:283
  106.9 3.2 %collective-permute-done.30 = bf16[8,24,1152]{2,1,0:T(8,128)(2,1)S(1)} collective-permute-done((bf16[8,24,1152]{2,1,0:T(8,128)(2,1)S(1)}, bf16[8,24,1152]{2,1,0:T(8,128)(2,1)S(1)}, u32[]{:S(2)}, u32[]{:S(2)}) %collective-permute-start.30) | collective-permute-done | bytes 442400 | tf_op jit(solution)/shard_map/ppermute | solution.py:283
  112.6 1.9 %collective-permute-start.17 = (bf16[2,24,1152]{2,1,0:T(8,128)(2,1)S(1)}, bf16[2,24,1152]{2,1,0:T(8,128)(2,1)S(1)}, u32[]{:S(2)}, u32[]{:S(2)}) collective-permute-start(bf16[2,24,1152]{2,1,0:T(8,128)(2,1)S(1)} %get-tuple-element.97), channel_id=1, source_target_pairs={{0,56},{8,16},{16,8},{24,32},{32,24},{40,48},{48,40},{56,0},{64,12... | collective-permute-start | bytes 331784 | tf_op jit(solution)/shard_map/ppermute | solution.py:283
  116.7 3.6 %collective-permute-start.32 = (bf16[2,24,1152]{2,1,0:T(8,128)(2,1)S(1)}, bf16[2,24,1152]{2,1,0:T(8,128)(2,1)S(1)}, u32[]{:S(2)}, u32[]{:S(2)}) collective-permute-start(bf16[2,24,1152]{2,1,0:T(8,128)(2,1)S(1)} %get-tuple-element.91), channel_id=1, source_target_pairs={{0,64},{8,72},{16,80},{24,88},{32,96},{40,104},{48,112},{56,120},{... | collective-permute-start | bytes 331784 | tf_op jit(solution)/shard_map/ppermute | solution.py:283
  121.0 1.9 %collective-permute-start.18 = (bf16[1,24,1152]{2,1,0:T(8,128)(2,1)}, bf16[1,24,1152]{2,1,0:T(8,128)(2,1)}, u32[]{:S(2)}, u32[]{:S(2)}) collective-permute-start(bf16[1,24,1152]{2,1,0:T(8,128)(2,1)} %add_convert_fusion.31), channel_id=1, source_target_pairs={{0,24},{8,48},{16,40},{24,0},{32,56},{40,16},{48,8},{56,32},{64,88... | collective-permute-start | bytes 165896 | tf_op jit(solution)/shard_map/ppermute | solution.py:283
  123.5 2.2 %collective-permute-start.23 = (bf16[1,24,1152]{2,1,0:T(8,128)(2,1)}, bf16[1,24,1152]{2,1,0:T(8,128)(2,1)}, u32[]{:S(2)}, u32[]{:S(2)}) collective-permute-start(bf16[1,24,1152]{2,1,0:T(8,128)(2,1)} %add_convert_fusion.30), channel_id=1, source_target_pairs={{0,40},{8,32},{16,56},{24,48},{32,8},{40,0},{48,24},{56,16},{64,10... | collective-permute-start | bytes 165896 | tf_op jit(solution)/shard_map/ppermute | solution.py:283
  126.4 1.9 %collective-permute-start.28 = (bf16[1,24,1152]{2,1,0:T(8,128)(2,1)}, bf16[1,24,1152]{2,1,0:T(8,128)(2,1)}, u32[]{:S(2)}, u32[]{:S(2)}) collective-permute-start(bf16[1,24,1152]{2,1,0:T(8,128)(2,1)} %add_convert_fusion.29), channel_id=1, source_target_pairs={{0,24},{8,48},{16,40},{24,0},{32,56},{40,16},{48,8},{56,32},{64,88... | collective-permute-start | bytes 165896 | tf_op jit(solution)/shard_map/ppermute | solution.py:283
  129.0 2.2 %collective-permute-start.33 = (bf16[1,24,1152]{2,1,0:T(8,128)(2,1)S(1)}, bf16[1,24,1152]{2,1,0:T(8,128)(2,1)}, u32[]{:S(2)}, u32[]{:S(2)}) collective-permute-start(bf16[1,24,1152]{2,1,0:T(8,128)(2,1)S(1)} %add_convert_fusion.28._), channel_id=1, source_target_pairs={{0,40},{8,32},{16,56},{24,48},{32,8},{40,0},{48,24},{56,16},{64,10... | collective-permute-start | bytes 165896 | tf_op jit(solution)/shard_map/ppermute | solution.py:283
  131.3 3.0 %shard_map.125 = (bf16[256,768]{1,0:T(8,128)(2,1)}, bf16[256,768]{1,0:T(8,128)(2,1)}) custom-call(s32[2,256]{1,0:T(2,128)S(1)} %bitcast.5, s32[2,256]{1,0:T(2,128)S(1)} %bitcast.7, bf16[1,24,1152]{2,1,0:T(8,128)(2,1)S(1)} %add_convert_fusion.28._, bf16[8,2,4,32,768]{4,3,2,1,0:T(8,128)(2,1)S(1)} %all-to-all-done.ret), custom_call_target="tpu_custom_call" | custom-call | flops 1207959552 | bytes 7864320 | tf_op jit(solution)/shard_map/pallas_call | solution.py:233
  134.3 2.1 %collective-permute-done.33 = bf16[1,24,1152]{2,1,0:T(8,128)(2,1)} collective-permute-done((bf16[1,24,1152]{2,1,0:T(8,128)(2,1)S(1)}, bf16[1,24,1152]{2,1,0:T(8,128)(2,1)}, u32[]{:S(2)}, u32[]{:S(2)}) %collective-permute-start.33) | collective-permute-done | bytes 55328 | tf_op jit(solution)/shard_map/ppermute | solution.py:283
  (119 shorter events, 23.5 us)
Async XLA Ops:
  2.5 12.9 %collective-permute-start.1 = (bf16[272,768]{1,0:T(8,128)(2,1)}, bf16[272,768]{1,0:T(8,128)(2,1)S(1)}, u32[]{:S(2)}, u32[]{:S(2)}) collective-permute-start(bf16[272,768]{1,0:T(8,128)(2,1)} %shard_map.119.refs_0_), channel_id=1, source_target_pairs={{0,2},{1,3},{2,4},{3,5},{4,6},{5,7},{6,0},{7,1},{8,10},{9,11},{10,... | collective-permute-start | bytes 1253384 | tf_op jit(solution)/shard_map/ppermute | solution.py:308
  4.1 10.8 %collective-permute-start.2 = (bf16[256,768]{1,0:T(8,128)(2,1)}, bf16[256,768]{1,0:T(8,128)(2,1)S(1)}, u32[]{:S(2)}, u32[]{:S(2)}) collective-permute-start(bf16[256,768]{1,0:T(8,128)(2,1)} %refs_6_.1), channel_id=1, source_target_pairs={{0,6},{1,7},{2,0},{3,1},{4,2},{5,3},{6,4},{7,5},{8,14},{9,15},{10,... | collective-permute-start | bytes 1179656 | tf_op jit(solution)/shard_map/ppermute | solution.py:308
  15.3 13.4 %collective-permute-start.4 = (bf16[272,768]{1,0:T(8,128)(2,1)}, bf16[272,768]{1,0:T(8,128)(2,1)S(1)}, u32[]{:S(2)}, u32[]{:S(2)}) collective-permute-start(bf16[272,768]{1,0:T(8,128)(2,1)} %shard_map.119.refs_0_), channel_id=1, source_target_pairs={{0,6},{1,7},{2,0},{3,1},{4,2},{5,3},{6,4},{7,5},{8,14},{9,15},{10,... | collective-permute-start | bytes 1253384 | tf_op jit(solution)/shard_map/ppermute | solution.py:308
  17.8 10.9 %collective-permute-start.3 = (bf16[256,768]{1,0:T(8,128)(2,1)}, bf16[256,768]{1,0:T(8,128)(2,1)S(1)}, u32[]{:S(2)}, u32[]{:S(2)}) collective-permute-start(bf16[256,768]{1,0:T(8,128)(2,1)} %refs_6_.1), channel_id=1, source_target_pairs={{0,2},{1,3},{2,4},{3,5},{4,6},{5,7},{6,0},{7,1},{8,10},{9,11},{10,... | collective-permute-start | bytes 1179656 | tf_op jit(solution)/shard_map/ppermute | solution.py:308
  17.9 11.4 %collective-permute-start.7 = (bf16[256,768]{1,0:T(8,128)(2,1)}, bf16[256,768]{1,0:T(8,128)(2,1)S(1)}, u32[]{:S(2)}, u32[]{:S(2)}) collective-permute-start(bf16[256,768]{1,0:T(8,128)(2,1)} %refs_6_.1), channel_id=1, source_target_pairs={{0,1},{1,0},{2,3},{3,2},{4,5},{5,4},{6,7},{7,6},{8,9},{9,8},{10,11... | collective-permute-start | bytes 1179656 | tf_op jit(solution)/shard_map/ppermute | solution.py:308
  17.9 12.1 %collective-permute-start = (bf16[272,768]{1,0:T(8,128)(2,1)}, bf16[272,768]{1,0:T(8,128)(2,1)S(1)}, u32[]{:S(2)}, u32[]{:S(2)}) collective-permute-start(bf16[272,768]{1,0:T(8,128)(2,1)} %shard_map.119.refs_0_), channel_id=1, source_target_pairs={{0,1},{1,0},{2,3},{3,2},{4,5},{5,4},{6,7},{7,6},{8,9},{9,8},{10,11... | collective-permute-start | bytes 1253384 | tf_op jit(solution)/shard_map/ppermute | solution.py:308
  18.4 11.6 %collective-permute-start.8 = (bf16[256,768]{1,0:T(8,128)(2,1)S(1)}, bf16[256,768]{1,0:T(8,128)(2,1)S(1)}, u32[]{:S(2)}, u32[]{:S(2)}) collective-permute-start(bf16[256,768]{1,0:T(8,128)(2,1)S(1)} %collective-permute-done.2.refs_8_), channel_id=1, source_target_pairs={{0,1},{1,0},{2,3},{3,2},{4,5},{5,4},{6,7},{7,6},{8,9},{9,8},{10,11... | collective-permute-start | bytes 1179656 | tf_op jit(solution)/shard_map/ppermute | solution.py:308
  28.7 5.3 %collective-permute-start.6 = (bf16[272,768]{1,0:T(8,128)(2,1)S(1)}, bf16[272,768]{1,0:T(8,128)(2,1)S(1)}, u32[]{:S(2)}, u32[]{:S(2)}) collective-permute-start(bf16[272,768]{1,0:T(8,128)(2,1)S(1)} %collective-permute-done.1.refs_4_), channel_id=1, source_target_pairs={{0,1},{1,0},{2,3},{3,2},{4,5},{5,4},{6,7},{7,6},{8,9},{9,8},{10,11... | collective-permute-start | bytes 1253384 | tf_op jit(solution)/shard_map/ppermute | solution.py:308
  28.7 5.3 %collective-permute-start.5 = (bf16[272,768]{1,0:T(8,128)(2,1)S(1)}, bf16[272,768]{1,0:T(8,128)(2,1)S(1)}, u32[]{:S(2)}, u32[]{:S(2)}) collective-permute-start(bf16[272,768]{1,0:T(8,128)(2,1)S(1)} %collective-permute-done.4.refs_2_), channel_id=1, source_target_pairs={{0,1},{1,0},{2,3},{3,2},{4,5},{5,4},{6,7},{7,6},{8,9},{9,8},{10,11... | collective-permute-start | bytes 1253384 | tf_op jit(solution)/shard_map/ppermute | solution.py:308
  30.0 12.9 %collective-permute-start.10 = (bf16[272,768]{1,0:T(8,128)(2,1)S(1)}, bf16[272,768]{1,0:T(8,128)(2,1)S(1)}, u32[]{:S(2)}, u32[]{:S(2)}) collective-permute-start(bf16[272,768]{1,0:T(8,128)(2,1)S(1)} %collective-permute-done.1.refs_4_), channel_id=1, source_target_pairs={{0,2},{1,3},{2,4},{3,5},{4,6},{5,7},{6,0},{7,1},{8,10},{9,11},{10,... | collective-permute-start | bytes 1253384 | tf_op jit(solution)/shard_map/ppermute | solution.py:308
  30.8 11.6 %collective-permute-start.11 = (bf16[256,768]{1,0:T(8,128)(2,1)S(1)}, bf16[256,768]{1,0:T(8,128)(2,1)}, u32[]{:S(2)}, u32[]{:S(2)}) collective-permute-start(bf16[256,768]{1,0:T(8,128)(2,1)S(1)} %collective-permute-done.2.refs_8_), channel_id=1, source_target_pairs={{0,6},{1,7},{2,0},{3,1},{4,2},{5,3},{6,4},{7,5},{8,14},{9,15},{10,... | collective-permute-start | bytes 1179656 | tf_op jit(solution)/shard_map/ppermute | solution.py:308
  57.0 28.8 %collective-permute-start.14 = (bf16[16,24,1152]{2,1,0:T(8,128)(2,1)}, bf16[16,24,1152]{2,1,0:T(8,128)(2,1)}, u32[]{:S(2)}, u32[]{:S(2)}) collective-permute-start(bf16[16,24,1152]{2,1,0:T(8,128)(2,1)} %get-tuple-element.55), channel_id=1, source_target_pairs={{0,64},{8,72},{16,80},{24,88},{32,96},{40,104},{48,112},{56,120},{... | collective-permute-start | bytes 2654216 | tf_op jit(solution)/shard_map/ppermute | solution.py:283
  57.1 30.5 %collective-permute-start.19 = (bf16[16,24,1152]{2,1,0:T(8,128)(2,1)}, bf16[16,24,1152]{2,1,0:T(8,128)(2,1)}, u32[]{:S(2)}, u32[]{:S(2)}) collective-permute-start(bf16[16,24,1152]{2,1,0:T(8,128)(2,1)} %get-tuple-element.57), channel_id=1, source_target_pairs={{0,192},{8,200},{16,208},{24,216},{32,224},{40,232},{48,240},{56,2... | collective-permute-start | bytes 2654216 | tf_op jit(solution)/shard_map/ppermute | solution.py:283
  67.1 24.7 %collective-permute-start.24 = (bf16[16,24,1152]{2,1,0:T(8,128)(2,1)}, bf16[16,24,1152]{2,1,0:T(8,128)(2,1)}, u32[]{:S(2)}, u32[]{:S(2)}) collective-permute-start(bf16[16,24,1152]{2,1,0:T(8,128)(2,1)} %get-tuple-element.59), channel_id=1, source_target_pairs={{0,8},{8,0},{16,24},{24,16},{32,40},{40,32},{48,56},{56,48},{64,72... | collective-permute-start | bytes 2654216 | tf_op jit(solution)/shard_map/ppermute | solution.py:283
  69.1 26.8 %collective-permute-start.29 = (bf16[16,24,1152]{2,1,0:T(8,128)(2,1)}, bf16[16,24,1152]{2,1,0:T(8,128)(2,1)}, u32[]{:S(2)}, u32[]{:S(2)}) collective-permute-start(bf16[16,24,1152]{2,1,0:T(8,128)(2,1)} %get-tuple-element.61), channel_id=1, source_target_pairs={{0,56},{8,16},{16,8},{24,32},{32,24},{40,48},{48,40},{56,0},{64,12... | collective-permute-start | bytes 2654216 | tf_op jit(solution)/shard_map/ppermute | solution.py:283
  81.2 50.0 %all-to-all-start = ((bf16[8,2,4,32,768]{4,3,2,1,0:T(8,128)(2,1)}), bf16[8,2,4,32,768]{4,3,2,1,0:T(8,128)(2,1)S(1)}, u32[]{:S(2)}, u32[]{:S(2)}) async-start(bf16[8,2,4,32,768]{4,3,2,1,0:T(8,128)(2,1)} %shard_map.124), calls=%async_computation | async-start | bytes 6291456 | tf_op jit(solution)/shard_map/all_to_all | solution.py:333
  87.5 12.7 %collective-permute-start.15 = (bf16[8,24,1152]{2,1,0:T(8,128)(2,1)S(1)}, bf16[8,24,1152]{2,1,0:T(8,128)(2,1)S(1)}, u32[]{:S(2)}, u32[]{:S(2)}) collective-permute-start(bf16[8,24,1152]{2,1,0:T(8,128)(2,1)S(1)} %get-tuple-element.78), channel_id=1, source_target_pairs={{0,192},{8,200},{16,208},{24,216},{32,224},{40,232},{48,240},{56,2... | collective-permute-start | bytes 1327112 | tf_op jit(solution)/shard_map/ppermute | solution.py:283
  89.1 13.2 %collective-permute-start.20 = (bf16[8,24,1152]{2,1,0:T(8,128)(2,1)S(1)}, bf16[8,24,1152]{2,1,0:T(8,128)(2,1)S(1)}, u32[]{:S(2)}, u32[]{:S(2)}) collective-permute-start(bf16[8,24,1152]{2,1,0:T(8,128)(2,1)S(1)} %get-tuple-element.76), channel_id=1, source_target_pairs={{0,64},{8,72},{16,80},{24,88},{32,96},{40,104},{48,112},{56,120},{... | collective-permute-start | bytes 1327112 | tf_op jit(solution)/shard_map/ppermute | solution.py:283
  93.1 13.4 %collective-permute-start.25 = (bf16[8,24,1152]{2,1,0:T(8,128)(2,1)S(1)}, bf16[8,24,1152]{2,1,0:T(8,128)(2,1)S(1)}, u32[]{:S(2)}, u32[]{:S(2)}) collective-permute-start(bf16[8,24,1152]{2,1,0:T(8,128)(2,1)S(1)} %get-tuple-element.74), channel_id=1, source_target_pairs={{0,56},{8,16},{16,8},{24,32},{32,24},{40,48},{48,40},{56,0},{64,12... | collective-permute-start | bytes 1327112 | tf_op jit(solution)/shard_map/ppermute | solution.py:283
  97.2 12.9 %collective-permute-start.30 = (bf16[8,24,1152]{2,1,0:T(8,128)(2,1)S(1)}, bf16[8,24,1152]{2,1,0:T(8,128)(2,1)S(1)}, u32[]{:S(2)}, u32[]{:S(2)}) collective-permute-start(bf16[8,24,1152]{2,1,0:T(8,128)(2,1)S(1)} %get-tuple-element.72), channel_id=1, source_target_pairs={{0,8},{8,0},{16,24},{24,16},{32,40},{40,32},{48,56},{56,48},{64,72... | collective-permute-start | bytes 1327112 | tf_op jit(solution)/shard_map/ppermute | solution.py:283
  100.3 12.2 %collective-permute-start.16 = (bf16[4,24,1152]{2,1,0:T(8,128)(2,1)S(1)}, bf16[4,24,1152]{2,1,0:T(8,128)(2,1)S(1)}, u32[]{:S(2)}, u32[]{:S(2)}) collective-permute-start(bf16[4,24,1152]{2,1,0:T(8,128)(2,1)S(1)} %get-tuple-element.86), channel_id=1, source_target_pairs={{0,8},{8,0},{16,24},{24,16},{32,40},{40,32},{48,56},{56,48},{64,72... | collective-permute-start | bytes 663560 | tf_op jit(solution)/shard_map/ppermute | solution.py:283
  102.4 12.1 %collective-permute-start.21 = (bf16[4,24,1152]{2,1,0:T(8,128)(2,1)S(1)}, bf16[4,24,1152]{2,1,0:T(8,128)(2,1)S(1)}, u32[]{:S(2)}, u32[]{:S(2)}) collective-permute-start(bf16[4,24,1152]{2,1,0:T(8,128)(2,1)S(1)} %get-tuple-element.84), channel_id=1, source_target_pairs={{0,56},{8,16},{16,8},{24,32},{32,24},{40,48},{48,40},{56,0},{64,12... | collective-permute-start | bytes 663560 | tf_op jit(solution)/shard_map/ppermute | solution.py:283
  106.6 8.0 %collective-permute-start.26 = (bf16[4,24,1152]{2,1,0:T(8,128)(2,1)S(1)}, bf16[4,24,1152]{2,1,0:T(8,128)(2,1)S(1)}, u32[]{:S(2)}, u32[]{:S(2)}) collective-permute-start(bf16[4,24,1152]{2,1,0:T(8,128)(2,1)S(1)} %get-tuple-element.82), channel_id=1, source_target_pairs={{0,64},{8,72},{16,80},{24,88},{32,96},{40,104},{48,112},{56,120},{... | collective-permute-start | bytes 663560 | tf_op jit(solution)/shard_map/ppermute | solution.py:283
  110.3 6.4 %collective-permute-start.31 = (bf16[4,24,1152]{2,1,0:T(8,128)(2,1)S(1)}, bf16[4,24,1152]{2,1,0:T(8,128)(2,1)S(1)}, u32[]{:S(2)}, u32[]{:S(2)}) collective-permute-start(bf16[4,24,1152]{2,1,0:T(8,128)(2,1)S(1)} %get-tuple-element.80), channel_id=1, source_target_pairs={{0,192},{8,200},{16,208},{24,216},{32,224},{40,232},{48,240},{56,2... | collective-permute-start | bytes 663560 | tf_op jit(solution)/shard_map/ppermute | solution.py:283
  112.6 7.7 %collective-permute-start.17 = (bf16[2,24,1152]{2,1,0:T(8,128)(2,1)S(1)}, bf16[2,24,1152]{2,1,0:T(8,128)(2,1)S(1)}, u32[]{:S(2)}, u32[]{:S(2)}) collective-permute-start(bf16[2,24,1152]{2,1,0:T(8,128)(2,1)S(1)} %get-tuple-element.97), channel_id=1, source_target_pairs={{0,56},{8,16},{16,8},{24,32},{32,24},{40,48},{48,40},{56,0},{64,12... | collective-permute-start | bytes 331784 | tf_op jit(solution)/shard_map/ppermute | solution.py:283
  114.5 8.3 %collective-permute-start.22 = (bf16[2,24,1152]{2,1,0:T(8,128)(2,1)S(1)}, bf16[2,24,1152]{2,1,0:T(8,128)(2,1)S(1)}, u32[]{:S(2)}, u32[]{:S(2)}) collective-permute-start(bf16[2,24,1152]{2,1,0:T(8,128)(2,1)S(1)} %get-tuple-element.95), channel_id=1, source_target_pairs={{0,8},{8,0},{16,24},{24,16},{32,40},{40,32},{48,56},{56,48},{64,72... | collective-permute-start | bytes 331784 | tf_op jit(solution)/shard_map/ppermute | solution.py:283
  114.7 11.0 %collective-permute-start.27 = (bf16[2,24,1152]{2,1,0:T(8,128)(2,1)S(1)}, bf16[2,24,1152]{2,1,0:T(8,128)(2,1)S(1)}, u32[]{:S(2)}, u32[]{:S(2)}) collective-permute-start(bf16[2,24,1152]{2,1,0:T(8,128)(2,1)S(1)} %get-tuple-element.93), channel_id=1, source_target_pairs={{0,192},{8,200},{16,208},{24,216},{32,224},{40,232},{48,240},{56,2... | collective-permute-start | bytes 331784 | tf_op jit(solution)/shard_map/ppermute | solution.py:283
  116.7 11.7 %collective-permute-start.32 = (bf16[2,24,1152]{2,1,0:T(8,128)(2,1)S(1)}, bf16[2,24,1152]{2,1,0:T(8,128)(2,1)S(1)}, u32[]{:S(2)}, u32[]{:S(2)}) collective-permute-start(bf16[2,24,1152]{2,1,0:T(8,128)(2,1)S(1)} %get-tuple-element.91), channel_id=1, source_target_pairs={{0,64},{8,72},{16,80},{24,88},{32,96},{40,104},{48,112},{56,120},{... | collective-permute-start | bytes 331784 | tf_op jit(solution)/shard_map/ppermute | solution.py:283
  121.0 13.3 %collective-permute-start.18 = (bf16[1,24,1152]{2,1,0:T(8,128)(2,1)}, bf16[1,24,1152]{2,1,0:T(8,128)(2,1)}, u32[]{:S(2)}, u32[]{:S(2)}) collective-permute-start(bf16[1,24,1152]{2,1,0:T(8,128)(2,1)} %add_convert_fusion.31), channel_id=1, source_target_pairs={{0,24},{8,48},{16,40},{24,0},{32,56},{40,16},{48,8},{56,32},{64,88... | collective-permute-start | bytes 165896 | tf_op jit(solution)/shard_map/ppermute | solution.py:283
  123.5 10.7 %collective-permute-start.23 = (bf16[1,24,1152]{2,1,0:T(8,128)(2,1)}, bf16[1,24,1152]{2,1,0:T(8,128)(2,1)}, u32[]{:S(2)}, u32[]{:S(2)}) collective-permute-start(bf16[1,24,1152]{2,1,0:T(8,128)(2,1)} %add_convert_fusion.30), channel_id=1, source_target_pairs={{0,40},{8,32},{16,56},{24,48},{32,8},{40,0},{48,24},{56,16},{64,10... | collective-permute-start | bytes 165896 | tf_op jit(solution)/shard_map/ppermute | solution.py:283
  126.4 7.9 %collective-permute-start.28 = (bf16[1,24,1152]{2,1,0:T(8,128)(2,1)}, bf16[1,24,1152]{2,1,0:T(8,128)(2,1)}, u32[]{:S(2)}, u32[]{:S(2)}) collective-permute-start(bf16[1,24,1152]{2,1,0:T(8,128)(2,1)} %add_convert_fusion.29), channel_id=1, source_target_pairs={{0,24},{8,48},{16,40},{24,0},{32,56},{40,16},{48,8},{56,32},{64,88... | collective-permute-start | bytes 165896 | tf_op jit(solution)/shard_map/ppermute | solution.py:283
  129.0 7.4 %collective-permute-start.33 = (bf16[1,24,1152]{2,1,0:T(8,128)(2,1)S(1)}, bf16[1,24,1152]{2,1,0:T(8,128)(2,1)}, u32[]{:S(2)}, u32[]{:S(2)}) collective-permute-start(bf16[1,24,1152]{2,1,0:T(8,128)(2,1)S(1)} %add_convert_fusion.28._), channel_id=1, source_target_pairs={{0,40},{8,32},{16,56},{24,48},{32,8},{40,0},{48,24},{56,16},{64,10... | collective-permute-start | bytes 165896 | tf_op jit(solution)/shard_map/ppermute | solution.py:283
  (30 other events, 191.0 us)

commit v2 on v1

--- a/solution.py
+++ b/solution.py
@@ -56,7 +56,7 @@
 
 def pack_kernel(n, cap, n_e, me_ref, *refs):
     tok, cot = refs[:n], refs[n : 2 * n]
-    rows_ref, grads_ref = refs[2 * n :]
+    rows_ref, grads_ref = refs[-2:]
     n_t = cot[0].shape[0]
     eid = (me_ref[0] * n_e + lax.broadcasted_iota(jnp.int32, (n_e, n_t), 0)).astype(F32)
     masks, gates = [], []
@@ -87,27 +87,31 @@
             grads_ref[e, r * cap : (r + 1) * cap, :] = grads[e * cap : (e + 1) * cap]
 
 
-def pack(me, tok, cot, cap, n_e):
+def pack(me, tok, cot, cap, n_e, before=()):
     n, (n_t, d) = len(cot), cot[0].shape
-    out = jax.ShapeDtypeStruct((n_e, n * cap, d), BF16)
+    out = jax.ShapeDtypeStruct((n_e, 8 * cap, d), BF16)
+    at = 8 // n - 1 if before else 0
     return pl.pallas_call(
         functools.partial(pack_kernel, n, cap, n_e),
         grid=(1,),
-        in_specs=[SCALARS] + [whole(a.shape) for a in (*tok, *cot)],
-        out_specs=[whole(out.shape)] * 2,
+        in_specs=[SCALARS]
+        + [whole(a.shape) for a in (*tok, *cot)]
+        + [pl.BlockSpec(memory_space=pl.ANY)] * len(before),
+        out_specs=[pl.BlockSpec((n_e, n * cap, d), lambda i: (0, at, 0))] * 2,
         out_shape=[out, out],
+        input_output_aliases={2 * n + 1 + i: i for i in range(len(before))},
         compiler_params=ROOM,
         cost_estimate=pl.CostEstimate(
             flops=4 * n * n_e * cap * n_t * d, bytes_accessed=4 * n * (n_t + n_e * cap) * d, transcendentals=0
         ),
-    )(me, *tok, *cot)
-
-
-def grads_kernel(first, scale, place_ref, order_ref, near_x, far_x, near_g, far_g, wg_ref, wu_ref, wd_ref, *refs):
-    saved, send, keep, acc = refs[0], refs[1:3], refs[3:5], refs[5:8]
+    )(me, *tok, *cot, *before)
+
+
+def grads_kernel(scale, place_ref, order_ref, x_ref, dy_ref, wg_ref, wu_ref, wd_ref, *refs):
+    n_e = pl.num_programs(0)
+    saved, send, keep, acc = refs[0], refs[1:5], refs[5:9], refs[9]
     step = pl.program_id(0)
-    x = jnp.concatenate([near_x[0], far_x[0]], 0)
-    dy = jnp.concatenate([near_g[0], far_g[0]], 0)
+    x, dy = x_ref[0], dy_ref[0]
     pre_gate, pre_up = dot(x, wg_ref[0]), dot(x, wu_ref[0])
     hidden_grad = dot(dy, wd_ref[0])
     sig = jax.nn.sigmoid(pre_gate)
@@ -115,50 +119,48 @@
     hidden = (act * pre_up).astype(BF16)
     gate_grad = (hidden_grad * pre_up * sig * (1.0 + pre_gate * (1.0 - sig))).astype(BF16)
     up_grad = (hidden_grad * act).astype(BF16)
-    ff, half = hidden.shape[1], acc[0].shape[0] // 2
-    for k, a in enumerate((hidden, gate_grad, up_grad)):
-        saved[0, :, k * ff : (k + 1) * ff] = a
-    shape = acc[0].shape
-    acc[0][...] = (dot(x, gate_grad, ((0,), (0,))) * scale).reshape(shape)
-    acc[1][...] = (dot(x, up_grad, ((0,), (0,))) * scale).reshape(shape)
-    acc[2][...] = (dot(dy, hidden, ((0,), (0,))) * scale).reshape(shape)
-    for i in range(2):
+    ff, replicas = hidden.shape[1], acc.shape[0]
+    half = replicas // 2
+    both = jnp.concatenate([gate_grad, up_grad], 1)
+    saved[0, :, :ff] = hidden
+    saved[0, :, ff:] = both
+    acc[:, :, : 2 * ff] = (dot(x, both, ((0,), (0,))) * scale).reshape(replicas, -1, 2 * ff)
+    acc[:, :, 2 * ff :] = (dot(dy, hidden, ((0,), (0,))) * scale).reshape(replicas, -1, ff)
+    for i in range(4):
 
         @pl.when(step == i)
         def _(i=i):
-            for p in range(2 * half):
-                chunk = order_ref[place_ref[0], (first + i) * 2 * half + p]
-                to = (send if p < half else keep)[i]
-                for k in range(3):
-                    to[p % half, :, k * ff : (k + 1) * ff] = acc[k][chunk].astype(BF16)
-
-
-def expert_grads(first, place, order, near, far, weights, scale):
+            for p in range(replicas):
+                chunk = order_ref[place_ref[0], i * replicas + p]
+                (send if p < half else keep)[i][p % half] = acc[chunk].astype(BF16)
+
+
+def expert_grads(place, order, rows, grads, weights, scale):
     n_e, d, ff = weights[0].shape
     replicas = order.shape[0]
-    slots = near[0].shape[1] + far[0].shape[1]
-    part = lambda a: pl.BlockSpec((1, *a.shape[1:]), lambda e: (first + e, 0, 0))
-    rows = [near[0], far[0], near[1], far[1]]
+    slots = rows.shape[1]
+    part = lambda a: pl.BlockSpec((1, *a.shape[1:]), lambda e: (e, 0, 0))
+    saved = jax.ShapeDtypeStruct((n_e, slots, 3 * ff), BF16)
     chunks = jax.ShapeDtypeStruct((replicas // 2, d // replicas, 3 * ff), BF16)
     out = pl.pallas_call(
-        functools.partial(grads_kernel, first, scale),
-        grid=(2,),
-        in_specs=[SCALARS] * 2 + [part(a) for a in (*rows, *weights)],
-        out_specs=[pl.BlockSpec((1, slots, 3 * ff), lambda e: (e, 0, 0))] + [whole(chunks.shape)] * 4,
-        out_shape=[jax.ShapeDtypeStruct((2, slots, 3 * ff), BF16)] + [chunks] * 4,
-        scratch_shapes=[pltpu.VMEM((replicas, d // replicas, ff), F32)] * 3,
+        functools.partial(grads_kernel, scale),
+        grid=(n_e,),
+        in_specs=[SCALARS] * 2 + [part(a) for a in (rows, grads, *weights)],
+        out_specs=[part(saved)] + [whole(chunks.shape)] * 8,
+        out_shape=[saved] + [chunks] * 8,
+        scratch_shapes=[pltpu.VMEM((replicas, d // replicas, 3 * ff), F32)],
         compiler_params=ROOM,
         cost_estimate=pl.CostEstimate(
-            flops=24 * slots * d * ff, bytes_accessed=24 * d * ff + 8 * slots * d, transcendentals=2 * slots * ff
-        ),
-    )(place, order, *rows, *weights)
-    return out[0], out[1:3], out[3:5]
-
-
-def returns_kernel(cap, order, me_ref, saved_a, saved_b, wg_ref, wu_ref, wd_ref, ret):
-    step = pl.program_id(0)
-    half = pl.num_programs(0) // 2
-    saved = jnp.where(step < half, saved_a[0], saved_b[0])
+            flops=12 * n_e * slots * d * ff,
+            bytes_accessed=n_e * (12 * d * ff + 4 * slots * d),
+            transcendentals=n_e * slots * ff,
+        ),
+    )(place, order, rows, grads, *weights)
+    return out[0], out[1:5], out[5:9]
+
+
+def returns_kernel(cap, order, me_ref, saved_ref, wg_ref, wu_ref, wd_ref, ret):
+    saved = saved_ref[0]
     ff = saved.shape[1] // 3
     hidden, gate_grad, up_grad = saved[:, :ff], saved[:, ff : 2 * ff], saved[:, 2 * ff :]
     out = dot(hidden, wd_ref[0], ((1,), (1,))).astype(BF16)
@@ -171,20 +173,14 @@
         ret[source, 1, 0] = entry[r * cap : (r + 1) * cap]
 
 
-def expert_returns(me, order, saved_a, saved_b, weights, cap):
+def expert_returns(me, order, saved, weights, cap):
     n_e, d, ff = weights[0].shape
-    half, slots = n_e // 2, saved_a.shape[1]
-    weight = pl.BlockSpec((1, d, ff), lambda e: (e, 0, 0))
-    block = (1, slots, 3 * ff)
+    slots = saved.shape[1]
+    part = lambda a: pl.BlockSpec((1, *a.shape[1:]), lambda e: (e, 0, 0))
     return pl.pallas_call(
         functools.partial(returns_kernel, cap, order),
         grid=(n_e,),
-        in_specs=[
-            SCALARS,
-            pl.BlockSpec(block, lambda e: (jnp.minimum(e, half - 1), 0, 0)),
-            pl.BlockSpec(block, lambda e: (jnp.maximum(e - half, 0), 0, 0)),
-        ]
-        + [weight] * 3,
+        in_specs=[SCALARS] + [part(a) for a in (saved, *weights)],
         out_specs=pl.BlockSpec((8, 2, 1, cap, d), lambda e: (0, 0, e, 0, 0)),
         out_shape=jax.ShapeDtypeStruct((8, 2, n_e, cap, d), BF16),
         compiler_params=ROOM,
@@ -193,7 +189,7 @@
             bytes_accessed=6 * n_e * (d * ff + slots * ff) + 4 * n_e * slots * d,
             transcendentals=0,
         ),
-    )(me, saved_a, saved_b, *weights)
+    )(me, saved, *weights)
 
 
 def columns(a):
@@ -245,9 +241,9 @@
 
 PLANS = (
     ("xp", "xq", "zp", "zq", "zf"),
-    ("xq", "xp", "zq", "zp", "zg"),
+    ("xq", "xp", "zp", "zq", "zf"),
     ("zp", "zq", "xp", "xq", "zf"),
-    ("zq", "zp", "xq", "xp", "zg"),
+    ("zq", "zp", "xp", "xq", "zg"),
 )
 FAR = {"zf": (3, 6, 5, 0, 7, 2, 1, 4), "zg": (5, 4, 7, 6, 1, 0, 3, 2)}
 
@@ -278,18 +274,67 @@
     return np.asarray(plans, np.int32).swapaxes(0, 1)
 
 
+def halve_kernel(n, plans, *refs):
+    keep, got, out = refs[:n], refs[n : 2 * n], refs[2 * n :]
+    at = 0
+    for k_ref, g_ref in zip(keep, got):
+        count = k_ref.shape[0] // plans
+        half = count // 2
+        for v in range(plans):
+            for i, ref in enumerate((out[:-1][at // half] if len(out) > 2 else out[0], out[-1])):
+                rows = pl.ds(v * count + i * half, half)
+                to = 0 if len(out) > 2 and i == 0 else at
+                ref[to : to + half] = (k_ref[rows].astype(F32) + g_ref[rows].astype(F32)).astype(BF16)
+            at += half
+
+
+def halve(keep, got, plans=1, apart=False):
+    total = sum(a.shape[0] for a in keep) // 2
+    shape = lambda count: jax.ShapeDtypeStruct((count, *keep[0].shape[1:]), BF16)
+    n = len(keep)
+    sends = [shape(total // (n * plans))] * (n * plans) if apart else [shape(total)]
+    vmem = pl.BlockSpec(memory_space=pltpu.VMEM)
+    out = pl.pallas_call(
+        functools.partial(halve_kernel, n, plans),
+        in_specs=[vmem] * (2 * n),
+        out_specs=[vmem] * (len(sends) + 1),
+        out_shape=[*sends, shape(total)],
+        compiler_params=pltpu.CompilerParams(vmem_limit_bytes=8 * 2**20),
+        cost_estimate=pl.CostEstimate(
+            flops=2 * total * keep[0][0].size, bytes_accessed=12 * total * keep[0][0].size, transcendentals=0
+        ),
+    )(*keep, *got)
+    return out[:-1], out[-1]
+
+
+def halve_plain(keep, got, plans=1, apart=False):
+    sends, kept = [], []
+    for k, g in zip(keep, got):
+        count = k.shape[0] // plans
+        half = count // 2
+        for v in range(plans):
+            a, b, c = v * count, v * count + half, (v + 1) * count
+            sends.append((k[a:b].astype(F32) + g[a:b].astype(F32)).astype(BF16))
+            kept.append((k[b:c].astype(F32) + g[b:c].astype(F32)).astype(BF16))
+    join = lambda a: a[0] if len(a) == 1 else jnp.concatenate(a, 0)
+    return (sends if apart else [join(sends)]), join(kept)
+
+
 def reduce_grads(send, keep, nx, nz):
-    send, keep = list(send), list(keep)
     swap = lambda a, kind: lax.ppermute(a, "dp", list(enumerate(partners(kind, nx, nz))))
-    steps = len(PLANS[0])
-    for k in range(steps):
-        got = [swap(send[v], PLANS[v][k]) for v in range(4)]
-        if k == steps - 1:
-            return keep, got, send
-        half = keep[0].shape[0] // 2
-        for v in range(4):
-            send[v] = (keep[v][:half].astype(F32) + got[v][:half].astype(F32)).astype(BF16)
-            keep[v] = (keep[v][half:].astype(F32) + got[v][half:].astype(F32)).astype(BF16)
+    got = [swap(send[v], PLANS[v][0]) for v in range(4)]
+    first = [halve_plain([keep[v]], [got[v]]) for v in range(4)]
+    got = [swap(first[v][0][0], PLANS[v][1]) for v in range(4)]
+    terms, sends = [], []
+    for a, b in ((0, 1), (2, 3)):
+        sent, kept = halve([first[a][1], first[b][1]], [got[a], got[b]])
+        sent, kept = halve([kept], [swap(sent[0], PLANS[a][2])], 2)
+        apart = PLANS[a][4] != PLANS[b][4]
+        sent, kept = halve([kept], [swap(sent[0], PLANS[a][3])], 2, apart)
+        last = [swap(sent[i], PLANS[v][4]) for i, v in enumerate((a, b)[: len(sent)])]
+        terms.append((kept, last))
+        sends += sent
+    return [k for k, _ in terms], [g for _, g in terms], sends
 
 
 def shards(nx, nz, tokens, expert_ids, gate_fixed, cotangent, w_gate, w_up, w_down):
@@ -310,30 +355,30 @@
     ids, gate = expert_ids.T, gate_fixed.T
     tok = {(0, 0): with_meta(ids, gate, tokens)}
     cot = {(0, 0): cotangent}
-    tok[3, 0], cot[1, 0] = to(tok[0, 0], 1, 0), to(cotangent, -1, 0)
+    cot[3, 0], cot[1, 0] = to(cotangent, 1, 0), to(cotangent, -1, 0)
     tok[0, 1], cot[0, 1] = to(tok[0, 0], 0, 1), to(cotangent, 0, 1)
-    own_t, own_c, tok[3, 0], cot[1, 0] = lax.optimization_barrier((tok[0, 0], cotangent, tok[3, 0], cot[1, 0]))
-    cot[3, 0], tok[1, 0] = to(own_c, 1, 0), to(own_t, -1, 0)
-    tok[3, 1], cot[1, 1] = to(tok[3, 0], 0, 1), to(cot[1, 0], 0, 1)
-    by_t, by_c, cot[3, 0], tok[1, 0] = lax.optimization_barrier((tok[3, 0], cot[1, 0], cot[3, 0], tok[1, 0]))
-    tok[2, 0], cot[2, 0] = to(by_t, 1, 0), to(by_c, -1, 0)
-    cot[3, 1], tok[1, 1] = to(cot[3, 0], 0, 1), to(tok[1, 0], 0, 1)
+    own, cot[3, 0], cot[1, 0] = lax.optimization_barrier((tok[0, 0], cot[3, 0], cot[1, 0]))
+    tok[3, 0], tok[1, 0] = to(own, 1, 0), to(own, -1, 0)
+    cot[3, 1], cot[1, 1] = to(cot[3, 0], 0, 1), to(cot[1, 0], 0, 1)
+    by_c, tok[3, 0], tok[1, 0] = lax.optimization_barrier((cot[3, 0], tok[3, 0], tok[1, 0]))
+    cot[2, 0], tok[2, 0] = to(by_c, 1, 0), to(tok[1, 0], -1, 0)
+    tok[3, 1], tok[1, 1] = to(tok[3, 0], 0, 1), to(tok[1, 0], 0, 1)
     order = tuple((dy, dc) for dy in (0, 1, 3, 2) for dc in range(2))
     mine, here = me.reshape(1), place.reshape(1)
     near = pack(mine, [tok[r] for r in order[:6]], [cot[r] for r in order[:6]], cap, n_e)
     near, tok[2, 0], cot[2, 0] = lax.optimization_barrier((near, tok[2, 0], cot[2, 0]))
     tok[2, 1], cot[2, 1] = to(tok[2, 0], 0, 1), to(cot[2, 0], 0, 1)
-    far = pack(mine, [tok[r] for r in order[6:]], [cot[r] for r in order[6:]], cap, n_e)
+    rows, grads = pack(mine, [tok[r] for r in order[6:]], [cot[r] for r in order[6:]], cap, n_e, near)
     chunks = jnp.asarray(chunk_orders(nx, nz).reshape(replicas, -1))
     weights = (w_gate, w_up, w_down)
-    saved_a, send_a, keep_a = expert_grads(0, here, chunks, near, far, weights, scale)
-    saved_b, send_b, keep_b = expert_grads(2, here, chunks, near, far, weights, scale)
-    keep, got, last = reduce_grads((*send_a, *send_b), (*keep_a, *keep_b), nx, nz)
-    ret = expert_returns(mine, order, saved_a, saved_b, weights, cap)
+    saved, send, keep = expert_grads(here, chunks, rows, grads, weights, scale)
+    keep, got, last = reduce_grads(send, keep, nx, nz)
+    ret = expert_returns(mine, order, saved, weights, cap)
     back = lax.all_to_all(ret, "expert", split_axis=0, concat_axis=0, tiled=True)
     layer_out, input_grad = combine(ids, gate, last[-1], back)
     got, layer_out = lax.optimization_barrier((got, layer_out))
-    total = jnp.concatenate([a.astype(F32) + b.astype(F32) for a, b in zip(keep, got)], 0)
+    total = [k.astype(F32) + jnp.concatenate(g, 0).astype(F32) for k, g in zip(keep, got)]
+    total = jnp.concatenate(total, 0)
     return (layer_out, input_grad, total[:, :, :ff], total[:, :, ff : 2 * ff], total[:, :, 2 * ff :])
 
 

time: 140 us -> 140 us (level)
  waiting for transfers between devices: 40.9 us -> 54.4 us
  starting transfers between devices: 47.4 us -> 40.4 us
  other arithmetic: 10.4 us -> 7.62 us
  local copies, waits for them, and re-layouts: 5.22 us -> 3.78 us
    ppermute x20 -> x15, waiting for transfers between devices: 15.7 us -> 27.9 us  [reduce_grads(): lax.ppermute(a, 'dp', list(enumerate(partners(kind, nx, nz))))]
    ppermute x20 -> x15, starting transfers between devices: 32.3 us -> 28 us  [reduce_grads(): lax.ppermute(a, 'dp', list(enumerate(partners(kind, nx, nz))))]
    convert_element_type x16 -> x4, other arithmetic: 8.54 us -> 5.84 us  [halve_plain(): sends.append((k[a:b].astype(F32) + g[a:b].astype(F32)).astype(BF16))]
    ppermute x14, starting transfers between devices: 10.6 us -> 8.77 us  [to(): return lax.ppermute(a, 'expert', perm)]
    pallas_call x2 -> x7, Pallas kernels: 14.6 us -> 13.1 us  [the longest x1 11.8 us: expert_grads(): pl.pallas_call(functools.partial(grads_kernel, scale), grid=(n_e,), in_sp...]
    unnamed x54 -> x34, local copies, waits for them, and re-layouts: 4.45 us -> 3.78 us
  transfers between devices with their start and end apart: 35 -> 30, of which waited for: 13 -> 14; matrix products, arithmetic and copies ran while one was open for 6% -> 4% of each run, Pallas kernels for 16% -> 13%
where the time goes in v2:
time: 140 us
  waiting for transfers between devices  54.4 us (39%)
  starting transfers between devices  40.4 us (29%)
  Pallas kernels  32.6 us (23%)
  other arithmetic  7.62 us (5%)
  local copies, waits for them, and re-layouts  3.78 us (3%)
    ppermute x15, starting transfers between devices, reduce_grads(): lax.ppermute(a, 'dp', list(enumerate(partners(kind, nx, nz))))  28 us
    ppermute x15, waiting for transfers between devices, reduce_grads(): lax.ppermute(a, 'dp', list(enumerate(partners(kind, nx, nz))))  27.9 us
    ppermute x14, waiting for transfers between devices, to(): return lax.ppermute(a, 'expert', perm)  26.5 us
    pallas_call x1, Pallas kernels, expert_grads(): pl.pallas_call(functools.partial(grads_kernel, scale), grid=(n_e,), in_sp...  11.8 us
    ppermute x14, starting transfers between devices, to(): return lax.ppermute(a, 'expert', perm)  8.77 us
    pallas_call x2, Pallas kernels, pack(): pl.pallas_call(functools.partial(pack_kernel, n, cap, n_e), grid=(1,), in...  7.58 us
    pallas_call x1, Pallas kernels, expert_returns(): pl.pallas_call(functools.partial(returns_kernel, cap, order), grid=(n_e,)...  7.16 us
    convert_element_type x4, other arithmetic, halve_plain(): sends.append((k[a:b].astype(F32) + g[a:b].astype(F32)).astype(BF16))  5.84 us
  transfers between devices with their start and end apart: 30, of which 14 were waited for; matrix products, arithmetic and copies ran while one was open for 4% of the time, Pallas kernels for 13%

profile of v2, /device:TPU:2, one launch (start us, length us, event | category | flops | bytes accessed | tf_op | source)
XLA Modules:
  0.0 139.6 jit_solution(6418248083513002230)
XLA Ops:
  0.6 3.1 %collective-permute-start.2 = (bf16[256,768]{1,0:T(8,128)(2,1)}, bf16[256,768]{1,0:T(8,128)(2,1)S(1)}, u32[]{:S(2)}, u32[]{:S(2)}) collective-permute-start(bf16[256,768]{1,0:T(8,128)(2,1)} %refs_6_.1), channel_id=1, source_target_pairs={{0,6},{1,7},{2,0},{3,1},{4,2},{5,3},{6,4},{7,5},{8,14},{9,15},{10,... | collective-permute-start | bytes 1179656 | tf_op jit(solution)/shard_map/ppermute | solution.py:353
  3.7 1.8 %shard_map.119.refs_0_ = bf16[272,768]{1,0:T(8,128)(2,1)} custom-call(s32[2,256]{1,0:T(2,128)} %bitcast.4, s32[2,256]{1,0:T(2,128)} %bitcast.6, bf16[256,768]{1,0:T(8,128)(2,1)} %tok_ref.1), custom_call_target="tpu_custom_call" | custom-call | flops 196608 | bytes 786432 | tf_op jit(solution)/shard_map/pallas_call | solution.py:46
  5.5 6.9 %collective-permute-done.2.refs_8_ = bf16[256,768]{1,0:T(8,128)(2,1)S(1)} collective-permute-done((bf16[256,768]{1,0:T(8,128)(2,1)}, bf16[256,768]{1,0:T(8,128)(2,1)S(1)}, u32[]{:S(2)}, u32[]{:S(2)}) %collective-permute-start.2) | collective-permute-done | bytes 393248 | tf_op jit(solution)/shard_map/ppermute | solution.py:353
  12.4 3.3 %collective-permute-done.1.refs_10_ = bf16[256,768]{1,0:T(8,128)(2,1)S(1)} collective-permute-done((bf16[256,768]{1,0:T(8,128)(2,1)}, bf16[256,768]{1,0:T(8,128)(2,1)S(1)}, u32[]{:S(2)}, u32[]{:S(2)}) %collective-permute-start.1) | collective-permute-done | bytes 393248 | tf_op jit(solution)/shard_map/ppermute | solution.py:353
  16.1 1.7 %collective-permute-start.3 = (bf16[272,768]{1,0:T(8,128)(2,1)}, bf16[272,768]{1,0:T(8,128)(2,1)S(1)}, u32[]{:S(2)}, u32[]{:S(2)}) collective-permute-start(bf16[272,768]{1,0:T(8,128)(2,1)} %shard_map.119.refs_0_), channel_id=1, source_target_pairs={{0,2},{1,3},{2,4},{3,5},{4,6},{5,7},{6,0},{7,1},{8,10},{9,11},{10,... | collective-permute-start | bytes 1253384 | tf_op jit(solution)/shard_map/ppermute | solution.py:353
  18.3 7.9 %collective-permute-done.4.refs_2_ = bf16[272,768]{1,0:T(8,128)(2,1)S(1)} collective-permute-done((bf16[272,768]{1,0:T(8,128)(2,1)}, bf16[272,768]{1,0:T(8,128)(2,1)S(1)}, u32[]{:S(2)}, u32[]{:S(2)}) %collective-permute-start.4) | collective-permute-done | bytes 417824 | tf_op jit(solution)/shard_map/ppermute | solution.py:353
  26.1 1.6 %collective-permute-done.3.refs_4_ = bf16[272,768]{1,0:T(8,128)(2,1)S(1)} collective-permute-done((bf16[272,768]{1,0:T(8,128)(2,1)}, bf16[272,768]{1,0:T(8,128)(2,1)S(1)}, u32[]{:S(2)}, u32[]{:S(2)}) %collective-permute-start.3) | collective-permute-done | bytes 417824 | tf_op jit(solution)/shard_map/ppermute | solution.py:353
  30.1 1.7 %collective-permute-start.11 = (bf16[256,768]{1,0:T(8,128)(2,1)S(1)}, bf16[256,768]{1,0:T(8,128)(2,1)}, u32[]{:S(2)}, u32[]{:S(2)}) collective-permute-start(bf16[256,768]{1,0:T(8,128)(2,1)S(1)} %collective-permute-done.1.refs_10_), channel_id=1, source_target_pairs={{0,2},{1,3},{2,4},{3,5},{4,6},{5,7},{6,0},{7,1},{8,10},{9,11},{10,... | collective-permute-start | bytes 1179656 | tf_op jit(solution)/shard_map/ppermute | solution.py:353
  32.7 4.8 %shard_map.120 = (bf16[4,256,768]{2,1,0:T(8,128)(2,1)}, bf16[4,256,768]{2,1,0:T(8,128)(2,1)}) custom-call(s32[1]{0:T(128)} %bitcast.1.me_ref, bf16[272,768]{1,0:T(8,128)(2,1)} %shard_map.119.refs_0_, bf16[272,768]{1,0:T(8,128)(2,1)} %copy-done.8, bf16[272,768]{1,0:T(8,128)(2,1)} %copy-done.5, bf16[272,768]{1,0:T(8,128)(2,1)} %copy-done.10, ...), custom_call_target="tpu_custom_call" | custom-call | flops 603979776 | bytes 7077888 | tf_op jit(solution)/shard_map/pallas_call | solution.py:94
  37.5 4.8 %collective-permute-done.11.refs_2_ = bf16[256,768]{1,0:T(8,128)(2,1)} collective-permute-done((bf16[256,768]{1,0:T(8,128)(2,1)S(1)}, bf16[256,768]{1,0:T(8,128)(2,1)}, u32[]{:S(2)}, u32[]{:S(2)}) %collective-permute-start.11) | collective-permute-done | bytes 393248 | tf_op jit(solution)/shard_map/ppermute | solution.py:353
  42.8 2.0 %collective-permute-done.13.refs_3_ = bf16[256,768]{1,0:T(8,128)(2,1)S(1)} collective-permute-done((bf16[256,768]{1,0:T(8,128)(2,1)}, bf16[256,768]{1,0:T(8,128)(2,1)S(1)}, u32[]{:S(2)}, u32[]{:S(2)}) %collective-permute-start.13) | collective-permute-done | bytes 393248 | tf_op jit(solution)/shard_map/ppermute | solution.py:353
  46.3 2.8 %shard_map.121 = (bf16[4,256,768]{2,1,0:T(8,128)(2,1)}, bf16[4,256,768]{2,1,0:T(8,128)(2,1)}) custom-call(s32[1]{0:T(128)} %bitcast.1.me_ref, bf16[272,768]{1,0:T(8,128)(2,1)} %copy-done.6, bf16[272,768]{1,0:T(8,128)(2,1)} %copy-done.11, bf16[256,768]{1,0:T(8,128)(2,1)} %collective-permute-done.11.refs_2_, ...), custom_call_target="tpu_custom_call", output_to_operand_aliasing={{0}: (5, {}), {1}: (6, {})} | custom-call | flops 201326592 | bytes 2359296 | tf_op jit(solution)/shard_map/pallas_call | solution.py:94
  49.1 11.8 %shard_map.122 = (bf16[4,256,1152]{2,1,0:T(8,128)(2,1)}, bf16[16,24,1152]{2,1,0:T(8,128)(2,1)}, bf16[16,24,1152]{2,1,0:T(8,128)(2,1)}, bf16[16,24,1152]{2,1,0:T(...) custom-call(s32[1]{0:T(128)} %bitcast.place_ref, ...), custom_call_target="tpu_custom_call" | custom-call | flops 3623878656 | bytes 17301504 | tf_op jit(solution)/shard_map/pallas_call | solution.py:145
  61.5 2.2 %collective-permute-start.15 = (bf16[16,24,1152]{2,1,0:T(8,128)(2,1)}, bf16[16,24,1152]{2,1,0:T(8,128)(2,1)}, u32[]{:S(2)}, u32[]{:S(2)}) collective-permute-start(bf16[16,24,1152]{2,1,0:T(8,128)(2,1)} %get-tuple-element.64), channel_id=1, source_target_pairs={{0,192},{8,200},{16,208},{24,216},{32,224},{40,232},{48,240},{56,2... | collective-permute-start | bytes 2654216 | tf_op jit(solution)/shard_map/ppermute | solution.py:324
  63.7 1.9 %collective-permute-start.21 = (bf16[16,24,1152]{2,1,0:T(8,128)(2,1)}, bf16[16,24,1152]{2,1,0:T(8,128)(2,1)}, u32[]{:S(2)}, u32[]{:S(2)}) collective-permute-start(bf16[16,24,1152]{2,1,0:T(8,128)(2,1)} %get-tuple-element.71), channel_id=1, source_target_pairs={{0,8},{8,0},{16,24},{24,16},{32,40},{40,32},{48,56},{56,48},{64,72... | collective-permute-start | bytes 2654216 | tf_op jit(solution)/shard_map/ppermute | solution.py:324
  65.6 5.0 %collective-permute-start.22 = (bf16[16,24,1152]{2,1,0:T(8,128)(2,1)}, bf16[16,24,1152]{2,1,0:T(8,128)(2,1)}, u32[]{:S(2)}, u32[]{:S(2)}) collective-permute-start(bf16[16,24,1152]{2,1,0:T(8,128)(2,1)} %get-tuple-element.73), channel_id=1, source_target_pairs={{0,56},{8,16},{16,8},{24,32},{32,24},{40,48},{48,40},{56,0},{64,12... | collective-permute-start | bytes 2654216 | tf_op jit(solution)/shard_map/ppermute | solution.py:324
  70.5 7.2 %shard_map.129 = bf16[8,2,4,32,768]{4,3,2,1,0:T(8,128)(2,1)} custom-call(s32[1]{0:T(128)} %bitcast.1.me_ref, bf16[4,256,1152]{2,1,0:T(8,128)(2,1)} %get-tuple-element.80.saved_ref, bf16[4,768,384]{2,1,0:T(8,128)(2,1)} %wg_ref.3, bf16[4,768,384]{2,1,0:T(8,128)(2,1)} %wu_ref.3, bf16[4,768,384]{2,1,0:T(8,128)(2,1)} %wd_ref.3), custom_call_target="tpu_custom_call" | custom-call | flops 1811939328 | bytes 12582912 | tf_op jit(solution)/shard_map/pallas_call | solution.py:180
  77.7 3.6 %all-to-all-start = ((bf16[8,2,4,32,768]{4,3,2,1,0:T(8,128)(2,1)}), bf16[8,2,4,32,768]{4,3,2,1,0:T(8,128)(2,1)S(1)}, u32[]{:S(2)}, u32[]{:S(2)}) async-start(bf16[8,2,4,32,768]{4,3,2,1,0:T(8,128)(2,1)} %shard_map.129), calls=%async_computation | async-start | bytes 6291456 | tf_op jit(solution)/shard_map/all_to_all | solution.py:377
  81.4 1.6 %collective-permute-done.14 = bf16[16,24,1152]{2,1,0:T(8,128)(2,1)} collective-permute-done((bf16[16,24,1152]{2,1,0:T(8,128)(2,1)}, bf16[16,24,1152]{2,1,0:T(8,128)(2,1)}, u32[]{:S(2)}, u32[]{:S(2)}) %collective-permute-start.14) | collective-permute-done | bytes 884768 | tf_op jit(solution)/shard_map/ppermute | solution.py:324
  83.0 1.7 %add_convert_fusion.5 = (bf16[8,24,1152]{2,1,0:T(8,128)(2,1)S(1)}, bf16[8,24,1152]{2,1,0:T(8,128)(2,1)S(1)}) fusion(bf16[16,24,1152]{2,1,0:T(8,128)(2,1)} %collective-permute-done.14, bf16[16,24,1152]{2,1,0:T(8,128)(2,1)} %get-tuple-element.61), kind=kLoop, calls=%fused_computation.5 | loop fusion | flops 1769472 | bytes 2654208 | tf_op jit(solution)/shard_map/convert_element_type | solution.py:317
  87.7 1.9 %collective-permute-start.17 = (bf16[8,24,1152]{2,1,0:T(8,128)(2,1)S(1)}, bf16[8,24,1152]{2,1,0:T(8,128)(2,1)S(1)}, u32[]{:S(2)}, u32[]{:S(2)}) collective-permute-start(bf16[8,24,1152]{2,1,0:T(8,128)(2,1)S(1)} %get-tuple-element.93), channel_id=1, source_target_pairs={{0,64},{8,72},{16,80},{24,88},{32,96},{40,104},{48,112},{56,120},{... | collective-permute-start | bytes 1327112 | tf_op jit(solution)/shard_map/ppermute | solution.py:324
  91.0 5.9 %collective-permute-start.23 = (bf16[8,24,1152]{2,1,0:T(8,128)(2,1)S(1)}, bf16[8,24,1152]{2,1,0:T(8,128)(2,1)S(1)}, u32[]{:S(2)}, u32[]{:S(2)}) collective-permute-start(bf16[8,24,1152]{2,1,0:T(8,128)(2,1)S(1)} %get-tuple-element.91), channel_id=1, source_target_pairs={{0,56},{8,16},{16,8},{24,32},{32,24},{40,48},{48,40},{56,0},{64,12... | collective-permute-start | bytes 1327112 | tf_op jit(solution)/shard_map/ppermute | solution.py:324
  99.2 2.0 %collective-permute-start.18 = (bf16[8,24,1152]{2,1,0:T(8,128)(2,1)S(1)}, bf16[8,24,1152]{2,1,0:T(8,128)(2,1)S(1)}, u32[]{:S(2)}, u32[]{:S(2)}) collective-permute-start(bf16[8,24,1152]{2,1,0:T(8,128)(2,1)S(1)} %get-tuple-element.66), channel_id=1, source_target_pairs={{0,8},{8,0},{16,24},{24,16},{32,40},{40,32},{48,56},{56,48},{64,72... | collective-permute-start | bytes 1327112 | tf_op jit(solution)/shard_map/ppermute | solution.py:324
  101.2 4.8 %collective-permute-done.23.refs_2_ = bf16[8,24,1152]{2,1,0:T(8,128)(2,1)S(1)} collective-permute-done((bf16[8,24,1152]{2,1,0:T(8,128)(2,1)S(1)}, bf16[8,24,1152]{2,1,0:T(8,128)(2,1)S(1)}, u32[]{:S(2)}, u32[]{:S(2)}) %collective-permute-start.23) | collective-permute-done | bytes 442400 | tf_op jit(solution)/shard_map/ppermute | solution.py:324
  106.0 5.5 %collective-permute-done.24.refs_3_ = bf16[8,24,1152]{2,1,0:T(8,128)(2,1)S(1)} collective-permute-done((bf16[8,24,1152]{2,1,0:T(8,128)(2,1)S(1)}, bf16[8,24,1152]{2,1,0:T(8,128)(2,1)S(1)}, u32[]{:S(2)}, u32[]{:S(2)}) %collective-permute-start.24) | collective-permute-done | bytes 442400 | tf_op jit(solution)/shard_map/ppermute | solution.py:324
  112.0 6.4 %collective-permute-done.18.refs_1_ = bf16[8,24,1152]{2,1,0:T(8,128)(2,1)S(1)} collective-permute-done((bf16[8,24,1152]{2,1,0:T(8,128)(2,1)S(1)}, bf16[8,24,1152]{2,1,0:T(8,128)(2,1)S(1)}, u32[]{:S(2)}, u32[]{:S(2)}) %collective-permute-start.18) | collective-permute-done | bytes 442400 | tf_op jit(solution)/shard_map/ppermute | solution.py:324
  120.3 5.4 %collective-permute-done.19.refs_1_ = bf16[4,24,1152]{2,1,0:T(8,128)(2,1)S(1)} collective-permute-done((bf16[4,24,1152]{2,1,0:T(8,128)(2,1)S(1)}, bf16[4,24,1152]{2,1,0:T(8,128)(2,1)S(1)}, u32[]{:S(2)}, u32[]{:S(2)}) %collective-permute-start.19) | collective-permute-done | bytes 221216 | tf_op jit(solution)/shard_map/ppermute | solution.py:324
  125.8 2.2 %collective-permute-start.20 = (bf16[2,24,1152]{2,1,0:T(8,128)(2,1)S(1)}, bf16[2,24,1152]{2,1,0:T(8,128)(2,1)}, u32[]{:S(2)}, u32[]{:S(2)}) collective-permute-start(bf16[2,24,1152]{2,1,0:T(8,128)(2,1)S(1)} %get-tuple-element.69), channel_id=1, source_target_pairs={{0,24},{8,48},{16,40},{24,0},{32,56},{40,16},{48,8},{56,32},{64,88... | collective-permute-start | bytes 331784 | tf_op jit(solution)/shard_map/ppermute | solution.py:324
  128.6 1.9 %collective-permute-start.27 = (bf16[1,24,1152]{2,1,0:T(8,128)(2,1)}, bf16[1,24,1152]{2,1,0:T(8,128)(2,1)}, u32[]{:S(2)}, u32[]{:S(2)}) collective-permute-start(bf16[1,24,1152]{2,1,0:T(8,128)(2,1)} %get-tuple-element.78), channel_id=1, source_target_pairs={{0,24},{8,48},{16,40},{24,0},{32,56},{40,16},{48,8},{56,32},{64,88... | collective-permute-start | bytes 165896 | tf_op jit(solution)/shard_map/ppermute | solution.py:324
  130.6 1.9 %collective-permute-start.28 = (bf16[1,24,1152]{2,1,0:T(8,128)(2,1)S(1)}, bf16[1,24,1152]{2,1,0:T(8,128)(2,1)}, u32[]{:S(2)}, u32[]{:S(2)}) collective-permute-start(bf16[1,24,1152]{2,1,0:T(8,128)(2,1)S(1)} %get-tuple-element.79._), channel_id=1, source_target_pairs={{0,40},{8,32},{16,56},{24,48},{32,8},{40,0},{48,24},{56,16},{64,10... | collective-permute-start | bytes 165896 | tf_op jit(solution)/shard_map/ppermute | solution.py:324
  132.5 3.0 %shard_map.130 = (bf16[256,768]{1,0:T(8,128)(2,1)}, bf16[256,768]{1,0:T(8,128)(2,1)}) custom-call(s32[2,256]{1,0:T(2,128)S(1)} %bitcast.5, s32[2,256]{1,0:T(2,128)S(1)} %bitcast.7, bf16[1,24,1152]{2,1,0:T(8,128)(2,1)S(1)} %get-tuple-element.79._, bf16[8,2,4,32,768]{4,3,2,1,0:T(8,128)(2,1)S(1)} %all-to-all-done.ret), custom_call_target="tpu_custom_call" | custom-call | flops 1207959552 | bytes 7864320 | tf_op jit(solution)/shard_map/pallas_call | solution.py:229
  135.4 2.4 %collective-permute-done.28 = bf16[1,24,1152]{2,1,0:T(8,128)(2,1)} collective-permute-done((bf16[1,24,1152]{2,1,0:T(8,128)(2,1)S(1)}, bf16[1,24,1152]{2,1,0:T(8,128)(2,1)}, u32[]{:S(2)}, u32[]{:S(2)}) %collective-permute-start.28) | collective-permute-done | bytes 55328 | tf_op jit(solution)/shard_map/ppermute | solution.py:324
  (80 shorter events, 18.2 us)
Async XLA Ops:
  0.6 11.8 %collective-permute-start.2 = (bf16[256,768]{1,0:T(8,128)(2,1)}, bf16[256,768]{1,0:T(8,128)(2,1)S(1)}, u32[]{:S(2)}, u32[]{:S(2)}) collective-permute-start(bf16[256,768]{1,0:T(8,128)(2,1)} %refs_6_.1), channel_id=1, source_target_pairs={{0,6},{1,7},{2,0},{3,1},{4,2},{5,3},{6,4},{7,5},{8,14},{9,15},{10,... | collective-permute-start | bytes 1179656 | tf_op jit(solution)/shard_map/ppermute | solution.py:353
  3.7 12.0 %collective-permute-start.1 = (bf16[256,768]{1,0:T(8,128)(2,1)}, bf16[256,768]{1,0:T(8,128)(2,1)S(1)}, u32[]{:S(2)}, u32[]{:S(2)}) collective-permute-start(bf16[256,768]{1,0:T(8,128)(2,1)} %refs_6_.1), channel_id=1, source_target_pairs={{0,2},{1,3},{2,4},{3,5},{4,6},{5,7},{6,0},{7,1},{8,10},{9,11},{10,... | collective-permute-start | bytes 1179656 | tf_op jit(solution)/shard_map/ppermute | solution.py:353
  15.7 10.4 %collective-permute-start.4 = (bf16[272,768]{1,0:T(8,128)(2,1)}, bf16[272,768]{1,0:T(8,128)(2,1)S(1)}, u32[]{:S(2)}, u32[]{:S(2)}) collective-permute-start(bf16[272,768]{1,0:T(8,128)(2,1)} %shard_map.119.refs_0_), channel_id=1, source_target_pairs={{0,6},{1,7},{2,0},{3,1},{4,2},{5,3},{6,4},{7,5},{8,14},{9,15},{10,... | collective-permute-start | bytes 1253384 | tf_op jit(solution)/shard_map/ppermute | solution.py:353
  16.1 11.7 %collective-permute-start.3 = (bf16[272,768]{1,0:T(8,128)(2,1)}, bf16[272,768]{1,0:T(8,128)(2,1)S(1)}, u32[]{:S(2)}, u32[]{:S(2)}) collective-permute-start(bf16[272,768]{1,0:T(8,128)(2,1)} %shard_map.119.refs_0_), channel_id=1, source_target_pairs={{0,2},{1,3},{2,4},{3,5},{4,6},{5,7},{6,0},{7,1},{8,10},{9,11},{10,... | collective-permute-start | bytes 1253384 | tf_op jit(solution)/shard_map/ppermute | solution.py:353
  17.7 10.5 %collective-permute-start.7 = (bf16[256,768]{1,0:T(8,128)(2,1)}, bf16[256,768]{1,0:T(8,128)(2,1)S(1)}, u32[]{:S(2)}, u32[]{:S(2)}) collective-permute-start(bf16[256,768]{1,0:T(8,128)(2,1)} %refs_6_.1), channel_id=1, source_target_pairs={{0,1},{1,0},{2,3},{3,2},{4,5},{5,4},{6,7},{7,6},{8,9},{9,8},{10,11... | collective-permute-start | bytes 1179656 | tf_op jit(solution)/shard_map/ppermute | solution.py:353
  17.8 11.2 %collective-permute-start = (bf16[272,768]{1,0:T(8,128)(2,1)}, bf16[272,768]{1,0:T(8,128)(2,1)S(1)}, u32[]{:S(2)}, u32[]{:S(2)}) collective-permute-start(bf16[272,768]{1,0:T(8,128)(2,1)} %shard_map.119.refs_0_), channel_id=1, source_target_pairs={{0,1},{1,0},{2,3},{3,2},{4,5},{5,4},{6,7},{7,6},{8,9},{9,8},{10,11... | collective-permute-start | bytes 1253384 | tf_op jit(solution)/shard_map/ppermute | solution.py:353
  18.3 11.1 %collective-permute-start.8 = (bf16[256,768]{1,0:T(8,128)(2,1)S(1)}, bf16[256,768]{1,0:T(8,128)(2,1)S(1)}, u32[]{:S(2)}, u32[]{:S(2)}) collective-permute-start(bf16[256,768]{1,0:T(8,128)(2,1)S(1)} %collective-permute-done.2.refs_8_), channel_id=1, source_target_pairs={{0,1},{1,0},{2,3},{3,2},{4,5},{5,4},{6,7},{7,6},{8,9},{9,8},{10,11... | collective-permute-start | bytes 1179656 | tf_op jit(solution)/shard_map/ppermute | solution.py:353
  27.7 4.1 %collective-permute-start.6 = (bf16[272,768]{1,0:T(8,128)(2,1)S(1)}, bf16[272,768]{1,0:T(8,128)(2,1)S(1)}, u32[]{:S(2)}, u32[]{:S(2)}) collective-permute-start(bf16[272,768]{1,0:T(8,128)(2,1)S(1)} %collective-permute-done.3.refs_4_), channel_id=1, source_target_pairs={{0,1},{1,0},{2,3},{3,2},{4,5},{5,4},{6,7},{7,6},{8,9},{9,8},{10,11... | collective-permute-start | bytes 1253384 | tf_op jit(solution)/shard_map/ppermute | solution.py:353
  27.7 4.1 %collective-permute-start.5 = (bf16[272,768]{1,0:T(8,128)(2,1)S(1)}, bf16[272,768]{1,0:T(8,128)(2,1)S(1)}, u32[]{:S(2)}, u32[]{:S(2)}) collective-permute-start(bf16[272,768]{1,0:T(8,128)(2,1)S(1)} %collective-permute-done.4.refs_2_), channel_id=1, source_target_pairs={{0,1},{1,0},{2,3},{3,2},{4,5},{5,4},{6,7},{7,6},{8,9},{9,8},{10,11... | collective-permute-start | bytes 1253384 | tf_op jit(solution)/shard_map/ppermute | solution.py:353
  28.2 3.5 %collective-permute-start.9 = (bf16[256,768]{1,0:T(8,128)(2,1)S(1)}, bf16[256,768]{1,0:T(8,128)(2,1)}, u32[]{:S(2)}, u32[]{:S(2)}) collective-permute-start(bf16[256,768]{1,0:T(8,128)(2,1)S(1)} %collective-permute-done.1.refs_10_), channel_id=1, source_target_pairs={{0,1},{1,0},{2,3},{3,2},{4,5},{5,4},{6,7},{7,6},{8,9},{9,8},{10,11... | collective-permute-start | bytes 1179656 | tf_op jit(solution)/shard_map/ppermute | solution.py:353
  29.0 13.3 %collective-permute-start.10 = (bf16[272,768]{1,0:T(8,128)(2,1)S(1)}, bf16[272,768]{1,0:T(8,128)(2,1)S(1)}, u32[]{:S(2)}, u32[]{:S(2)}) collective-permute-start(bf16[272,768]{1,0:T(8,128)(2,1)S(1)} %collective-permute-done.4.refs_2_), channel_id=1, source_target_pairs={{0,6},{1,7},{2,0},{3,1},{4,2},{5,3},{6,4},{7,5},{8,14},{9,15},{10,... | collective-permute-start | bytes 1253384 | tf_op jit(solution)/shard_map/ppermute | solution.py:353
  30.1 12.2 %collective-permute-start.11 = (bf16[256,768]{1,0:T(8,128)(2,1)S(1)}, bf16[256,768]{1,0:T(8,128)(2,1)}, u32[]{:S(2)}, u32[]{:S(2)}) collective-permute-start(bf16[256,768]{1,0:T(8,128)(2,1)S(1)} %collective-permute-done.1.refs_10_), channel_id=1, source_target_pairs={{0,2},{1,3},{2,4},{3,5},{4,6},{5,7},{6,0},{7,1},{8,10},{9,11},{10,... | collective-permute-start | bytes 1179656 | tf_op jit(solution)/shard_map/ppermute | solution.py:353
  42.3 2.5 %collective-permute-start.12 = (bf16[272,768]{1,0:T(8,128)(2,1)S(1)}, bf16[272,768]{1,0:T(8,128)(2,1)S(1)}, u32[]{:S(2)}, u32[]{:S(2)}) collective-permute-start(bf16[272,768]{1,0:T(8,128)(2,1)S(1)} %collective-permute-done.10.refs_0_), channel_id=1, source_target_pairs={{0,1},{1,0},{2,3},{3,2},{4,5},{5,4},{6,7},{7,6},{8,9},{9,8},{10,11... | collective-permute-start | bytes 1253384 | tf_op jit(solution)/shard_map/ppermute | solution.py:353
  42.3 2.5 %collective-permute-start.13 = (bf16[256,768]{1,0:T(8,128)(2,1)}, bf16[256,768]{1,0:T(8,128)(2,1)S(1)}, u32[]{:S(2)}, u32[]{:S(2)}) collective-permute-start(bf16[256,768]{1,0:T(8,128)(2,1)} %collective-permute-done.11.refs_2_), channel_id=1, source_target_pairs={{0,1},{1,0},{2,3},{3,2},{4,5},{5,4},{6,7},{7,6},{8,9},{9,8},{10,11... | collective-permute-start | bytes 1179656 | tf_op jit(solution)/shard_map/ppermute | solution.py:353
  60.9 22.1 %collective-permute-start.14 = (bf16[16,24,1152]{2,1,0:T(8,128)(2,1)}, bf16[16,24,1152]{2,1,0:T(8,128)(2,1)}, u32[]{:S(2)}, u32[]{:S(2)}) collective-permute-start(bf16[16,24,1152]{2,1,0:T(8,128)(2,1)} %get-tuple-element.62), channel_id=1, source_target_pairs={{0,64},{8,72},{16,80},{24,88},{32,96},{40,104},{48,112},{56,120},{... | collective-permute-start | bytes 2654216 | tf_op jit(solution)/shard_map/ppermute | solution.py:324
  61.5 24.8 %collective-permute-start.15 = (bf16[16,24,1152]{2,1,0:T(8,128)(2,1)}, bf16[16,24,1152]{2,1,0:T(8,128)(2,1)}, u32[]{:S(2)}, u32[]{:S(2)}) collective-permute-start(bf16[16,24,1152]{2,1,0:T(8,128)(2,1)} %get-tuple-element.64), channel_id=1, source_target_pairs={{0,192},{8,200},{16,208},{24,216},{32,224},{40,232},{48,240},{56,2... | collective-permute-start | bytes 2654216 | tf_op jit(solution)/shard_map/ppermute | solution.py:324
  63.7 25.9 %collective-permute-start.21 = (bf16[16,24,1152]{2,1,0:T(8,128)(2,1)}, bf16[16,24,1152]{2,1,0:T(8,128)(2,1)}, u32[]{:S(2)}, u32[]{:S(2)}) collective-permute-start(bf16[16,24,1152]{2,1,0:T(8,128)(2,1)} %get-tuple-element.71), channel_id=1, source_target_pairs={{0,8},{8,0},{16,24},{24,16},{32,40},{40,32},{48,56},{56,48},{64,72... | collective-permute-start | bytes 2654216 | tf_op jit(solution)/shard_map/ppermute | solution.py:324
  65.6 31.3 %collective-permute-start.22 = (bf16[16,24,1152]{2,1,0:T(8,128)(2,1)}, bf16[16,24,1152]{2,1,0:T(8,128)(2,1)}, u32[]{:S(2)}, u32[]{:S(2)}) collective-permute-start(bf16[16,24,1152]{2,1,0:T(8,128)(2,1)} %get-tuple-element.73), channel_id=1, source_target_pairs={{0,56},{8,16},{16,8},{24,32},{32,24},{40,48},{48,40},{56,0},{64,12... | collective-permute-start | bytes 2654216 | tf_op jit(solution)/shard_map/ppermute | solution.py:324
  77.7 54.8 %all-to-all-start = ((bf16[8,2,4,32,768]{4,3,2,1,0:T(8,128)(2,1)}), bf16[8,2,4,32,768]{4,3,2,1,0:T(8,128)(2,1)S(1)}, u32[]{:S(2)}, u32[]{:S(2)}) async-start(bf16[8,2,4,32,768]{4,3,2,1,0:T(8,128)(2,1)} %shard_map.129), calls=%async_computation | async-start | bytes 6291456 | tf_op jit(solution)/shard_map/all_to_all | solution.py:377
  84.7 13.7 %collective-permute-start.16 = (bf16[8,24,1152]{2,1,0:T(8,128)(2,1)S(1)}, bf16[8,24,1152]{2,1,0:T(8,128)(2,1)S(1)}, u32[]{:S(2)}, u32[]{:S(2)}) collective-permute-start(bf16[8,24,1152]{2,1,0:T(8,128)(2,1)S(1)} %get-tuple-element.95), channel_id=1, source_target_pairs={{0,192},{8,200},{16,208},{24,216},{32,224},{40,232},{48,240},{56,2... | collective-permute-start | bytes 1327112 | tf_op jit(solution)/shard_map/ppermute | solution.py:324
  87.7 11.2 %collective-permute-start.17 = (bf16[8,24,1152]{2,1,0:T(8,128)(2,1)S(1)}, bf16[8,24,1152]{2,1,0:T(8,128)(2,1)S(1)}, u32[]{:S(2)}, u32[]{:S(2)}) collective-permute-start(bf16[8,24,1152]{2,1,0:T(8,128)(2,1)S(1)} %get-tuple-element.93), channel_id=1, source_target_pairs={{0,64},{8,72},{16,80},{24,88},{32,96},{40,104},{48,112},{56,120},{... | collective-permute-start | bytes 1327112 | tf_op jit(solution)/shard_map/ppermute | solution.py:324
  91.0 15.0 %collective-permute-start.23 = (bf16[8,24,1152]{2,1,0:T(8,128)(2,1)S(1)}, bf16[8,24,1152]{2,1,0:T(8,128)(2,1)S(1)}, u32[]{:S(2)}, u32[]{:S(2)}) collective-permute-start(bf16[8,24,1152]{2,1,0:T(8,128)(2,1)S(1)} %get-tuple-element.91), channel_id=1, source_target_pairs={{0,56},{8,16},{16,8},{24,32},{32,24},{40,48},{48,40},{56,0},{64,12... | collective-permute-start | bytes 1327112 | tf_op jit(solution)/shard_map/ppermute | solution.py:324
  98.3 13.2 %collective-permute-start.24 = (bf16[8,24,1152]{2,1,0:T(8,128)(2,1)S(1)}, bf16[8,24,1152]{2,1,0:T(8,128)(2,1)S(1)}, u32[]{:S(2)}, u32[]{:S(2)}) collective-permute-start(bf16[8,24,1152]{2,1,0:T(8,128)(2,1)S(1)} %get-tuple-element.89), channel_id=1, source_target_pairs={{0,8},{8,0},{16,24},{24,16},{32,40},{40,32},{48,56},{56,48},{64,72... | collective-permute-start | bytes 1327112 | tf_op jit(solution)/shard_map/ppermute | solution.py:324
  99.2 33.3 %copy-start = (s32[256,2]{0,1:T(2,128)S(1)}, s32[256,2]{0,1:T(2,128)}, u32[]{:S(2)}) copy-start(s32[256,2]{0,1:T(2,128)} %param.9) | copy-start | bytes 6148
  99.2 33.3 %copy-start.1 = (s32[256,2]{0,1:T(2,128)S(1)}, s32[256,2]{0,1:T(2,128)}, u32[]{:S(2)}) copy-start(s32[256,2]{0,1:T(2,128)} %param.10) | copy-start | bytes 6148
  99.2 19.2 %collective-permute-start.18 = (bf16[8,24,1152]{2,1,0:T(8,128)(2,1)S(1)}, bf16[8,24,1152]{2,1,0:T(8,128)(2,1)S(1)}, u32[]{:S(2)}, u32[]{:S(2)}) collective-permute-start(bf16[8,24,1152]{2,1,0:T(8,128)(2,1)S(1)} %get-tuple-element.66), channel_id=1, source_target_pairs={{0,8},{8,0},{16,24},{24,16},{32,40},{40,32},{48,56},{56,48},{64,72... | collective-permute-start | bytes 1327112 | tf_op jit(solution)/shard_map/ppermute | solution.py:324
  111.7 8.4 %collective-permute-start.25 = (bf16[8,24,1152]{2,1,0:T(8,128)(2,1)S(1)}, bf16[8,24,1152]{2,1,0:T(8,128)(2,1)S(1)}, u32[]{:S(2)}, u32[]{:S(2)}) collective-permute-start(bf16[8,24,1152]{2,1,0:T(8,128)(2,1)S(1)} %get-tuple-element.75), channel_id=1, source_target_pairs={{0,64},{8,72},{16,80},{24,88},{32,96},{40,104},{48,112},{56,120},{... | collective-permute-start | bytes 1327112 | tf_op jit(solution)/shard_map/ppermute | solution.py:324
  118.5 7.2 %collective-permute-start.19 = (bf16[4,24,1152]{2,1,0:T(8,128)(2,1)S(1)}, bf16[4,24,1152]{2,1,0:T(8,128)(2,1)S(1)}, u32[]{:S(2)}, u32[]{:S(2)}) collective-permute-start(bf16[4,24,1152]{2,1,0:T(8,128)(2,1)S(1)} %get-tuple-element.68), channel_id=1, source_target_pairs={{0,56},{8,16},{16,8},{24,32},{32,24},{40,48},{48,40},{56,0},{64,12... | collective-permute-start | bytes 663560 | tf_op jit(solution)/shard_map/ppermute | solution.py:324
  120.2 7.8 %collective-permute-start.26 = (bf16[4,24,1152]{2,1,0:T(8,128)(2,1)S(1)}, bf16[4,24,1152]{2,1,0:T(8,128)(2,1)S(1)}, u32[]{:S(2)}, u32[]{:S(2)}) collective-permute-start(bf16[4,24,1152]{2,1,0:T(8,128)(2,1)S(1)} %get-tuple-element.77), channel_id=1, source_target_pairs={{0,192},{8,200},{16,208},{24,216},{32,224},{40,232},{48,240},{56,2... | collective-permute-start | bytes 663560 | tf_op jit(solution)/shard_map/ppermute | solution.py:324
  125.8 12.1 %collective-permute-start.20 = (bf16[2,24,1152]{2,1,0:T(8,128)(2,1)S(1)}, bf16[2,24,1152]{2,1,0:T(8,128)(2,1)}, u32[]{:S(2)}, u32[]{:S(2)}) collective-permute-start(bf16[2,24,1152]{2,1,0:T(8,128)(2,1)S(1)} %get-tuple-element.69), channel_id=1, source_target_pairs={{0,24},{8,48},{16,40},{24,0},{32,56},{40,16},{48,8},{56,32},{64,88... | collective-permute-start | bytes 331784 | tf_op jit(solution)/shard_map/ppermute | solution.py:324
  128.6 6.8 %collective-permute-start.27 = (bf16[1,24,1152]{2,1,0:T(8,128)(2,1)}, bf16[1,24,1152]{2,1,0:T(8,128)(2,1)}, u32[]{:S(2)}, u32[]{:S(2)}) collective-permute-start(bf16[1,24,1152]{2,1,0:T(8,128)(2,1)} %get-tuple-element.78), channel_id=1, source_target_pairs={{0,24},{8,48},{16,40},{24,0},{32,56},{40,16},{48,8},{56,32},{64,88... | collective-permute-start | bytes 165896 | tf_op jit(solution)/shard_map/ppermute | solution.py:324
  130.6 7.3 %collective-permute-start.28 = (bf16[1,24,1152]{2,1,0:T(8,128)(2,1)S(1)}, bf16[1,24,1152]{2,1,0:T(8,128)(2,1)}, u32[]{:S(2)}, u32[]{:S(2)}) collective-permute-start(bf16[1,24,1152]{2,1,0:T(8,128)(2,1)S(1)} %get-tuple-element.79._), channel_id=1, source_target_pairs={{0,40},{8,32},{16,56},{24,48},{32,8},{40,0},{48,24},{56,16},{64,10... | collective-permute-start | bytes 165896 | tf_op jit(solution)/shard_map/ppermute | solution.py:324
  (15 other events, 77.6 us)

commit v3 on v2

--- a/solution.py
+++ b/solution.py
@@ -16,7 +16,7 @@
     return lax.dot_general(a, b, (dims, ((), ())), preferred_element_type=F32)
 
 
-ROOM = pltpu.CompilerParams(vmem_limit_bytes=56 * 2**20)
+ROOM = pltpu.CompilerParams(vmem_limit_bytes=61 * 2**20)
 SCALARS = pl.BlockSpec(memory_space=pltpu.SMEM)
 
 
@@ -241,9 +241,9 @@
 
 PLANS = (
     ("xp", "xq", "zp", "zq", "zf"),
-    ("xq", "xp", "zp", "zq", "zf"),
+    ("xq", "xp", "zq", "zp", "zg"),
     ("zp", "zq", "xp", "xq", "zf"),
-    ("zq", "zp", "xp", "xq", "zg"),
+    ("zq", "zp", "xq", "xp", "zg"),
 )
 FAR = {"zf": (3, 6, 5, 0, 7, 2, 1, 4), "zg": (5, 4, 7, 6, 1, 0, 3, 2)}
 
@@ -323,16 +323,15 @@
 def reduce_grads(send, keep, nx, nz):
     swap = lambda a, kind: lax.ppermute(a, "dp", list(enumerate(partners(kind, nx, nz))))
     got = [swap(send[v], PLANS[v][0]) for v in range(4)]
-    first = [halve_plain([keep[v]], [got[v]]) for v in range(4)]
-    got = [swap(first[v][0][0], PLANS[v][1]) for v in range(4)]
+    held = [halve_plain([keep[v]], [got[v]]) for v in range(4)]
+    for step in (1, 2):
+        got = [swap(held[v][0][0], PLANS[v][step]) for v in range(4)]
+        held = [halve([held[v][1]], [got[v]]) for v in range(4)]
+    got = [swap(held[v][0][0], PLANS[v][3]) for v in range(4)]
     terms, sends = [], []
-    for a, b in ((0, 1), (2, 3)):
-        sent, kept = halve([first[a][1], first[b][1]], [got[a], got[b]])
-        sent, kept = halve([kept], [swap(sent[0], PLANS[a][2])], 2)
-        apart = PLANS[a][4] != PLANS[b][4]
-        sent, kept = halve([kept], [swap(sent[0], PLANS[a][3])], 2, apart)
-        last = [swap(sent[i], PLANS[v][4]) for i, v in enumerate((a, b)[: len(sent)])]
-        terms.append((kept, last))
+    for a, b in ((0, 2), (1, 3)):
+        sent, kept = halve([held[a][1], held[b][1]], [got[a], got[b]])
+        terms.append((kept, [swap(sent[0], PLANS[a][4])]))
         sends += sent
     return [k for k, _ in terms], [g for _, g in terms], sends
 
@@ -357,16 +356,16 @@
     cot = {(0, 0): cotangent}
     cot[3, 0], cot[1, 0] = to(cotangent, 1, 0), to(cotangent, -1, 0)
     tok[0, 1], cot[0, 1] = to(tok[0, 0], 0, 1), to(cotangent, 0, 1)
-    own, cot[3, 0], cot[1, 0] = lax.optimization_barrier((tok[0, 0], cot[3, 0], cot[1, 0]))
-    tok[3, 0], tok[1, 0] = to(own, 1, 0), to(own, -1, 0)
+    later, cot[3, 0], cot[1, 0], tok[0, 1], cot[0, 1] = lax.optimization_barrier(
+        (tok[0, 0], cot[3, 0], cot[1, 0], tok[0, 1], cot[0, 1])
+    )
+    tok[3, 0], tok[1, 0] = to(later, 1, 0), to(later, -1, 0)
     cot[3, 1], cot[1, 1] = to(cot[3, 0], 0, 1), to(cot[1, 0], 0, 1)
-    by_c, tok[3, 0], tok[1, 0] = lax.optimization_barrier((cot[3, 0], tok[3, 0], tok[1, 0]))
-    cot[2, 0], tok[2, 0] = to(by_c, 1, 0), to(tok[1, 0], -1, 0)
+    cot[2, 0], tok[2, 0] = to(cot[3, 0], 1, 0), to(tok[1, 0], -1, 0)
     tok[3, 1], tok[1, 1] = to(tok[3, 0], 0, 1), to(tok[1, 0], 0, 1)
     order = tuple((dy, dc) for dy in (0, 1, 3, 2) for dc in range(2))
     mine, here = me.reshape(1), place.reshape(1)
     near = pack(mine, [tok[r] for r in order[:6]], [cot[r] for r in order[:6]], cap, n_e)
-    near, tok[2, 0], cot[2, 0] = lax.optimization_barrier((near, tok[2, 0], cot[2, 0]))
     tok[2, 1], cot[2, 1] = to(tok[2, 0], 0, 1), to(cot[2, 0], 0, 1)
     rows, grads = pack(mine, [tok[r] for r in order[6:]], [cot[r] for r in order[6:]], cap, n_e, near)
     chunks = jnp.asarray(chunk_orders(nx, nz).reshape(replicas, -1))
@@ -378,7 +377,7 @@
     layer_out, input_grad = combine(ids, gate, last[-1], back)
     got, layer_out = lax.optimization_barrier((got, layer_out))
     total = [k.astype(F32) + jnp.concatenate(g, 0).astype(F32) for k, g in zip(keep, got)]
-    total = jnp.concatenate(total, 0)
+    total = jnp.concatenate([t[i : i + 1] for i in range(2) for t in total], 0)
     return (layer_out, input_grad, total[:, :, :ff], total[:, :, ff : 2 * ff], total[:, :, 2 * ff :])
 
 

time: 140 us -> 138 us (0.986)
  starting transfers between devices: 40.4 us -> 43 us
  waiting for transfers between devices: 54.4 us -> 51.8 us
    ppermute x15 -> x18, waiting for transfers between devices: 27.9 us -> 20.1 us  [reduce_grads(): lax.ppermute(a, 'dp', list(enumerate(partners(kind, nx, nz))))]
    ppermute x14, waiting for transfers between devices: 26.5 us -> 31.7 us  [to(): return lax.ppermute(a, 'expert', perm)]
    ppermute x15 -> x18, starting transfers between devices: 28 us -> 31.3 us  [reduce_grads(): lax.ppermute(a, 'dp', list(enumerate(partners(kind, nx, nz))))]
    unnamed x34 -> x32, local copies, waits for them, and re-layouts: 3.78 us -> 1.67 us
  transfers between devices with their start and end apart: 30 -> 33, of which waited for: 14 -> 14; matrix products, arithmetic and copies ran while one was open for 4% -> 4% of each run, Pallas kernels for 13% -> 12%
where the time goes in v3:
time: 138 us
  waiting for transfers between devices  51.8 us (38%)
  starting transfers between devices  43 us (31%)
  Pallas kernels  32.7 us (24%)
  other arithmetic  6.88 us (5%)
  local copies, waits for them, and re-layouts  2.47 us (2%)
    ppermute x14, waiting for transfers between devices, to(): return lax.ppermute(a, 'expert', perm)  31.7 us
    ppermute x18, starting transfers between devices, reduce_grads(): lax.ppermute(a, 'dp', list(enumerate(partners(kind, nx, nz))))  31.3 us
    ppermute x18, waiting for transfers between devices, reduce_grads(): lax.ppermute(a, 'dp', list(enumerate(partners(kind, nx, nz))))  20.1 us
    pallas_call x1, Pallas kernels, expert_grads(): pl.pallas_call(functools.partial(grads_kernel, scale), grid=(n_e,), in_sp...  11.9 us
    ppermute x14, starting transfers between devices, to(): return lax.ppermute(a, 'expert', perm)  7.98 us
    pallas_call x2, Pallas kernels, pack(): pl.pallas_call(functools.partial(pack_kernel, n, cap, n_e), grid=(1,), in...  7.59 us
    pallas_call x1, Pallas kernels, expert_returns(): pl.pallas_call(functools.partial(returns_kernel, cap, order), grid=(n_e,)...  7.09 us
    convert_element_type x4, other arithmetic, halve_plain(): sends.append((k[a:b].astype(F32) + g[a:b].astype(F32)).astype(BF16))  5.84 us
  transfers between devices with their start and end apart: 33, of which 14 were waited for; matrix products, arithmetic and copies ran while one was open for 4% of the time, Pallas kernels for 12%

profile of v3, /device:TPU:2, one launch (start us, length us, event | category | flops | bytes accessed | tf_op | source)
XLA Modules:
  0.0 137.8 jit_solution(13047270088599376517)
XLA Ops:
  0.6 1.8 %shard_map.119.refs_0_ = bf16[272,768]{1,0:T(8,128)(2,1)} custom-call(s32[2,256]{1,0:T(2,128)} %bitcast.4, s32[2,256]{1,0:T(2,128)} %bitcast.6, bf16[256,768]{1,0:T(8,128)(2,1)} %tok_ref.1), custom_call_target="tpu_custom_call" | custom-call | flops 196608 | bytes 786432 | tf_op jit(solution)/shard_map/pallas_call | solution.py:46
  2.5 3.0 %collective-permute-start.1 = (bf16[256,768]{1,0:T(8,128)(2,1)}, bf16[256,768]{1,0:T(8,128)(2,1)S(1)}, u32[]{:S(2)}, u32[]{:S(2)}) collective-permute-start(bf16[256,768]{1,0:T(8,128)(2,1)} %refs_6_.1), channel_id=1, source_target_pairs={{0,6},{1,7},{2,0},{3,1},{4,2},{5,3},{6,4},{7,5},{8,14},{9,15},{10,... | collective-permute-start | bytes 1179656 | tf_op jit(solution)/shard_map/ppermute | solution.py:352
  5.7 9.1 %collective-permute-done.1.refs_8_ = bf16[256,768]{1,0:T(8,128)(2,1)S(1)} collective-permute-done((bf16[256,768]{1,0:T(8,128)(2,1)}, bf16[256,768]{1,0:T(8,128)(2,1)S(1)}, u32[]{:S(2)}, u32[]{:S(2)}) %collective-permute-start.1) | collective-permute-done | bytes 393248 | tf_op jit(solution)/shard_map/ppermute | solution.py:352
  14.8 3.3 %collective-permute-done.refs_10_ = bf16[256,768]{1,0:T(8,128)(2,1)S(1)} collective-permute-done((bf16[256,768]{1,0:T(8,128)(2,1)}, bf16[256,768]{1,0:T(8,128)(2,1)S(1)}, u32[]{:S(2)}, u32[]{:S(2)}) %collective-permute-start) | collective-permute-done | bytes 393248 | tf_op jit(solution)/shard_map/ppermute | solution.py:352
  18.6 1.7 %collective-permute-start.10 = (bf16[272,768]{1,0:T(8,128)(2,1)}, bf16[272,768]{1,0:T(8,128)(2,1)S(1)}, u32[]{:S(2)}, u32[]{:S(2)}) collective-permute-start(bf16[272,768]{1,0:T(8,128)(2,1)} %shard_map.119.refs_0_), channel_id=1, source_target_pairs={{0,2},{1,3},{2,4},{3,5},{4,6},{5,7},{6,0},{7,1},{8,10},{9,11},{10,... | collective-permute-start | bytes 1253384 | tf_op jit(solution)/shard_map/ppermute | solution.py:352
  20.3 9.1 %collective-permute-done.4.refs_2_ = bf16[272,768]{1,0:T(8,128)(2,1)S(1)} collective-permute-done((bf16[272,768]{1,0:T(8,128)(2,1)}, bf16[272,768]{1,0:T(8,128)(2,1)S(1)}, u32[]{:S(2)}, u32[]{:S(2)}) %collective-permute-start.4) | collective-permute-done | bytes 417824 | tf_op jit(solution)/shard_map/ppermute | solution.py:352
  29.4 1.8 %collective-permute-start.5 = (bf16[272,768]{1,0:T(8,128)(2,1)S(1)}, bf16[272,768]{1,0:T(8,128)(2,1)S(1)}, u32[]{:S(2)}, u32[]{:S(2)}) collective-permute-start(bf16[272,768]{1,0:T(8,128)(2,1)S(1)} %collective-permute-done.4.refs_2_), channel_id=1, source_target_pairs={{0,6},{1,7},{2,0},{3,1},{4,2},{5,3},{6,4},{7,5},{8,14},{9,15},{10,... | collective-permute-start | bytes 1253384 | tf_op jit(solution)/shard_map/ppermute | solution.py:352
  32.1 7.4 %collective-permute-done.5.refs_0_ = bf16[272,768]{1,0:T(8,128)(2,1)S(1)} collective-permute-done((bf16[272,768]{1,0:T(8,128)(2,1)S(1)}, bf16[272,768]{1,0:T(8,128)(2,1)S(1)}, u32[]{:S(2)}, u32[]{:S(2)}) %collective-permute-start.5) | collective-permute-done | bytes 417824 | tf_op jit(solution)/shard_map/ppermute | solution.py:352
  39.5 2.7 %collective-permute-done.7.refs_2_ = bf16[256,768]{1,0:T(8,128)(2,1)} collective-permute-done((bf16[256,768]{1,0:T(8,128)(2,1)S(1)}, bf16[256,768]{1,0:T(8,128)(2,1)}, u32[]{:S(2)}, u32[]{:S(2)}) %collective-permute-start.7) | collective-permute-done | bytes 393248 | tf_op jit(solution)/shard_map/ppermute | solution.py:352
  43.1 4.8 %shard_map.120 = (bf16[4,256,768]{2,1,0:T(8,128)(2,1)}, bf16[4,256,768]{2,1,0:T(8,128)(2,1)}) custom-call(s32[1]{0:T(128)} %bitcast.1.me_ref, bf16[272,768]{1,0:T(8,128)(2,1)} %shard_map.119.refs_0_, bf16[272,768]{1,0:T(8,128)(2,1)} %copy-done.5, bf16[272,768]{1,0:T(8,128)(2,1)} %copy-done.7, bf16[272,768]{1,0:T(8,128)(2,1)} %copy-done.10, ...), custom_call_target="tpu_custom_call" | custom-call | flops 603979776 | bytes 7077888 | tf_op jit(solution)/shard_map/pallas_call | solution.py:94
  48.7 2.8 %shard_map.121 = (bf16[4,256,768]{2,1,0:T(8,128)(2,1)}, bf16[4,256,768]{2,1,0:T(8,128)(2,1)}) custom-call(s32[1]{0:T(128)} %bitcast.1.me_ref, bf16[272,768]{1,0:T(8,128)(2,1)} %copy-done.6, bf16[272,768]{1,0:T(8,128)(2,1)} %copy-done.11, bf16[256,768]{1,0:T(8,128)(2,1)} %collective-permute-done.7.refs_2_, ...), custom_call_target="tpu_custom_call", output_to_operand_aliasing={{0}: (5, {}), {1}: (6, {})} | custom-call | flops 201326592 | bytes 2359296 | tf_op jit(solution)/shard_map/pallas_call | solution.py:94
  51.5 11.9 %shard_map.122 = (bf16[4,256,1152]{2,1,0:T(8,128)(2,1)}, bf16[16,24,1152]{2,1,0:T(8,128)(2,1)}, bf16[16,24,1152]{2,1,0:T(8,128)(2,1)}, bf16[16,24,1152]{2,1,0:T(...) custom-call(s32[1]{0:T(128)} %bitcast.place_ref, ...), custom_call_target="tpu_custom_call" | custom-call | flops 3623878656 | bytes 17301504 | tf_op jit(solution)/shard_map/pallas_call | solution.py:145
  64.0 1.9 %collective-permute-start.17 = (bf16[16,24,1152]{2,1,0:T(8,128)(2,1)}, bf16[16,24,1152]{2,1,0:T(8,128)(2,1)}, u32[]{:S(2)}, u32[]{:S(2)}) collective-permute-start(bf16[16,24,1152]{2,1,0:T(8,128)(2,1)} %get-tuple-element.63), channel_id=1, source_target_pairs={{0,8},{8,0},{16,24},{24,16},{32,40},{40,32},{48,56},{56,48},{64,72... | collective-permute-start | bytes 2654216 | tf_op jit(solution)/shard_map/ppermute | solution.py:324
  65.9 2.1 %collective-permute-start.23 = (bf16[16,24,1152]{2,1,0:T(8,128)(2,1)}, bf16[16,24,1152]{2,1,0:T(8,128)(2,1)}, u32[]{:S(2)}, u32[]{:S(2)}) collective-permute-start(bf16[16,24,1152]{2,1,0:T(8,128)(2,1)} %get-tuple-element.71), channel_id=1, source_target_pairs={{0,192},{8,200},{16,208},{24,216},{32,224},{40,232},{48,240},{56,2... | collective-permute-start | bytes 2654216 | tf_op jit(solution)/shard_map/ppermute | solution.py:324
  68.0 5.0 %collective-permute-start.26 = (bf16[16,24,1152]{2,1,0:T(8,128)(2,1)}, bf16[16,24,1152]{2,1,0:T(8,128)(2,1)}, u32[]{:S(2)}, u32[]{:S(2)}) collective-permute-start(bf16[16,24,1152]{2,1,0:T(8,128)(2,1)} %get-tuple-element.76), channel_id=1, source_target_pairs={{0,56},{8,16},{16,8},{24,32},{32,24},{40,48},{48,40},{56,0},{64,12... | collective-permute-start | bytes 2654216 | tf_op jit(solution)/shard_map/ppermute | solution.py:324
  73.0 7.1 %shard_map.133 = bf16[8,2,4,32,768]{4,3,2,1,0:T(8,128)(2,1)} custom-call(s32[1]{0:T(128)} %bitcast.1.me_ref, bf16[4,256,1152]{2,1,0:T(8,128)(2,1)} %get-tuple-element.83.saved_ref, bf16[4,768,384]{2,1,0:T(8,128)(2,1)} %wg_ref.3, bf16[4,768,384]{2,1,0:T(8,128)(2,1)} %wu_ref.3, bf16[4,768,384]{2,1,0:T(8,128)(2,1)} %wd_ref.3), custom_call_target="tpu_custom_call" | custom-call | flops 1811939328 | bytes 12582912 | tf_op jit(solution)/shard_map/pallas_call | solution.py:180
  80.1 3.6 %all-to-all-start = ((bf16[8,2,4,32,768]{4,3,2,1,0:T(8,128)(2,1)}), bf16[8,2,4,32,768]{4,3,2,1,0:T(8,128)(2,1)S(1)}, u32[]{:S(2)}, u32[]{:S(2)}) async-start(bf16[8,2,4,32,768]{4,3,2,1,0:T(8,128)(2,1)} %shard_map.133), calls=%async_computation | async-start | bytes 6291456 | tf_op jit(solution)/shard_map/all_to_all | solution.py:376
  83.7 2.0 %collective-permute-done.14 = bf16[16,24,1152]{2,1,0:T(8,128)(2,1)} collective-permute-done((bf16[16,24,1152]{2,1,0:T(8,128)(2,1)}, bf16[16,24,1152]{2,1,0:T(8,128)(2,1)}, u32[]{:S(2)}, u32[]{:S(2)}) %collective-permute-start.14) | collective-permute-done | bytes 884768 | tf_op jit(solution)/shard_map/ppermute | solution.py:324
  85.8 1.7 %add_convert_fusion.6 = (bf16[8,24,1152]{2,1,0:T(8,128)(2,1)S(1)}, bf16[8,24,1152]{2,1,0:T(8,128)(2,1)S(1)}) fusion(bf16[16,24,1152]{2,1,0:T(8,128)(2,1)} %collective-permute-done.14, bf16[16,24,1152]{2,1,0:T(8,128)(2,1)} %get-tuple-element.57), kind=kLoop, calls=%fused_computation.6 | loop fusion | flops 1769472 | bytes 2654208 | tf_op jit(solution)/shard_map/convert_element_type | solution.py:317
  90.5 5.9 %collective-permute-start.18 = (bf16[8,24,1152]{2,1,0:T(8,128)(2,1)S(1)}, bf16[8,24,1152]{2,1,0:T(8,128)(2,1)S(1)}, u32[]{:S(2)}, u32[]{:S(2)}) collective-permute-start(bf16[8,24,1152]{2,1,0:T(8,128)(2,1)S(1)} %get-tuple-element.95), channel_id=1, source_target_pairs={{0,56},{8,16},{16,8},{24,32},{32,24},{40,48},{48,40},{56,0},{64,12... | collective-permute-start | bytes 1327112 | tf_op jit(solution)/shard_map/ppermute | solution.py:324
  97.8 1.9 %collective-permute-start.24 = (bf16[8,24,1152]{2,1,0:T(8,128)(2,1)S(1)}, bf16[8,24,1152]{2,1,0:T(8,128)(2,1)S(1)}, u32[]{:S(2)}, u32[]{:S(2)}) collective-permute-start(bf16[8,24,1152]{2,1,0:T(8,128)(2,1)S(1)} %get-tuple-element.93), channel_id=1, source_target_pairs={{0,64},{8,72},{16,80},{24,88},{32,96},{40,104},{48,112},{56,120},{... | collective-permute-start | bytes 1327112 | tf_op jit(solution)/shard_map/ppermute | solution.py:324
  101.3 2.1 %collective-permute-start.16 = (bf16[4,24,1152]{2,1,0:T(8,128)(2,1)S(1)}, bf16[4,24,1152]{2,1,0:T(8,128)(2,1)S(1)}, u32[]{:S(2)}, u32[]{:S(2)}) collective-permute-start(bf16[4,24,1152]{2,1,0:T(8,128)(2,1)S(1)} %get-tuple-element.60), channel_id=1, source_target_pairs={{0,8},{8,0},{16,24},{24,16},{32,40},{40,32},{48,56},{56,48},{64,72... | collective-permute-start | bytes 663560 | tf_op jit(solution)/shard_map/ppermute | solution.py:324
  103.4 2.8 %collective-permute-done.18.refs_1_ = bf16[8,24,1152]{2,1,0:T(8,128)(2,1)S(1)} collective-permute-done((bf16[8,24,1152]{2,1,0:T(8,128)(2,1)S(1)}, bf16[8,24,1152]{2,1,0:T(8,128)(2,1)S(1)}, u32[]{:S(2)}, u32[]{:S(2)}) %collective-permute-start.18) | collective-permute-done | bytes 442400 | tf_op jit(solution)/shard_map/ppermute | solution.py:324
  106.3 1.9 %collective-permute-start.19 = (bf16[4,24,1152]{2,1,0:T(8,128)(2,1)S(1)}, bf16[4,24,1152]{2,1,0:T(8,128)(2,1)S(1)}, u32[]{:S(2)}, u32[]{:S(2)}) collective-permute-start(bf16[4,24,1152]{2,1,0:T(8,128)(2,1)S(1)} %get-tuple-element.65), channel_id=1, source_target_pairs={{0,64},{8,72},{16,80},{24,88},{32,96},{40,104},{48,112},{56,120},{... | collective-permute-start | bytes 663560 | tf_op jit(solution)/shard_map/ppermute | solution.py:324
  108.2 2.2 %collective-permute-done.24.refs_1_ = bf16[8,24,1152]{2,1,0:T(8,128)(2,1)S(1)} collective-permute-done((bf16[8,24,1152]{2,1,0:T(8,128)(2,1)S(1)}, bf16[8,24,1152]{2,1,0:T(8,128)(2,1)S(1)}, u32[]{:S(2)}, u32[]{:S(2)}) %collective-permute-start.24) | collective-permute-done | bytes 442400 | tf_op jit(solution)/shard_map/ppermute | solution.py:324
  111.4 2.9 %collective-permute-done.27.refs_1_ = bf16[8,24,1152]{2,1,0:T(8,128)(2,1)S(1)} collective-permute-done((bf16[8,24,1152]{2,1,0:T(8,128)(2,1)S(1)}, bf16[8,24,1152]{2,1,0:T(8,128)(2,1)S(1)}, u32[]{:S(2)}, u32[]{:S(2)}) %collective-permute-start.27) | collective-permute-done | bytes 442400 | tf_op jit(solution)/shard_map/ppermute | solution.py:324
  114.7 2.2 %collective-permute-done.16.refs_1_ = bf16[4,24,1152]{2,1,0:T(8,128)(2,1)S(1)} collective-permute-done((bf16[4,24,1152]{2,1,0:T(8,128)(2,1)S(1)}, bf16[4,24,1152]{2,1,0:T(8,128)(2,1)S(1)}, u32[]{:S(2)}, u32[]{:S(2)}) %collective-permute-start.16) | collective-permute-done | bytes 221216 | tf_op jit(solution)/shard_map/ppermute | solution.py:324
  118.6 3.0 %collective-permute-done.28.refs_1_ = bf16[4,24,1152]{2,1,0:T(8,128)(2,1)S(1)} collective-permute-done((bf16[4,24,1152]{2,1,0:T(8,128)(2,1)S(1)}, bf16[4,24,1152]{2,1,0:T(8,128)(2,1)S(1)}, u32[]{:S(2)}, u32[]{:S(2)}) %collective-permute-start.28) | collective-permute-done | bytes 221216 | tf_op jit(solution)/shard_map/ppermute | solution.py:324
  123.4 1.9 %collective-permute-start.22 = (bf16[2,24,1152]{2,1,0:T(8,128)(2,1)S(1)}, bf16[2,24,1152]{2,1,0:T(8,128)(2,1)}, u32[]{:S(2)}, u32[]{:S(2)}) collective-permute-start(bf16[2,24,1152]{2,1,0:T(8,128)(2,1)S(1)} %get-tuple-element.69), channel_id=1, source_target_pairs={{0,24},{8,48},{16,40},{24,0},{32,56},{40,16},{48,8},{56,32},{64,88... | collective-permute-start | bytes 331784 | tf_op jit(solution)/shard_map/ppermute | solution.py:324
  127.1 2.1 %collective-permute-start.31 = (bf16[2,24,1152]{2,1,0:T(8,128)(2,1)}, bf16[2,24,1152]{2,1,0:T(8,128)(2,1)}, u32[]{:S(2)}, u32[]{:S(2)}) collective-permute-start(bf16[2,24,1152]{2,1,0:T(8,128)(2,1)} %get-tuple-element.82._), channel_id=1, source_target_pairs={{0,40},{8,32},{16,56},{24,48},{32,8},{40,0},{48,24},{56,16},{64,10... | collective-permute-start | bytes 331784 | tf_op jit(solution)/shard_map/ppermute | solution.py:324
  129.3 3.0 %shard_map.134 = (bf16[256,768]{1,0:T(8,128)(2,1)}, bf16[256,768]{1,0:T(8,128)(2,1)}) custom-call(s32[2,256]{1,0:T(2,128)S(1)} %bitcast.5, s32[2,256]{1,0:T(2,128)S(1)} %bitcast.7, bf16[2,24,1152]{2,1,0:T(8,128)(2,1)} %get-tuple-element.82._, bf16[8,2,4,32,768]{4,3,2,1,0:T(8,128)(2,1)S(1)} %all-to-all-done.ret), custom_call_target="tpu_custom_call" | custom-call | flops 1207959552 | bytes 7864320 | tf_op jit(solution)/shard_map/pallas_call | solution.py:229
  132.3 3.6 %collective-permute-done.31 = bf16[2,24,1152]{2,1,0:T(8,128)(2,1)} collective-permute-done((bf16[2,24,1152]{2,1,0:T(8,128)(2,1)}, bf16[2,24,1152]{2,1,0:T(8,128)(2,1)}, u32[]{:S(2)}, u32[]{:S(2)}) %collective-permute-start.31) | collective-permute-done | bytes 110624 | tf_op jit(solution)/shard_map/ppermute | solution.py:324
  (91 shorter events, 18.4 us)
Async XLA Ops:
  2.5 15.7 %collective-permute-start.2 = (bf16[272,768]{1,0:T(8,128)(2,1)}, bf16[272,768]{1,0:T(8,128)(2,1)S(1)}, u32[]{:S(2)}, u32[]{:S(2)}) collective-permute-start(bf16[272,768]{1,0:T(8,128)(2,1)} %shard_map.119.refs_0_), channel_id=1, source_target_pairs={{0,1},{1,0},{2,3},{3,2},{4,5},{5,4},{6,7},{7,6},{8,9},{9,8},{10,11... | collective-permute-start | bytes 1253384 | tf_op jit(solution)/shard_map/ppermute | solution.py:352
  2.5 12.4 %collective-permute-start.1 = (bf16[256,768]{1,0:T(8,128)(2,1)}, bf16[256,768]{1,0:T(8,128)(2,1)S(1)}, u32[]{:S(2)}, u32[]{:S(2)}) collective-permute-start(bf16[256,768]{1,0:T(8,128)(2,1)} %refs_6_.1), channel_id=1, source_target_pairs={{0,6},{1,7},{2,0},{3,1},{4,2},{5,3},{6,4},{7,5},{8,14},{9,15},{10,... | collective-permute-start | bytes 1179656 | tf_op jit(solution)/shard_map/ppermute | solution.py:352
  5.5 12.7 %collective-permute-start = (bf16[256,768]{1,0:T(8,128)(2,1)}, bf16[256,768]{1,0:T(8,128)(2,1)S(1)}, u32[]{:S(2)}, u32[]{:S(2)}) collective-permute-start(bf16[256,768]{1,0:T(8,128)(2,1)} %refs_6_.1), channel_id=1, source_target_pairs={{0,2},{1,3},{2,4},{3,5},{4,6},{5,7},{6,0},{7,1},{8,10},{9,11},{10,... | collective-permute-start | bytes 1179656 | tf_op jit(solution)/shard_map/ppermute | solution.py:352
  5.5 12.7 %collective-permute-start.3 = (bf16[256,768]{1,0:T(8,128)(2,1)}, bf16[256,768]{1,0:T(8,128)(2,1)S(1)}, u32[]{:S(2)}, u32[]{:S(2)}) collective-permute-start(bf16[256,768]{1,0:T(8,128)(2,1)} %refs_6_.1), channel_id=1, source_target_pairs={{0,1},{1,0},{2,3},{3,2},{4,5},{5,4},{6,7},{7,6},{8,9},{9,8},{10,11... | collective-permute-start | bytes 1179656 | tf_op jit(solution)/shard_map/ppermute | solution.py:352
  18.2 11.2 %collective-permute-start.4 = (bf16[272,768]{1,0:T(8,128)(2,1)}, bf16[272,768]{1,0:T(8,128)(2,1)S(1)}, u32[]{:S(2)}, u32[]{:S(2)}) collective-permute-start(bf16[272,768]{1,0:T(8,128)(2,1)} %shard_map.119.refs_0_), channel_id=1, source_target_pairs={{0,6},{1,7},{2,0},{3,1},{4,2},{5,3},{6,4},{7,5},{8,14},{9,15},{10,... | collective-permute-start | bytes 1253384 | tf_op jit(solution)/shard_map/ppermute | solution.py:352
  18.6 12.9 %collective-permute-start.10 = (bf16[272,768]{1,0:T(8,128)(2,1)}, bf16[272,768]{1,0:T(8,128)(2,1)S(1)}, u32[]{:S(2)}, u32[]{:S(2)}) collective-permute-start(bf16[272,768]{1,0:T(8,128)(2,1)} %shard_map.119.refs_0_), channel_id=1, source_target_pairs={{0,2},{1,3},{2,4},{3,5},{4,6},{5,7},{6,0},{7,1},{8,10},{9,11},{10,... | collective-permute-start | bytes 1253384 | tf_op jit(solution)/shard_map/ppermute | solution.py:352
  20.3 11.7 %collective-permute-start.12 = (bf16[256,768]{1,0:T(8,128)(2,1)S(1)}, bf16[256,768]{1,0:T(8,128)(2,1)S(1)}, u32[]{:S(2)}, u32[]{:S(2)}) collective-permute-start(bf16[256,768]{1,0:T(8,128)(2,1)S(1)} %collective-permute-done.1.refs_8_), channel_id=1, source_target_pairs={{0,1},{1,0},{2,3},{3,2},{4,5},{5,4},{6,7},{7,6},{8,9},{9,8},{10,11... | collective-permute-start | bytes 1179656 | tf_op jit(solution)/shard_map/ppermute | solution.py:352
  29.4 10.0 %collective-permute-start.5 = (bf16[272,768]{1,0:T(8,128)(2,1)S(1)}, bf16[272,768]{1,0:T(8,128)(2,1)S(1)}, u32[]{:S(2)}, u32[]{:S(2)}) collective-permute-start(bf16[272,768]{1,0:T(8,128)(2,1)S(1)} %collective-permute-done.4.refs_2_), channel_id=1, source_target_pairs={{0,6},{1,7},{2,0},{3,1},{4,2},{5,3},{6,4},{7,5},{8,14},{9,15},{10,... | collective-permute-start | bytes 1253384 | tf_op jit(solution)/shard_map/ppermute | solution.py:352
  31.2 10.9 %collective-permute-start.7 = (bf16[256,768]{1,0:T(8,128)(2,1)S(1)}, bf16[256,768]{1,0:T(8,128)(2,1)}, u32[]{:S(2)}, u32[]{:S(2)}) collective-permute-start(bf16[256,768]{1,0:T(8,128)(2,1)S(1)} %collective-permute-done.refs_10_), channel_id=1, source_target_pairs={{0,2},{1,3},{2,4},{3,5},{4,6},{5,7},{6,0},{7,1},{8,10},{9,11},{10,... | collective-permute-start | bytes 1179656 | tf_op jit(solution)/shard_map/ppermute | solution.py:352
  31.4 10.7 %collective-permute-start.11 = (bf16[272,768]{1,0:T(8,128)(2,1)S(1)}, bf16[272,768]{1,0:T(8,128)(2,1)S(1)}, u32[]{:S(2)}, u32[]{:S(2)}) collective-permute-start(bf16[272,768]{1,0:T(8,128)(2,1)S(1)} %collective-permute-done.10.refs_4_), channel_id=1, source_target_pairs={{0,1},{1,0},{2,3},{3,2},{4,5},{5,4},{6,7},{7,6},{8,9},{9,8},{10,11... | collective-permute-start | bytes 1253384 | tf_op jit(solution)/shard_map/ppermute | solution.py:352
  31.5 10.7 %collective-permute-start.9 = (bf16[272,768]{1,0:T(8,128)(2,1)S(1)}, bf16[272,768]{1,0:T(8,128)(2,1)S(1)}, u32[]{:S(2)}, u32[]{:S(2)}) collective-permute-start(bf16[272,768]{1,0:T(8,128)(2,1)S(1)} %collective-permute-done.4.refs_2_), channel_id=1, source_target_pairs={{0,1},{1,0},{2,3},{3,2},{4,5},{5,4},{6,7},{7,6},{8,9},{9,8},{10,11... | collective-permute-start | bytes 1253384 | tf_op jit(solution)/shard_map/ppermute | solution.py:352
  32.0 10.2 %collective-permute-start.13 = (bf16[256,768]{1,0:T(8,128)(2,1)S(1)}, bf16[256,768]{1,0:T(8,128)(2,1)}, u32[]{:S(2)}, u32[]{:S(2)}) collective-permute-start(bf16[256,768]{1,0:T(8,128)(2,1)S(1)} %collective-permute-done.refs_10_), channel_id=1, source_target_pairs={{0,1},{1,0},{2,3},{3,2},{4,5},{5,4},{6,7},{7,6},{8,9},{9,8},{10,11... | collective-permute-start | bytes 1179656 | tf_op jit(solution)/shard_map/ppermute | solution.py:352
  39.5 8.4 %collective-permute-start.6 = (bf16[272,768]{1,0:T(8,128)(2,1)S(1)}, bf16[272,768]{1,0:T(8,128)(2,1)S(1)}, u32[]{:S(2)}, u32[]{:S(2)}) collective-permute-start(bf16[272,768]{1,0:T(8,128)(2,1)S(1)} %collective-permute-done.5.refs_0_), channel_id=1, source_target_pairs={{0,1},{1,0},{2,3},{3,2},{4,5},{5,4},{6,7},{7,6},{8,9},{9,8},{10,11... | collective-permute-start | bytes 1253384 | tf_op jit(solution)/shard_map/ppermute | solution.py:352
  42.1 5.8 %collective-permute-start.8 = (bf16[256,768]{1,0:T(8,128)(2,1)}, bf16[256,768]{1,0:T(8,128)(2,1)}, u32[]{:S(2)}, u32[]{:S(2)}) collective-permute-start(bf16[256,768]{1,0:T(8,128)(2,1)} %collective-permute-done.7.refs_2_), channel_id=1, source_target_pairs={{0,1},{1,0},{2,3},{3,2},{4,5},{5,4},{6,7},{7,6},{8,9},{9,8},{10,11... | collective-permute-start | bytes 1179656 | tf_op jit(solution)/shard_map/ppermute | solution.py:352
  63.3 22.4 %collective-permute-start.14 = (bf16[16,24,1152]{2,1,0:T(8,128)(2,1)}, bf16[16,24,1152]{2,1,0:T(8,128)(2,1)}, u32[]{:S(2)}, u32[]{:S(2)}) collective-permute-start(bf16[16,24,1152]{2,1,0:T(8,128)(2,1)} %get-tuple-element.58), channel_id=1, source_target_pairs={{0,64},{8,72},{16,80},{24,88},{32,96},{40,104},{48,112},{56,120},{... | collective-permute-start | bytes 2654216 | tf_op jit(solution)/shard_map/ppermute | solution.py:324
  64.0 25.1 %collective-permute-start.17 = (bf16[16,24,1152]{2,1,0:T(8,128)(2,1)}, bf16[16,24,1152]{2,1,0:T(8,128)(2,1)}, u32[]{:S(2)}, u32[]{:S(2)}) collective-permute-start(bf16[16,24,1152]{2,1,0:T(8,128)(2,1)} %get-tuple-element.63), channel_id=1, source_target_pairs={{0,8},{8,0},{16,24},{24,16},{32,40},{40,32},{48,56},{56,48},{64,72... | collective-permute-start | bytes 2654216 | tf_op jit(solution)/shard_map/ppermute | solution.py:324
  65.9 30.6 %collective-permute-start.23 = (bf16[16,24,1152]{2,1,0:T(8,128)(2,1)}, bf16[16,24,1152]{2,1,0:T(8,128)(2,1)}, u32[]{:S(2)}, u32[]{:S(2)}) collective-permute-start(bf16[16,24,1152]{2,1,0:T(8,128)(2,1)} %get-tuple-element.71), channel_id=1, source_target_pairs={{0,192},{8,200},{16,208},{24,216},{32,224},{40,232},{48,240},{56,2... | collective-permute-start | bytes 2654216 | tf_op jit(solution)/shard_map/ppermute | solution.py:324
  68.0 31.7 %collective-permute-start.26 = (bf16[16,24,1152]{2,1,0:T(8,128)(2,1)}, bf16[16,24,1152]{2,1,0:T(8,128)(2,1)}, u32[]{:S(2)}, u32[]{:S(2)}) collective-permute-start(bf16[16,24,1152]{2,1,0:T(8,128)(2,1)} %get-tuple-element.76), channel_id=1, source_target_pairs={{0,56},{8,16},{16,8},{24,32},{32,24},{40,48},{48,40},{56,0},{64,12... | collective-permute-start | bytes 2654216 | tf_op jit(solution)/shard_map/ppermute | solution.py:324
  80.1 49.2 %all-to-all-start = ((bf16[8,2,4,32,768]{4,3,2,1,0:T(8,128)(2,1)}), bf16[8,2,4,32,768]{4,3,2,1,0:T(8,128)(2,1)S(1)}, u32[]{:S(2)}, u32[]{:S(2)}) async-start(bf16[8,2,4,32,768]{4,3,2,1,0:T(8,128)(2,1)} %shard_map.133), calls=%async_computation | async-start | bytes 6291456 | tf_op jit(solution)/shard_map/all_to_all | solution.py:376
  87.5 13.7 %collective-permute-start.15 = (bf16[8,24,1152]{2,1,0:T(8,128)(2,1)S(1)}, bf16[8,24,1152]{2,1,0:T(8,128)(2,1)S(1)}, u32[]{:S(2)}, u32[]{:S(2)}) collective-permute-start(bf16[8,24,1152]{2,1,0:T(8,128)(2,1)S(1)} %get-tuple-element.97), channel_id=1, source_target_pairs={{0,192},{8,200},{16,208},{24,216},{32,224},{40,232},{48,240},{56,2... | collective-permute-start | bytes 1327112 | tf_op jit(solution)/shard_map/ppermute | solution.py:324
  90.5 15.7 %collective-permute-start.18 = (bf16[8,24,1152]{2,1,0:T(8,128)(2,1)S(1)}, bf16[8,24,1152]{2,1,0:T(8,128)(2,1)S(1)}, u32[]{:S(2)}, u32[]{:S(2)}) collective-permute-start(bf16[8,24,1152]{2,1,0:T(8,128)(2,1)S(1)} %get-tuple-element.95), channel_id=1, source_target_pairs={{0,56},{8,16},{16,8},{24,32},{32,24},{40,48},{48,40},{56,0},{64,12... | collective-permute-start | bytes 1327112 | tf_op jit(solution)/shard_map/ppermute | solution.py:324
  97.8 12.6 %collective-permute-start.24 = (bf16[8,24,1152]{2,1,0:T(8,128)(2,1)S(1)}, bf16[8,24,1152]{2,1,0:T(8,128)(2,1)S(1)}, u32[]{:S(2)}, u32[]{:S(2)}) collective-permute-start(bf16[8,24,1152]{2,1,0:T(8,128)(2,1)S(1)} %get-tuple-element.93), channel_id=1, source_target_pairs={{0,64},{8,72},{16,80},{24,88},{32,96},{40,104},{48,112},{56,120},{... | collective-permute-start | bytes 1327112 | tf_op jit(solution)/shard_map/ppermute | solution.py:324
  101.1 13.2 %collective-permute-start.27 = (bf16[8,24,1152]{2,1,0:T(8,128)(2,1)S(1)}, bf16[8,24,1152]{2,1,0:T(8,128)(2,1)S(1)}, u32[]{:S(2)}, u32[]{:S(2)}) collective-permute-start(bf16[8,24,1152]{2,1,0:T(8,128)(2,1)S(1)} %get-tuple-element.91), channel_id=1, source_target_pairs={{0,8},{8,0},{16,24},{24,16},{32,40},{40,32},{48,56},{56,48},{64,72... | collective-permute-start | bytes 1327112 | tf_op jit(solution)/shard_map/ppermute | solution.py:324
  101.3 15.5 %collective-permute-start.16 = (bf16[4,24,1152]{2,1,0:T(8,128)(2,1)S(1)}, bf16[4,24,1152]{2,1,0:T(8,128)(2,1)S(1)}, u32[]{:S(2)}, u32[]{:S(2)}) collective-permute-start(bf16[4,24,1152]{2,1,0:T(8,128)(2,1)S(1)} %get-tuple-element.60), channel_id=1, source_target_pairs={{0,8},{8,0},{16,24},{24,16},{32,40},{40,32},{48,56},{56,48},{64,72... | collective-permute-start | bytes 663560 | tf_op jit(solution)/shard_map/ppermute | solution.py:324
  106.3 11.0 %collective-permute-start.19 = (bf16[4,24,1152]{2,1,0:T(8,128)(2,1)S(1)}, bf16[4,24,1152]{2,1,0:T(8,128)(2,1)S(1)}, u32[]{:S(2)}, u32[]{:S(2)}) collective-permute-start(bf16[4,24,1152]{2,1,0:T(8,128)(2,1)S(1)} %get-tuple-element.65), channel_id=1, source_target_pairs={{0,64},{8,72},{16,80},{24,88},{32,96},{40,104},{48,112},{56,120},{... | collective-permute-start | bytes 663560 | tf_op jit(solution)/shard_map/ppermute | solution.py:324
  110.5 7.2 %collective-permute-start.25 = (bf16[4,24,1152]{2,1,0:T(8,128)(2,1)S(1)}, bf16[4,24,1152]{2,1,0:T(8,128)(2,1)S(1)}, u32[]{:S(2)}, u32[]{:S(2)}) collective-permute-start(bf16[4,24,1152]{2,1,0:T(8,128)(2,1)S(1)} %get-tuple-element.73), channel_id=1, source_target_pairs={{0,56},{8,16},{16,8},{24,32},{32,24},{40,48},{48,40},{56,0},{64,12... | collective-permute-start | bytes 663560 | tf_op jit(solution)/shard_map/ppermute | solution.py:324
  114.4 7.2 %collective-permute-start.28 = (bf16[4,24,1152]{2,1,0:T(8,128)(2,1)S(1)}, bf16[4,24,1152]{2,1,0:T(8,128)(2,1)S(1)}, u32[]{:S(2)}, u32[]{:S(2)}) collective-permute-start(bf16[4,24,1152]{2,1,0:T(8,128)(2,1)S(1)} %get-tuple-element.78), channel_id=1, source_target_pairs={{0,192},{8,200},{16,208},{24,216},{32,224},{40,232},{48,240},{56,2... | collective-permute-start | bytes 663560 | tf_op jit(solution)/shard_map/ppermute | solution.py:324
  116.9 6.4 %collective-permute-start.20 = (bf16[2,24,1152]{2,1,0:T(8,128)(2,1)S(1)}, bf16[2,24,1152]{2,1,0:T(8,128)(2,1)S(1)}, u32[]{:S(2)}, u32[]{:S(2)}) collective-permute-start(bf16[2,24,1152]{2,1,0:T(8,128)(2,1)S(1)} %get-tuple-element.67), channel_id=1, source_target_pairs={{0,56},{8,16},{16,8},{24,32},{32,24},{40,48},{48,40},{56,0},{64,12... | collective-permute-start | bytes 331784 | tf_op jit(solution)/shard_map/ppermute | solution.py:324
  117.4 6.0 %collective-permute-start.21 = (bf16[2,24,1152]{2,1,0:T(8,128)(2,1)S(1)}, bf16[2,24,1152]{2,1,0:T(8,128)(2,1)S(1)}, u32[]{:S(2)}, u32[]{:S(2)}) collective-permute-start(bf16[2,24,1152]{2,1,0:T(8,128)(2,1)S(1)} %get-tuple-element.68), channel_id=1, source_target_pairs={{0,192},{8,200},{16,208},{24,216},{32,224},{40,232},{48,240},{56,2... | collective-permute-start | bytes 331784 | tf_op jit(solution)/shard_map/ppermute | solution.py:324
  117.8 7.5 %collective-permute-start.29 = (bf16[2,24,1152]{2,1,0:T(8,128)(2,1)S(1)}, bf16[2,24,1152]{2,1,0:T(8,128)(2,1)S(1)}, u32[]{:S(2)}, u32[]{:S(2)}) collective-permute-start(bf16[2,24,1152]{2,1,0:T(8,128)(2,1)S(1)} %get-tuple-element.80), channel_id=1, source_target_pairs={{0,8},{8,0},{16,24},{24,16},{32,40},{40,32},{48,56},{56,48},{64,72... | collective-permute-start | bytes 331784 | tf_op jit(solution)/shard_map/ppermute | solution.py:324
  123.4 8.9 %collective-permute-start.22 = (bf16[2,24,1152]{2,1,0:T(8,128)(2,1)S(1)}, bf16[2,24,1152]{2,1,0:T(8,128)(2,1)}, u32[]{:S(2)}, u32[]{:S(2)}) collective-permute-start(bf16[2,24,1152]{2,1,0:T(8,128)(2,1)S(1)} %get-tuple-element.69), channel_id=1, source_target_pairs={{0,24},{8,48},{16,40},{24,0},{32,56},{40,16},{48,8},{56,32},{64,88... | collective-permute-start | bytes 331784 | tf_op jit(solution)/shard_map/ppermute | solution.py:324
  127.1 8.8 %collective-permute-start.31 = (bf16[2,24,1152]{2,1,0:T(8,128)(2,1)}, bf16[2,24,1152]{2,1,0:T(8,128)(2,1)}, u32[]{:S(2)}, u32[]{:S(2)}) collective-permute-start(bf16[2,24,1152]{2,1,0:T(8,128)(2,1)} %get-tuple-element.82._), channel_id=1, source_target_pairs={{0,40},{8,32},{16,56},{24,48},{32,8},{40,0},{48,24},{56,16},{64,10... | collective-permute-start | bytes 331784 | tf_op jit(solution)/shard_map/ppermute | solution.py:324
  (17 other events, 218.8 us)

commit v4 on v3

--- a/solution.py
+++ b/solution.py
@@ -323,7 +323,7 @@
 def reduce_grads(send, keep, nx, nz):
     swap = lambda a, kind: lax.ppermute(a, "dp", list(enumerate(partners(kind, nx, nz))))
     got = [swap(send[v], PLANS[v][0]) for v in range(4)]
-    held = [halve_plain([keep[v]], [got[v]]) for v in range(4)]
+    held = [(halve_plain if v < 4 else halve)([keep[v]], [got[v]]) for v in range(4)]
     for step in (1, 2):
         got = [swap(held[v][0][0], PLANS[v][step]) for v in range(4)]
         held = [halve([held[v][1]], [got[v]]) for v in range(4)]
@@ -336,6 +336,28 @@
     return [k for k, _ in terms], [g for _, g in terms], sends
 
 
+def finish_kernel(a_ref, b_ref, c_ref, d_ref, *outs):
+    ff = outs[0].shape[-1]
+    for i in range(a_ref.shape[0]):
+        for j, (k, g) in enumerate(((a_ref, c_ref), (b_ref, d_ref))):
+            total = k[i].astype(F32) + g[i].astype(F32)
+            for n, out in enumerate(outs):
+                out[2 * i + j] = total[:, n * ff : (n + 1) * ff]
+
+
+def finish(keep, got):
+    pairs, own, wide = keep[0].shape
+    out = jax.ShapeDtypeStruct((2 * pairs, own, wide // 3), F32)
+    return pl.pallas_call(
+        finish_kernel,
+        grid=(1,),
+        in_specs=[whole(keep[0].shape)] * 4,
+        out_specs=[whole(out.shape)] * 3,
+        out_shape=[out] * 3,
+        cost_estimate=pl.CostEstimate(flops=2 * out.size, bytes_accessed=24 * out.size, transcendentals=0),
+    )(*keep, *got)
+
+
 def shards(nx, nz, tokens, expert_ids, gate_fixed, cotangent, w_gate, w_up, w_down):
     n_t, top = expert_ids.shape
     n_e, d, ff = w_gate.shape
@@ -356,16 +378,16 @@
     cot = {(0, 0): cotangent}
     cot[3, 0], cot[1, 0] = to(cotangent, 1, 0), to(cotangent, -1, 0)
     tok[0, 1], cot[0, 1] = to(tok[0, 0], 0, 1), to(cotangent, 0, 1)
-    later, cot[3, 0], cot[1, 0], tok[0, 1], cot[0, 1] = lax.optimization_barrier(
-        (tok[0, 0], cot[3, 0], cot[1, 0], tok[0, 1], cot[0, 1])
-    )
-    tok[3, 0], tok[1, 0] = to(later, 1, 0), to(later, -1, 0)
+    own, cot[3, 0], cot[1, 0] = lax.optimization_barrier((tok[0, 0], cot[3, 0], cot[1, 0]))
+    tok[3, 0], tok[1, 0] = to(own, 1, 0), to(own, -1, 0)
     cot[3, 1], cot[1, 1] = to(cot[3, 0], 0, 1), to(cot[1, 0], 0, 1)
-    cot[2, 0], tok[2, 0] = to(cot[3, 0], 1, 0), to(tok[1, 0], -1, 0)
+    by_c, tok[3, 0], tok[1, 0] = lax.optimization_barrier((cot[3, 0], tok[3, 0], tok[1, 0]))
+    cot[2, 0], tok[2, 0] = to(by_c, 1, 0), to(tok[1, 0], -1, 0)
     tok[3, 1], tok[1, 1] = to(tok[3, 0], 0, 1), to(tok[1, 0], 0, 1)
     order = tuple((dy, dc) for dy in (0, 1, 3, 2) for dc in range(2))
     mine, here = me.reshape(1), place.reshape(1)
     near = pack(mine, [tok[r] for r in order[:6]], [cot[r] for r in order[:6]], cap, n_e)
+    near, tok[2, 0], cot[2, 0] = lax.optimization_barrier((near, tok[2, 0], cot[2, 0]))
     tok[2, 1], cot[2, 1] = to(tok[2, 0], 0, 1), to(cot[2, 0], 0, 1)
     rows, grads = pack(mine, [tok[r] for r in order[6:]], [cot[r] for r in order[6:]], cap, n_e, near)
     chunks = jnp.asarray(chunk_orders(nx, nz).reshape(replicas, -1))
@@ -376,9 +398,7 @@
     back = lax.all_to_all(ret, "expert", split_axis=0, concat_axis=0, tiled=True)
     layer_out, input_grad = combine(ids, gate, last[-1], back)
     got, layer_out = lax.optimization_barrier((got, layer_out))
-    total = [k.astype(F32) + jnp.concatenate(g, 0).astype(F32) for k, g in zip(keep, got)]
-    total = jnp.concatenate([t[i : i + 1] for i in range(2) for t in total], 0)
-    return (layer_out, input_grad, total[:, :, :ff], total[:, :, ff : 2 * ff], total[:, :, 2 * ff :])
+    return (layer_out, input_grad, *finish(keep, [g[0] for g in got]))
 
 
 def solution(mesh):

time: 138 us -> 133 us (0.964)
  waiting for transfers between devices: 51.8 us -> 44.5 us
  local copies, waits for them, and re-layouts: 2.47 us -> 4.33 us
    ppermute x14, waiting for transfers between devices: 31.7 us -> 25.9 us  [to(): return lax.ppermute(a, 'expert', perm)]
    unnamed x32 -> x38, local copies, waits for them, and re-layouts: 1.67 us -> 4.33 us
    pallas_call x0 -> x1, Pallas kernels: none -> 1.83 us  [finish(): pl.pallas_call(finish_kernel, grid=(1,), in_specs=[whole(keep[0].shape)]...]
    ppermute x18, waiting for transfers between devices: 20.1 us -> 18.6 us  [reduce_grads(): lax.ppermute(a, 'dp', list(enumerate(partners(kind, nx, nz))))]
  transfers between devices with their start and end apart: 33 -> 33, of which waited for: 14 -> 15; matrix products, arithmetic and copies ran while one was open for 4% -> 4% of each run, Pallas kernels for 12% -> 13%
where the time goes in v4:
time: 133 us
  waiting for transfers between devices  44.5 us (33%)
  starting transfers between devices  43.4 us (33%)
  Pallas kernels  33.9 us (25%)
  other arithmetic  5.84 us (4%)
  local copies, waits for them, and re-layouts  4.33 us (3%)
    ppermute x18, starting transfers between devices, reduce_grads(): lax.ppermute(a, 'dp', list(enumerate(partners(kind, nx, nz))))  30.9 us
    ppermute x14, waiting for transfers between devices, to(): return lax.ppermute(a, 'expert', perm)  25.9 us
    ppermute x18, waiting for transfers between devices, reduce_grads(): lax.ppermute(a, 'dp', list(enumerate(partners(kind, nx, nz))))  18.6 us
    pallas_call x1, Pallas kernels, expert_grads(): pl.pallas_call(functools.partial(grads_kernel, scale), grid=(n_e,), in_sp...  11.9 us
    ppermute x14, starting transfers between devices, to(): return lax.ppermute(a, 'expert', perm)  8.77 us
    pallas_call x2, Pallas kernels, pack(): pl.pallas_call(functools.partial(pack_kernel, n, cap, n_e), grid=(1,), in...  7.59 us
    pallas_call x1, Pallas kernels, expert_returns(): pl.pallas_call(functools.partial(returns_kernel, cap, order), grid=(n_e,)...  7.09 us
    convert_element_type x4, other arithmetic, halve_plain(): sends.append((k[a:b].astype(F32) + g[a:b].astype(F32)).astype(BF16))  5.84 us
  transfers between devices with their start and end apart: 33, of which 15 were waited for; matrix products, arithmetic and copies ran while one was open for 4% of the time, Pallas kernels for 13%

profile of v4, /device:TPU:2, one launch (start us, length us, event | category | flops | bytes accessed | tf_op | source)
XLA Modules:
  0.0 132.8 jit_solution(11248801505217486748)
XLA Ops:
  0.6 3.1 %collective-permute-start.2 = (bf16[256,768]{1,0:T(8,128)(2,1)}, bf16[256,768]{1,0:T(8,128)(2,1)}, u32[]{:S(2)}, u32[]{:S(2)}) collective-permute-start(bf16[256,768]{1,0:T(8,128)(2,1)} %refs_6_.1), channel_id=1, source_target_pairs={{0,6},{1,7},{2,0},{3,1},{4,2},{5,3},{6,4},{7,5},{8,14},{9,15},{10,... | collective-permute-start | bytes 1179656 | tf_op jit(solution)/shard_map/ppermute | solution.py:374
  3.7 1.8 %shard_map.119.refs_0_ = bf16[272,768]{1,0:T(8,128)(2,1)} custom-call(s32[2,256]{1,0:T(2,128)} %bitcast.4, s32[2,256]{1,0:T(2,128)} %bitcast.6, bf16[256,768]{1,0:T(8,128)(2,1)} %tok_ref.1), custom_call_target="tpu_custom_call" | custom-call | flops 196608 | bytes 786432 | tf_op jit(solution)/shard_map/pallas_call | solution.py:46
  5.5 6.9 %collective-permute-done.2.refs_8_ = bf16[256,768]{1,0:T(8,128)(2,1)} collective-permute-done((bf16[256,768]{1,0:T(8,128)(2,1)}, bf16[256,768]{1,0:T(8,128)(2,1)}, u32[]{:S(2)}, u32[]{:S(2)}) %collective-permute-start.2) | collective-permute-done | bytes 393248 | tf_op jit(solution)/shard_map/ppermute | solution.py:374
  12.4 3.3 %collective-permute-done.1.refs_10_ = bf16[256,768]{1,0:T(8,128)(2,1)S(1)} collective-permute-done((bf16[256,768]{1,0:T(8,128)(2,1)}, bf16[256,768]{1,0:T(8,128)(2,1)S(1)}, u32[]{:S(2)}, u32[]{:S(2)}) %collective-permute-start.1) | collective-permute-done | bytes 393248 | tf_op jit(solution)/shard_map/ppermute | solution.py:374
  18.3 7.9 %collective-permute-done.4.refs_2_ = bf16[272,768]{1,0:T(8,128)(2,1)S(1)} collective-permute-done((bf16[272,768]{1,0:T(8,128)(2,1)}, bf16[272,768]{1,0:T(8,128)(2,1)S(1)}, u32[]{:S(2)}, u32[]{:S(2)}) %collective-permute-start.4) | collective-permute-done | bytes 417824 | tf_op jit(solution)/shard_map/ppermute | solution.py:374
  32.6 4.8 %shard_map.120 = (bf16[4,256,768]{2,1,0:T(8,128)(2,1)}, bf16[4,256,768]{2,1,0:T(8,128)(2,1)}) custom-call(s32[1]{0:T(128)} %bitcast.1.me_ref, bf16[272,768]{1,0:T(8,128)(2,1)} %shard_map.119.refs_0_, bf16[272,768]{1,0:T(8,128)(2,1)} %copy-done.10, bf16[272,768]{1,0:T(8,128)(2,1)} %copy-done.7, bf16[272,768]{1,0:T(8,128)(2,1)} %copy-done.12, ...), custom_call_target="tpu_custom_call" | custom-call | flops 603979776 | bytes 7077888 | tf_op jit(solution)/shard_map/pallas_call | solution.py:94
  37.4 4.2 %collective-permute-done.11.refs_2_ = bf16[256,768]{1,0:T(8,128)(2,1)} collective-permute-done((bf16[256,768]{1,0:T(8,128)(2,1)S(1)}, bf16[256,768]{1,0:T(8,128)(2,1)}, u32[]{:S(2)}, u32[]{:S(2)}) %collective-permute-start.11) | collective-permute-done | bytes 393248 | tf_op jit(solution)/shard_map/ppermute | solution.py:374
  42.1 2.0 %collective-permute-done.13.refs_3_ = bf16[256,768]{1,0:T(8,128)(2,1)S(1)} collective-permute-done((bf16[256,768]{1,0:T(8,128)(2,1)}, bf16[256,768]{1,0:T(8,128)(2,1)S(1)}, u32[]{:S(2)}, u32[]{:S(2)}) %collective-permute-start.13) | collective-permute-done | bytes 393248 | tf_op jit(solution)/shard_map/ppermute | solution.py:374
  45.6 2.8 %shard_map.121 = (bf16[4,256,768]{2,1,0:T(8,128)(2,1)}, bf16[4,256,768]{2,1,0:T(8,128)(2,1)}) custom-call(s32[1]{0:T(128)} %bitcast.1.me_ref, bf16[272,768]{1,0:T(8,128)(2,1)} %copy-done.8, bf16[272,768]{1,0:T(8,128)(2,1)} %copy-done.13, bf16[256,768]{1,0:T(8,128)(2,1)} %collective-permute-done.11.refs_2_, ...), custom_call_target="tpu_custom_call", output_to_operand_aliasing={{0}: (5, {}), {1}: (6, {})} | custom-call | flops 201326592 | bytes 2359296 | tf_op jit(solution)/shard_map/pallas_call | solution.py:94
  48.4 11.9 %shard_map.122 = (bf16[4,256,1152]{2,1,0:T(8,128)(2,1)}, bf16[16,24,1152]{2,1,0:T(8,128)(2,1)}, bf16[16,24,1152]{2,1,0:T(8,128)(2,1)}, bf16[16,24,1152]{2,1,0:T(...) custom-call(s32[1]{0:T(128)} %bitcast.place_ref, ...), custom_call_target="tpu_custom_call" | custom-call | flops 3623878656 | bytes 17301504 | tf_op jit(solution)/shard_map/pallas_call | solution.py:145
  60.9 1.9 %collective-permute-start.17 = (bf16[16,24,1152]{2,1,0:T(8,128)(2,1)}, bf16[16,24,1152]{2,1,0:T(8,128)(2,1)}, u32[]{:S(2)}, u32[]{:S(2)}) collective-permute-start(bf16[16,24,1152]{2,1,0:T(8,128)(2,1)} %get-tuple-element.76), channel_id=1, source_target_pairs={{0,8},{8,0},{16,24},{24,16},{32,40},{40,32},{48,56},{56,48},{64,72... | collective-permute-start | bytes 2654216 | tf_op jit(solution)/shard_map/ppermute | solution.py:324
  62.8 2.1 %collective-permute-start.23 = (bf16[16,24,1152]{2,1,0:T(8,128)(2,1)}, bf16[16,24,1152]{2,1,0:T(8,128)(2,1)}, u32[]{:S(2)}, u32[]{:S(2)}) collective-permute-start(bf16[16,24,1152]{2,1,0:T(8,128)(2,1)} %get-tuple-element.84), channel_id=1, source_target_pairs={{0,192},{8,200},{16,208},{24,216},{32,224},{40,232},{48,240},{56,2... | collective-permute-start | bytes 2654216 | tf_op jit(solution)/shard_map/ppermute | solution.py:324
  65.0 5.0 %collective-permute-start.26 = (bf16[16,24,1152]{2,1,0:T(8,128)(2,1)}, bf16[16,24,1152]{2,1,0:T(8,128)(2,1)}, u32[]{:S(2)}, u32[]{:S(2)}) collective-permute-start(bf16[16,24,1152]{2,1,0:T(8,128)(2,1)} %get-tuple-element.89), channel_id=1, source_target_pairs={{0,56},{8,16},{16,8},{24,32},{32,24},{40,48},{48,40},{56,0},{64,12... | collective-permute-start | bytes 2654216 | tf_op jit(solution)/shard_map/ppermute | solution.py:324
  69.9 7.1 %shard_map.133 = bf16[8,2,4,32,768]{4,3,2,1,0:T(8,128)(2,1)} custom-call(s32[1]{0:T(128)} %bitcast.1.me_ref, bf16[4,256,1152]{2,1,0:T(8,128)(2,1)} %get-tuple-element.96.saved_ref, bf16[4,768,384]{2,1,0:T(8,128)(2,1)} %wg_ref.3, bf16[4,768,384]{2,1,0:T(8,128)(2,1)} %wu_ref.3, bf16[4,768,384]{2,1,0:T(8,128)(2,1)} %wd_ref.3), custom_call_target="tpu_custom_call" | custom-call | flops 1811939328 | bytes 12582912 | tf_op jit(solution)/shard_map/pallas_call | solution.py:180
  77.0 3.6 %all-to-all-start = ((bf16[8,2,4,32,768]{4,3,2,1,0:T(8,128)(2,1)}), bf16[8,2,4,32,768]{4,3,2,1,0:T(8,128)(2,1)S(1)}, u32[]{:S(2)}, u32[]{:S(2)}) async-start(bf16[8,2,4,32,768]{4,3,2,1,0:T(8,128)(2,1)} %shard_map.133), calls=%async_computation | async-start | bytes 6291456 | tf_op jit(solution)/shard_map/all_to_all | solution.py:398
  80.7 1.7 %collective-permute-done.14 = bf16[16,24,1152]{2,1,0:T(8,128)(2,1)} collective-permute-done((bf16[16,24,1152]{2,1,0:T(8,128)(2,1)}, bf16[16,24,1152]{2,1,0:T(8,128)(2,1)}, u32[]{:S(2)}, u32[]{:S(2)}) %collective-permute-start.14) | collective-permute-done | bytes 884768 | tf_op jit(solution)/shard_map/ppermute | solution.py:324
  82.4 1.7 %add_convert_fusion.6 = (bf16[8,24,1152]{2,1,0:T(8,128)(2,1)S(1)}, bf16[8,24,1152]{2,1,0:T(8,128)(2,1)S(1)}) fusion(bf16[16,24,1152]{2,1,0:T(8,128)(2,1)} %collective-permute-done.14, bf16[16,24,1152]{2,1,0:T(8,128)(2,1)} %get-tuple-element.70), kind=kLoop, calls=%fused_computation.6 | loop fusion | flops 1769472 | bytes 2654208 | tf_op jit(solution)/shard_map/convert_element_type | solution.py:317
  87.1 5.9 %collective-permute-start.18 = (bf16[8,24,1152]{2,1,0:T(8,128)(2,1)S(1)}, bf16[8,24,1152]{2,1,0:T(8,128)(2,1)S(1)}, u32[]{:S(2)}, u32[]{:S(2)}) collective-permute-start(bf16[8,24,1152]{2,1,0:T(8,128)(2,1)S(1)} %get-tuple-element.111), channel_id=1, source_target_pairs={{0,56},{8,16},{16,8},{24,32},{32,24},{40,48},{48,40},{56,0},{64,12... | collective-permute-start | bytes 1327112 | tf_op jit(solution)/shard_map/ppermute | solution.py:324
  94.4 1.9 %collective-permute-start.24 = (bf16[8,24,1152]{2,1,0:T(8,128)(2,1)S(1)}, bf16[8,24,1152]{2,1,0:T(8,128)(2,1)S(1)}, u32[]{:S(2)}, u32[]{:S(2)}) collective-permute-start(bf16[8,24,1152]{2,1,0:T(8,128)(2,1)S(1)} %get-tuple-element.109), channel_id=1, source_target_pairs={{0,64},{8,72},{16,80},{24,88},{32,96},{40,104},{48,112},{56,120},{... | collective-permute-start | bytes 1327112 | tf_op jit(solution)/shard_map/ppermute | solution.py:324
  97.9 2.1 %collective-permute-start.16 = (bf16[4,24,1152]{2,1,0:T(8,128)(2,1)S(1)}, bf16[4,24,1152]{2,1,0:T(8,128)(2,1)S(1)}, u32[]{:S(2)}, u32[]{:S(2)}) collective-permute-start(bf16[4,24,1152]{2,1,0:T(8,128)(2,1)S(1)} %get-tuple-element.73), channel_id=1, source_target_pairs={{0,8},{8,0},{16,24},{24,16},{32,40},{40,32},{48,56},{56,48},{64,72... | collective-permute-start | bytes 663560 | tf_op jit(solution)/shard_map/ppermute | solution.py:324
  100.0 2.4 %collective-permute-done.18.refs_1_ = bf16[8,24,1152]{2,1,0:T(8,128)(2,1)S(1)} collective-permute-done((bf16[8,24,1152]{2,1,0:T(8,128)(2,1)S(1)}, bf16[8,24,1152]{2,1,0:T(8,128)(2,1)S(1)}, u32[]{:S(2)}, u32[]{:S(2)}) %collective-permute-start.18) | collective-permute-done | bytes 442400 | tf_op jit(solution)/shard_map/ppermute | solution.py:324
  102.5 1.9 %collective-permute-start.19 = (bf16[4,24,1152]{2,1,0:T(8,128)(2,1)S(1)}, bf16[4,24,1152]{2,1,0:T(8,128)(2,1)S(1)}, u32[]{:S(2)}, u32[]{:S(2)}) collective-permute-start(bf16[4,24,1152]{2,1,0:T(8,128)(2,1)S(1)} %get-tuple-element.78), channel_id=1, source_target_pairs={{0,64},{8,72},{16,80},{24,88},{32,96},{40,104},{48,112},{56,120},{... | collective-permute-start | bytes 663560 | tf_op jit(solution)/shard_map/ppermute | solution.py:324
  104.4 2.6 %collective-permute-done.24.refs_1_ = bf16[8,24,1152]{2,1,0:T(8,128)(2,1)S(1)} collective-permute-done((bf16[8,24,1152]{2,1,0:T(8,128)(2,1)S(1)}, bf16[8,24,1152]{2,1,0:T(8,128)(2,1)S(1)}, u32[]{:S(2)}, u32[]{:S(2)}) %collective-permute-start.24) | collective-permute-done | bytes 442400 | tf_op jit(solution)/shard_map/ppermute | solution.py:324
  107.6 3.1 %collective-permute-done.27.refs_1_ = bf16[8,24,1152]{2,1,0:T(8,128)(2,1)S(1)} collective-permute-done((bf16[8,24,1152]{2,1,0:T(8,128)(2,1)S(1)}, bf16[8,24,1152]{2,1,0:T(8,128)(2,1)S(1)}, u32[]{:S(2)}, u32[]{:S(2)}) %collective-permute-start.27) | collective-permute-done | bytes 442400 | tf_op jit(solution)/shard_map/ppermute | solution.py:324
  110.9 2.2 %collective-permute-done.16.refs_1_ = bf16[4,24,1152]{2,1,0:T(8,128)(2,1)S(1)} collective-permute-done((bf16[4,24,1152]{2,1,0:T(8,128)(2,1)S(1)}, bf16[4,24,1152]{2,1,0:T(8,128)(2,1)S(1)}, u32[]{:S(2)}, u32[]{:S(2)}) %collective-permute-start.16) | collective-permute-done | bytes 221216 | tf_op jit(solution)/shard_map/ppermute | solution.py:324
  115.0 2.5 %collective-permute-done.28.refs_1_ = bf16[4,24,1152]{2,1,0:T(8,128)(2,1)S(1)} collective-permute-done((bf16[4,24,1152]{2,1,0:T(8,128)(2,1)S(1)}, bf16[4,24,1152]{2,1,0:T(8,128)(2,1)S(1)}, u32[]{:S(2)}, u32[]{:S(2)}) %collective-permute-start.28) | collective-permute-done | bytes 221216 | tf_op jit(solution)/shard_map/ppermute | solution.py:324
  117.6 1.7 %collective-permute-start.30 = (bf16[2,24,1152]{2,1,0:T(8,128)(2,1)S(1)}, bf16[2,24,1152]{2,1,0:T(8,128)(2,1)S(1)}, u32[]{:S(2)}, u32[]{:S(2)}) collective-permute-start(bf16[2,24,1152]{2,1,0:T(8,128)(2,1)S(1)} %get-tuple-element.94), channel_id=1, source_target_pairs={{0,64},{8,72},{16,80},{24,88},{32,96},{40,104},{48,112},{56,120},{... | collective-permute-start | bytes 331784 | tf_op jit(solution)/shard_map/ppermute | solution.py:324
  119.4 2.0 %collective-permute-start.22 = (bf16[2,24,1152]{2,1,0:T(8,128)(2,1)S(1)}, bf16[2,24,1152]{2,1,0:T(8,128)(2,1)S(1)}, u32[]{:S(2)}, u32[]{:S(2)}) collective-permute-start(bf16[2,24,1152]{2,1,0:T(8,128)(2,1)S(1)} %get-tuple-element.82), channel_id=1, source_target_pairs={{0,24},{8,48},{16,40},{24,0},{32,56},{40,16},{48,8},{56,32},{64,88... | collective-permute-start | bytes 331784 | tf_op jit(solution)/shard_map/ppermute | solution.py:324
  123.1 2.3 %collective-permute-start.31 = (bf16[2,24,1152]{2,1,0:T(8,128)(2,1)S(1)}, bf16[2,24,1152]{2,1,0:T(8,128)(2,1)}, u32[]{:S(2)}, u32[]{:S(2)}) collective-permute-start(bf16[2,24,1152]{2,1,0:T(8,128)(2,1)S(1)} %get-tuple-element.95._), channel_id=1, source_target_pairs={{0,40},{8,32},{16,56},{24,48},{32,8},{40,0},{48,24},{56,16},{64,10... | collective-permute-start | bytes 331784 | tf_op jit(solution)/shard_map/ppermute | solution.py:324
  125.5 3.0 %shard_map.134 = (bf16[256,768]{1,0:T(8,128)(2,1)}, bf16[256,768]{1,0:T(8,128)(2,1)}) custom-call(s32[2,256]{1,0:T(2,128)S(1)} %bitcast.5, s32[2,256]{1,0:T(2,128)S(1)} %bitcast.7, bf16[2,24,1152]{2,1,0:T(8,128)(2,1)S(1)} %get-tuple-element.95._, bf16[8,2,4,32,768]{4,3,2,1,0:T(8,128)(2,1)S(1)} %all-to-all-done.ret), custom_call_target="tpu_custom_call" | custom-call | flops 1207959552 | bytes 7864320 | tf_op jit(solution)/shard_map/pallas_call | solution.py:229
  128.4 2.6 %collective-permute-done.31.d_ref = bf16[2,24,1152]{2,1,0:T(8,128)(2,1)} collective-permute-done((bf16[2,24,1152]{2,1,0:T(8,128)(2,1)S(1)}, bf16[2,24,1152]{2,1,0:T(8,128)(2,1)}, u32[]{:S(2)}, u32[]{:S(2)}) %collective-permute-start.31) | collective-permute-done | bytes 110624 | tf_op jit(solution)/shard_map/ppermute | solution.py:324
  131.0 1.8 %shard_map.135 = (f32[4,24,384]{2,1,0:T(8,128)}, f32[4,24,384]{2,1,0:T(8,128)}, f32[4,24,384]{2,1,0:T(8,128)}) custom-call(bf16[2,24,1152]{2,1,0:T(8,128)(2,1)} %copy-done, bf16[2,24,1152]{2,1,0:T(8,128)(2,1)} %copy-done.1, bf16[2,24,1152]{2,1,0:T(8,128)(2,1)} %copy-done.18, bf16[2,24,1152]{2,1,0:T(8,128)(2,1)} %collective-permute-done.31.d_ref), custom_call_target="tpu_custom_call" | custom-call | flops 73728 | bytes 884736 | tf_op jit(solution)/shard_map/pallas_call | solution.py:351
  (93 shorter events, 22.3 us)
Async XLA Ops:
  0.6 11.8 %collective-permute-start.2 = (bf16[256,768]{1,0:T(8,128)(2,1)}, bf16[256,768]{1,0:T(8,128)(2,1)}, u32[]{:S(2)}, u32[]{:S(2)}) collective-permute-start(bf16[256,768]{1,0:T(8,128)(2,1)} %refs_6_.1), channel_id=1, source_target_pairs={{0,6},{1,7},{2,0},{3,1},{4,2},{5,3},{6,4},{7,5},{8,14},{9,15},{10,... | collective-permute-start | bytes 1179656 | tf_op jit(solution)/shard_map/ppermute | solution.py:374
  3.7 12.0 %collective-permute-start.1 = (bf16[256,768]{1,0:T(8,128)(2,1)}, bf16[256,768]{1,0:T(8,128)(2,1)S(1)}, u32[]{:S(2)}, u32[]{:S(2)}) collective-permute-start(bf16[256,768]{1,0:T(8,128)(2,1)} %refs_6_.1), channel_id=1, source_target_pairs={{0,2},{1,3},{2,4},{3,5},{4,6},{5,7},{6,0},{7,1},{8,10},{9,11},{10,... | collective-permute-start | bytes 1179656 | tf_op jit(solution)/shard_map/ppermute | solution.py:374
  15.7 10.4 %collective-permute-start.4 = (bf16[272,768]{1,0:T(8,128)(2,1)}, bf16[272,768]{1,0:T(8,128)(2,1)S(1)}, u32[]{:S(2)}, u32[]{:S(2)}) collective-permute-start(bf16[272,768]{1,0:T(8,128)(2,1)} %shard_map.119.refs_0_), channel_id=1, source_target_pairs={{0,6},{1,7},{2,0},{3,1},{4,2},{5,3},{6,4},{7,5},{8,14},{9,15},{10,... | collective-permute-start | bytes 1253384 | tf_op jit(solution)/shard_map/ppermute | solution.py:374
  16.1 11.7 %collective-permute-start.3 = (bf16[272,768]{1,0:T(8,128)(2,1)}, bf16[272,768]{1,0:T(8,128)(2,1)S(1)}, u32[]{:S(2)}, u32[]{:S(2)}) collective-permute-start(bf16[272,768]{1,0:T(8,128)(2,1)} %shard_map.119.refs_0_), channel_id=1, source_target_pairs={{0,2},{1,3},{2,4},{3,5},{4,6},{5,7},{6,0},{7,1},{8,10},{9,11},{10,... | collective-permute-start | bytes 1253384 | tf_op jit(solution)/shard_map/ppermute | solution.py:374
  17.7 10.5 %collective-permute-start.7 = (bf16[256,768]{1,0:T(8,128)(2,1)}, bf16[256,768]{1,0:T(8,128)(2,1)S(1)}, u32[]{:S(2)}, u32[]{:S(2)}) collective-permute-start(bf16[256,768]{1,0:T(8,128)(2,1)} %refs_6_.1), channel_id=1, source_target_pairs={{0,1},{1,0},{2,3},{3,2},{4,5},{5,4},{6,7},{7,6},{8,9},{9,8},{10,11... | collective-permute-start | bytes 1179656 | tf_op jit(solution)/shard_map/ppermute | solution.py:374
  17.8 11.3 %collective-permute-start = (bf16[272,768]{1,0:T(8,128)(2,1)}, bf16[272,768]{1,0:T(8,128)(2,1)S(1)}, u32[]{:S(2)}, u32[]{:S(2)}) collective-permute-start(bf16[272,768]{1,0:T(8,128)(2,1)} %shard_map.119.refs_0_), channel_id=1, source_target_pairs={{0,1},{1,0},{2,3},{3,2},{4,5},{5,4},{6,7},{7,6},{8,9},{9,8},{10,11... | collective-permute-start | bytes 1253384 | tf_op jit(solution)/shard_map/ppermute | solution.py:374
  18.3 11.1 %collective-permute-start.8 = (bf16[256,768]{1,0:T(8,128)(2,1)}, bf16[256,768]{1,0:T(8,128)(2,1)}, u32[]{:S(2)}, u32[]{:S(2)}) collective-permute-start(bf16[256,768]{1,0:T(8,128)(2,1)} %collective-permute-done.2.refs_8_), channel_id=1, source_target_pairs={{0,1},{1,0},{2,3},{3,2},{4,5},{5,4},{6,7},{7,6},{8,9},{9,8},{10,11... | collective-permute-start | bytes 1179656 | tf_op jit(solution)/shard_map/ppermute | solution.py:374
  27.8 3.3 %collective-permute-start.6 = (bf16[272,768]{1,0:T(8,128)(2,1)S(1)}, bf16[272,768]{1,0:T(8,128)(2,1)S(1)}, u32[]{:S(2)}, u32[]{:S(2)}) collective-permute-start(bf16[272,768]{1,0:T(8,128)(2,1)S(1)} %collective-permute-done.3.refs_4_), channel_id=1, source_target_pairs={{0,1},{1,0},{2,3},{3,2},{4,5},{5,4},{6,7},{7,6},{8,9},{9,8},{10,11... | collective-permute-start | bytes 1253384 | tf_op jit(solution)/shard_map/ppermute | solution.py:374
  27.8 3.3 %collective-permute-start.5 = (bf16[272,768]{1,0:T(8,128)(2,1)S(1)}, bf16[272,768]{1,0:T(8,128)(2,1)S(1)}, u32[]{:S(2)}, u32[]{:S(2)}) collective-permute-start(bf16[272,768]{1,0:T(8,128)(2,1)S(1)} %collective-permute-done.4.refs_2_), channel_id=1, source_target_pairs={{0,1},{1,0},{2,3},{3,2},{4,5},{5,4},{6,7},{7,6},{8,9},{9,8},{10,11... | collective-permute-start | bytes 1253384 | tf_op jit(solution)/shard_map/ppermute | solution.py:374
  28.3 2.8 %collective-permute-start.9 = (bf16[256,768]{1,0:T(8,128)(2,1)S(1)}, bf16[256,768]{1,0:T(8,128)(2,1)S(1)}, u32[]{:S(2)}, u32[]{:S(2)}) collective-permute-start(bf16[256,768]{1,0:T(8,128)(2,1)S(1)} %collective-permute-done.1.refs_10_), channel_id=1, source_target_pairs={{0,1},{1,0},{2,3},{3,2},{4,5},{5,4},{6,7},{7,6},{8,9},{9,8},{10,11... | collective-permute-start | bytes 1179656 | tf_op jit(solution)/shard_map/ppermute | solution.py:374
  29.0 12.5 %collective-permute-start.10 = (bf16[272,768]{1,0:T(8,128)(2,1)S(1)}, bf16[272,768]{1,0:T(8,128)(2,1)S(1)}, u32[]{:S(2)}, u32[]{:S(2)}) collective-permute-start(bf16[272,768]{1,0:T(8,128)(2,1)S(1)} %collective-permute-done.4.refs_2_), channel_id=1, source_target_pairs={{0,6},{1,7},{2,0},{3,1},{4,2},{5,3},{6,4},{7,5},{8,14},{9,15},{10,... | collective-permute-start | bytes 1253384 | tf_op jit(solution)/shard_map/ppermute | solution.py:374
  29.4 12.2 %collective-permute-start.11 = (bf16[256,768]{1,0:T(8,128)(2,1)S(1)}, bf16[256,768]{1,0:T(8,128)(2,1)}, u32[]{:S(2)}, u32[]{:S(2)}) collective-permute-start(bf16[256,768]{1,0:T(8,128)(2,1)S(1)} %collective-permute-done.1.refs_10_), channel_id=1, source_target_pairs={{0,2},{1,3},{2,4},{3,5},{4,6},{5,7},{6,0},{7,1},{8,10},{9,11},{10,... | collective-permute-start | bytes 1179656 | tf_op jit(solution)/shard_map/ppermute | solution.py:374
  41.6 2.5 %collective-permute-start.12 = (bf16[272,768]{1,0:T(8,128)(2,1)S(1)}, bf16[272,768]{1,0:T(8,128)(2,1)S(1)}, u32[]{:S(2)}, u32[]{:S(2)}) collective-permute-start(bf16[272,768]{1,0:T(8,128)(2,1)S(1)} %collective-permute-done.10.refs_0_), channel_id=1, source_target_pairs={{0,1},{1,0},{2,3},{3,2},{4,5},{5,4},{6,7},{7,6},{8,9},{9,8},{10,11... | collective-permute-start | bytes 1253384 | tf_op jit(solution)/shard_map/ppermute | solution.py:374
  60.3 22.1 %collective-permute-start.14 = (bf16[16,24,1152]{2,1,0:T(8,128)(2,1)}, bf16[16,24,1152]{2,1,0:T(8,128)(2,1)}, u32[]{:S(2)}, u32[]{:S(2)}) collective-permute-start(bf16[16,24,1152]{2,1,0:T(8,128)(2,1)} %get-tuple-element.71), channel_id=1, source_target_pairs={{0,64},{8,72},{16,80},{24,88},{32,96},{40,104},{48,112},{56,120},{... | collective-permute-start | bytes 2654216 | tf_op jit(solution)/shard_map/ppermute | solution.py:324
  60.9 24.8 %collective-permute-start.17 = (bf16[16,24,1152]{2,1,0:T(8,128)(2,1)}, bf16[16,24,1152]{2,1,0:T(8,128)(2,1)}, u32[]{:S(2)}, u32[]{:S(2)}) collective-permute-start(bf16[16,24,1152]{2,1,0:T(8,128)(2,1)} %get-tuple-element.76), channel_id=1, source_target_pairs={{0,8},{8,0},{16,24},{24,16},{32,40},{40,32},{48,56},{56,48},{64,72... | collective-permute-start | bytes 2654216 | tf_op jit(solution)/shard_map/ppermute | solution.py:324
  62.8 30.2 %collective-permute-start.23 = (bf16[16,24,1152]{2,1,0:T(8,128)(2,1)}, bf16[16,24,1152]{2,1,0:T(8,128)(2,1)}, u32[]{:S(2)}, u32[]{:S(2)}) collective-permute-start(bf16[16,24,1152]{2,1,0:T(8,128)(2,1)} %get-tuple-element.84), channel_id=1, source_target_pairs={{0,192},{8,200},{16,208},{24,216},{32,224},{40,232},{48,240},{56,2... | collective-permute-start | bytes 2654216 | tf_op jit(solution)/shard_map/ppermute | solution.py:324
  65.0 31.3 %collective-permute-start.26 = (bf16[16,24,1152]{2,1,0:T(8,128)(2,1)}, bf16[16,24,1152]{2,1,0:T(8,128)(2,1)}, u32[]{:S(2)}, u32[]{:S(2)}) collective-permute-start(bf16[16,24,1152]{2,1,0:T(8,128)(2,1)} %get-tuple-element.89), channel_id=1, source_target_pairs={{0,56},{8,16},{16,8},{24,32},{32,24},{40,48},{48,40},{56,0},{64,12... | collective-permute-start | bytes 2654216 | tf_op jit(solution)/shard_map/ppermute | solution.py:324
  77.0 48.4 %all-to-all-start = ((bf16[8,2,4,32,768]{4,3,2,1,0:T(8,128)(2,1)}), bf16[8,2,4,32,768]{4,3,2,1,0:T(8,128)(2,1)S(1)}, u32[]{:S(2)}, u32[]{:S(2)}) async-start(bf16[8,2,4,32,768]{4,3,2,1,0:T(8,128)(2,1)} %shard_map.133), calls=%async_computation | async-start | bytes 6291456 | tf_op jit(solution)/shard_map/all_to_all | solution.py:398
  84.1 13.7 %collective-permute-start.15 = (bf16[8,24,1152]{2,1,0:T(8,128)(2,1)S(1)}, bf16[8,24,1152]{2,1,0:T(8,128)(2,1)S(1)}, u32[]{:S(2)}, u32[]{:S(2)}) collective-permute-start(bf16[8,24,1152]{2,1,0:T(8,128)(2,1)S(1)} %get-tuple-element.113), channel_id=1, source_target_pairs={{0,192},{8,200},{16,208},{24,216},{32,224},{40,232},{48,240},{56,2... | collective-permute-start | bytes 1327112 | tf_op jit(solution)/shard_map/ppermute | solution.py:324
  87.1 15.3 %collective-permute-start.18 = (bf16[8,24,1152]{2,1,0:T(8,128)(2,1)S(1)}, bf16[8,24,1152]{2,1,0:T(8,128)(2,1)S(1)}, u32[]{:S(2)}, u32[]{:S(2)}) collective-permute-start(bf16[8,24,1152]{2,1,0:T(8,128)(2,1)S(1)} %get-tuple-element.111), channel_id=1, source_target_pairs={{0,56},{8,16},{16,8},{24,32},{32,24},{40,48},{48,40},{56,0},{64,12... | collective-permute-start | bytes 1327112 | tf_op jit(solution)/shard_map/ppermute | solution.py:324
  94.4 12.6 %collective-permute-start.24 = (bf16[8,24,1152]{2,1,0:T(8,128)(2,1)S(1)}, bf16[8,24,1152]{2,1,0:T(8,128)(2,1)S(1)}, u32[]{:S(2)}, u32[]{:S(2)}) collective-permute-start(bf16[8,24,1152]{2,1,0:T(8,128)(2,1)S(1)} %get-tuple-element.109), channel_id=1, source_target_pairs={{0,64},{8,72},{16,80},{24,88},{32,96},{40,104},{48,112},{56,120},{... | collective-permute-start | bytes 1327112 | tf_op jit(solution)/shard_map/ppermute | solution.py:324
  97.7 13.0 %collective-permute-start.27 = (bf16[8,24,1152]{2,1,0:T(8,128)(2,1)S(1)}, bf16[8,24,1152]{2,1,0:T(8,128)(2,1)S(1)}, u32[]{:S(2)}, u32[]{:S(2)}) collective-permute-start(bf16[8,24,1152]{2,1,0:T(8,128)(2,1)S(1)} %get-tuple-element.107), channel_id=1, source_target_pairs={{0,8},{8,0},{16,24},{24,16},{32,40},{40,32},{48,56},{56,48},{64,72... | collective-permute-start | bytes 1327112 | tf_op jit(solution)/shard_map/ppermute | solution.py:324
  97.9 15.1 %collective-permute-start.16 = (bf16[4,24,1152]{2,1,0:T(8,128)(2,1)S(1)}, bf16[4,24,1152]{2,1,0:T(8,128)(2,1)S(1)}, u32[]{:S(2)}, u32[]{:S(2)}) collective-permute-start(bf16[4,24,1152]{2,1,0:T(8,128)(2,1)S(1)} %get-tuple-element.73), channel_id=1, source_target_pairs={{0,8},{8,0},{16,24},{24,16},{32,40},{40,32},{48,56},{56,48},{64,72... | collective-permute-start | bytes 663560 | tf_op jit(solution)/shard_map/ppermute | solution.py:324
  102.5 11.2 %collective-permute-start.19 = (bf16[4,24,1152]{2,1,0:T(8,128)(2,1)S(1)}, bf16[4,24,1152]{2,1,0:T(8,128)(2,1)S(1)}, u32[]{:S(2)}, u32[]{:S(2)}) collective-permute-start(bf16[4,24,1152]{2,1,0:T(8,128)(2,1)S(1)} %get-tuple-element.78), channel_id=1, source_target_pairs={{0,64},{8,72},{16,80},{24,88},{32,96},{40,104},{48,112},{56,120},{... | collective-permute-start | bytes 663560 | tf_op jit(solution)/shard_map/ppermute | solution.py:324
  107.1 7.2 %collective-permute-start.25 = (bf16[4,24,1152]{2,1,0:T(8,128)(2,1)S(1)}, bf16[4,24,1152]{2,1,0:T(8,128)(2,1)S(1)}, u32[]{:S(2)}, u32[]{:S(2)}) collective-permute-start(bf16[4,24,1152]{2,1,0:T(8,128)(2,1)S(1)} %get-tuple-element.86), channel_id=1, source_target_pairs={{0,56},{8,16},{16,8},{24,32},{32,24},{40,48},{48,40},{56,0},{64,12... | collective-permute-start | bytes 663560 | tf_op jit(solution)/shard_map/ppermute | solution.py:324
  110.8 6.8 %collective-permute-start.28 = (bf16[4,24,1152]{2,1,0:T(8,128)(2,1)S(1)}, bf16[4,24,1152]{2,1,0:T(8,128)(2,1)S(1)}, u32[]{:S(2)}, u32[]{:S(2)}) collective-permute-start(bf16[4,24,1152]{2,1,0:T(8,128)(2,1)S(1)} %get-tuple-element.91), channel_id=1, source_target_pairs={{0,192},{8,200},{16,208},{24,216},{32,224},{40,232},{48,240},{56,2... | collective-permute-start | bytes 663560 | tf_op jit(solution)/shard_map/ppermute | solution.py:324
  113.1 6.3 %collective-permute-start.20 = (bf16[2,24,1152]{2,1,0:T(8,128)(2,1)S(1)}, bf16[2,24,1152]{2,1,0:T(8,128)(2,1)S(1)}, u32[]{:S(2)}, u32[]{:S(2)}) collective-permute-start(bf16[2,24,1152]{2,1,0:T(8,128)(2,1)S(1)} %get-tuple-element.80), channel_id=1, source_target_pairs={{0,56},{8,16},{16,8},{24,32},{32,24},{40,48},{48,40},{56,0},{64,12... | collective-permute-start | bytes 331784 | tf_op jit(solution)/shard_map/ppermute | solution.py:324
  113.8 5.6 %collective-permute-start.21 = (bf16[2,24,1152]{2,1,0:T(8,128)(2,1)S(1)}, bf16[2,24,1152]{2,1,0:T(8,128)(2,1)S(1)}, u32[]{:S(2)}, u32[]{:S(2)}) collective-permute-start(bf16[2,24,1152]{2,1,0:T(8,128)(2,1)S(1)} %get-tuple-element.81), channel_id=1, source_target_pairs={{0,192},{8,200},{16,208},{24,216},{32,224},{40,232},{48,240},{56,2... | collective-permute-start | bytes 331784 | tf_op jit(solution)/shard_map/ppermute | solution.py:324
  114.4 7.0 %collective-permute-start.29 = (bf16[2,24,1152]{2,1,0:T(8,128)(2,1)S(1)}, bf16[2,24,1152]{2,1,0:T(8,128)(2,1)S(1)}, u32[]{:S(2)}, u32[]{:S(2)}) collective-permute-start(bf16[2,24,1152]{2,1,0:T(8,128)(2,1)S(1)} %get-tuple-element.93), channel_id=1, source_target_pairs={{0,8},{8,0},{16,24},{24,16},{32,40},{40,32},{48,56},{56,48},{64,72... | collective-permute-start | bytes 331784 | tf_op jit(solution)/shard_map/ppermute | solution.py:324
  117.6 4.8 %collective-permute-start.30 = (bf16[2,24,1152]{2,1,0:T(8,128)(2,1)S(1)}, bf16[2,24,1152]{2,1,0:T(8,128)(2,1)S(1)}, u32[]{:S(2)}, u32[]{:S(2)}) collective-permute-start(bf16[2,24,1152]{2,1,0:T(8,128)(2,1)S(1)} %get-tuple-element.94), channel_id=1, source_target_pairs={{0,64},{8,72},{16,80},{24,88},{32,96},{40,104},{48,112},{56,120},{... | collective-permute-start | bytes 331784 | tf_op jit(solution)/shard_map/ppermute | solution.py:324
  119.4 9.0 %collective-permute-start.22 = (bf16[2,24,1152]{2,1,0:T(8,128)(2,1)S(1)}, bf16[2,24,1152]{2,1,0:T(8,128)(2,1)S(1)}, u32[]{:S(2)}, u32[]{:S(2)}) collective-permute-start(bf16[2,24,1152]{2,1,0:T(8,128)(2,1)S(1)} %get-tuple-element.82), channel_id=1, source_target_pairs={{0,24},{8,48},{16,40},{24,0},{32,56},{40,16},{48,8},{56,32},{64,88... | collective-permute-start | bytes 331784 | tf_op jit(solution)/shard_map/ppermute | solution.py:324
  123.1 7.9 %collective-permute-start.31 = (bf16[2,24,1152]{2,1,0:T(8,128)(2,1)S(1)}, bf16[2,24,1152]{2,1,0:T(8,128)(2,1)}, u32[]{:S(2)}, u32[]{:S(2)}) collective-permute-start(bf16[2,24,1152]{2,1,0:T(8,128)(2,1)S(1)} %get-tuple-element.95._), channel_id=1, source_target_pairs={{0,40},{8,32},{16,56},{24,48},{32,8},{40,0},{48,24},{56,16},{64,10... | collective-permute-start | bytes 331784 | tf_op jit(solution)/shard_map/ppermute | solution.py:324
  (20 other events, 117.8 us)
